TPU v7x, 32 devices: a whole 2x2x4 slice. The times are simulated.
32 devices in a mesh: dp: 16 (over z, x, core), blk: 2 (over y).
Axes of the slice: x: 2, y: 2, z: 4, core: 2. Of those that a mesh axis runs over, the one named last changes fastest.
Arguments:
- tokens: bfloat16 [16, 2, 2048, 1152], P('dp', None, 'blk'), may hold values from -6 to 6
- cotangent: bfloat16 [16, 2, 2048, 1152], P('dp', None, 'blk'), may hold values from -6 to 6
- condition: bfloat16 [16, 2, 8, 1152], P('dp'), may hold values from -6 to 6
- lengths: int32 [16, 2, 8], P('dp'), may hold values from 0 to 1024, as said below
- adaptive_weight: bfloat16 [1152, 6912], P('dp', 'blk'), may hold values from -0.09375 to 0.09375
- joint_weight: bfloat16 [1152, 3456], P('dp', 'blk'), may hold values from -0.1875 to 0.1875
- output_weight: bfloat16 [1152, 1152], P('dp', 'blk'), may hold values from -0.75 to 0.75
- up_weight: bfloat16 [1152, 4608], P('dp', 'blk'), may hold values from -0.1875 to 0.1875
- down_weight: bfloat16 [4608, 1152], P('dp', 'blk'), may hold values from -0.09375 to 0.09375
- adaptive_bias: bfloat16 [6912], P('blk'), may hold values from -1.5 to 1.5
- query_bias: bfloat16 [1152], P('blk'), may hold values from -3 to 3
- value_bias: bfloat16 [1152], P('blk'), may hold values from -3 to 3
- output_bias: bfloat16 [1152], P('blk'), may hold values from -3 to 3
- up_bias: bfloat16 [4608], P('blk'), may hold values from -3 to 3
- down_bias: bfloat16 [1152], P('blk'), may hold values from -3 to 3
Outputs:
- block_output: float32 [16, 2, 2048, 1152], P('dp', None, 'blk')
- tokens_grad: float32 [16, 2, 2048, 1152], P('dp', None, 'blk')
- condition_grad: float32 [16, 2, 8, 1152], P('dp')
- adaptive_weight_grad: float32 [1152, 6912], P('dp', 'blk')
- joint_weight_grad: float32 [1152, 3456], P('dp', 'blk')
- output_weight_grad: float32 [1152, 1152], P('dp', 'blk')
- up_weight_grad: float32 [1152, 4608], P('dp', 'blk')
- down_weight_grad: float32 [4608, 1152], P('dp', 'blk')
- adaptive_bias_grad: float32 [6912], P('blk')
- query_bias_grad: float32 [1152], P('blk')
- value_bias_grad: float32 [1152], P('blk')
- output_bias_grad: float32 [1152], P('blk')
- up_bias_grad: float32 [4608], P('blk')
- down_bias_grad: float32 [1152], P('blk')
Inputs may be any that keep to these rules, and one draw needn't show every extreme that they name: `lengths`: every entry is 0, 256 or 1024; in each pack the nonzero entries come first and add up to 2048, and each pack holds at least one image of 1024 tokens and at least one empty slot.
All inputs are finite; a program needn't handle non-finite values.
Results may differ from a plain program's by a relative error of at most 0.025.
Values may be sent and summed in bfloat16 or wider, within the bound.
A program may use at most 576 MiB of HBM per device.

v0:
```python
import jax
import jax.numpy as jnp
from jax import lax
from jax.sharding import PartitionSpec as P

HEADS = 16


EPSILON = 1e-06
GELU_SCALE = 0.7978845608028654
HIGHEST = lax.Precision.HIGHEST
FLOAT = jnp.float32
HALF = jnp.bfloat16


def matmul(left, right):
    return jnp.dot(left, right, preferred_element_type=FLOAT)


def left_outer(left, right):
    return lax.dot_general(left, right, (((0,), (0,)), ((), ())), preferred_element_type=FLOAT)


def right_outer(left, right):
    return lax.dot_general(left, right, (((1,), (1,)), ((), ())), preferred_element_type=FLOAT)


def normalize(values):
    center = values - jnp.mean(values, axis=-1, keepdims=True)
    inverse = lax.rsqrt(jnp.mean(center * center, axis=-1, keepdims=True) + EPSILON)
    return (center * inverse, inverse)


def norm_backward(normed, inverse, grad):
    mean_grad = jnp.mean(grad, axis=-1, keepdims=True)
    mean_cross = jnp.mean(grad * normed, axis=-1, keepdims=True)
    return inverse * (grad - mean_grad - normed * mean_cross)


def gelu_tanh(values):
    return (
        0.5 * values * (1.0 + jnp.tanh(GELU_SCALE * (values + 0.044715 * values * values * values)))
    )


def gelu_slope(values):
    bend = jnp.tanh(GELU_SCALE * (values + 0.044715 * values * values * values))
    return 0.5 * (1.0 + bend) + 0.5 * values * (1.0 - bend * bend) * GELU_SCALE * (
        1.0 + 3.0 * 0.044715 * values * values
    )


def block_size():
    return 512


def block_scores(query_heads, key_part, query_slots, slot_part, scale):
    scores = jnp.einsum("qhd,khd->hqk", query_heads, key_part, preferred_element_type=FLOAT) * scale
    allowed = query_slots[:, None] == slot_part[None, :]
    return jnp.where(allowed[None], scores, -1e30)


def split_blocks(key_all, value_all, key_slots):
    total, width = key_all.shape
    size = block_size()
    count = total // size
    shape = (count, size, HEADS, width // HEADS)
    return (key_all.reshape(shape), value_all.reshape(shape), key_slots.reshape(count, size))


def attend_forward(query, key_all, value_all, query_slots, key_slots, scale):
    rows, width = query.shape
    query_heads = query.reshape(rows, HEADS, width // HEADS)
    key_blocks, value_blocks, slot_blocks = split_blocks(key_all, value_all, key_slots)

    def statistics(carry, item):
        top, mass = carry
        key_part, slot_part = item
        scores = block_scores(query_heads, key_part, query_slots, slot_part, scale)
        new_top = jnp.maximum(top, jnp.max(scores, axis=-1))
        mass = mass * jnp.exp(top - new_top) + jnp.sum(
            jnp.exp(scores - new_top[..., None]), axis=-1
        )
        return ((new_top, mass), None)

    start = (jnp.full((HEADS, rows), -1e30, FLOAT), jnp.zeros((HEADS, rows), FLOAT))
    (top, mass), unused = lax.scan(statistics, start, (key_blocks, slot_blocks))
    log_total = top + jnp.log(mass)

    def accumulate(running, item):
        key_part, value_part, slot_part = item
        scores = block_scores(query_heads, key_part, query_slots, slot_part, scale)
        weights = jnp.exp(scores - log_total[..., None]).astype(HALF)
        return (
            running + jnp.einsum("hqk,khd->qhd", weights, value_part, preferred_element_type=FLOAT),
            None,
        )

    empty = jnp.zeros((rows, HEADS, width // HEADS), FLOAT)
    attended, unused = lax.scan(accumulate, empty, (key_blocks, value_blocks, slot_blocks))
    return (log_total, attended.reshape(rows, width))


def attention_delta(d_attended, attended):
    rows, width = attended.shape
    grad_heads = d_attended.reshape(rows, HEADS, width // HEADS).astype(FLOAT)
    return jnp.einsum("qhd,qhd->hq", grad_heads, attended.reshape(rows, HEADS, width // HEADS))


def attend_backward(
    query, key_all, value_all, query_slots, key_slots, log_total, delta, d_attended, scale
):
    rows, width = query.shape
    total = key_all.shape[0]
    query_heads = query.reshape(rows, HEADS, width // HEADS)
    grad_heads = d_attended.reshape(rows, HEADS, width // HEADS)
    key_blocks, value_blocks, slot_blocks = split_blocks(key_all, value_all, key_slots)

    def one_block(d_query, item):
        key_part, value_part, slot_part = item
        scores = block_scores(query_heads, key_part, query_slots, slot_part, scale)
        weights = jnp.exp(scores - log_total[..., None])
        d_weights = jnp.einsum("qhd,khd->hqk", grad_heads, value_part, preferred_element_type=FLOAT)
        d_scores = (weights * (d_weights - delta[..., None])).astype(HALF)
        d_query = (
            d_query
            + jnp.einsum("hqk,khd->qhd", d_scores, key_part, preferred_element_type=FLOAT) * scale
        )
        d_value_part = jnp.einsum(
            "hqk,qhd->khd", weights.astype(HALF), grad_heads, preferred_element_type=FLOAT
        )
        d_key_part = (
            jnp.einsum("hqk,qhd->khd", d_scores, query_heads, preferred_element_type=FLOAT) * scale
        )
        return (d_query, (d_key_part, d_value_part))

    empty = jnp.zeros((rows, HEADS, width // HEADS), FLOAT)
    d_query, key_parts = lax.scan(one_block, empty, (key_blocks, value_blocks, slot_blocks))
    d_keys, d_values = key_parts
    return (
        d_query.reshape(rows, width),
        d_keys.reshape(total, width),
        d_values.reshape(total, width),
    )


def run_pack(full, tokens_in, cotangent_in, condition_in, lengths_in, blocks, first_block):
    (
        adaptive_matrix,
        joint_matrix,
        output_matrix,
        up_matrix,
        down_matrix,
        adaptive_vector,
        query_vector,
        value_vector,
        output_vector,
        up_vector,
        down_vector,
    ) = full
    rows, width = tokens_in.shape
    scale = (width // HEADS) ** (-0.5)
    inputs = tokens_in.astype(FLOAT)
    strip = lengths_in // blocks
    ends = jnp.cumsum(strip)
    starts = ends - strip
    place = jnp.arange(rows, dtype=jnp.int32)[:, None]
    inside = (place >= starts[None, :]) & (place < ends[None, :])
    member = inside.astype(FLOAT)
    slot_ids = jnp.sum(
        inside.astype(jnp.int32) * jnp.arange(strip.shape[0], dtype=jnp.int32)[None, :], axis=1
    )
    key_slots = jnp.tile(slot_ids, blocks)
    condition_full = condition_in.astype(FLOAT)
    cond_act = jax.nn.silu(condition_full).astype(HALF)
    modulation = matmul(cond_act, adaptive_matrix) + adaptive_vector.astype(FLOAT)
    per_token = jnp.dot(member, modulation, precision=HIGHEST, preferred_element_type=FLOAT)
    shift_one, scale_one, gate_one, shift_two, scale_two, gate_two = jnp.split(per_token, 6, axis=1)
    normed_one, inverse_one = normalize(inputs)
    hidden_one = (normed_one * (1.0 + scale_one) + shift_one).astype(HALF)
    projected = matmul(hidden_one, joint_matrix)
    query = (projected[:, :width] + query_vector.astype(FLOAT)).astype(HALF)
    keys = projected[:, width : 2 * width].astype(HALF)
    values = (projected[:, 2 * width :] + value_vector.astype(FLOAT)).astype(HALF)
    key_all, value_all = (
        lax.all_gather(keys, "blk", axis=0, tiled=True),
        lax.all_gather(values, "blk", axis=0, tiled=True),
    )
    log_total, attended = attend_forward(query, key_all, value_all, slot_ids, key_slots, scale)
    attended_half = attended.astype(HALF)
    branch_one = matmul(attended_half, output_matrix) + output_vector.astype(FLOAT)
    middle = inputs + gate_one * branch_one
    normed_two, inverse_two = normalize(middle)
    hidden_two = (normed_two * (1.0 + scale_two) + shift_two).astype(HALF)
    pre_act = matmul(hidden_two, up_matrix) + up_vector.astype(FLOAT)
    activated = gelu_tanh(pre_act).astype(HALF)
    branch_two = matmul(activated, down_matrix) + down_vector.astype(FLOAT)
    result = middle + gate_two * branch_two
    upstream = cotangent_in.astype(FLOAT)
    d_gate_two = upstream * branch_two
    d_branch_two = (upstream * gate_two).astype(HALF)
    d_pre = (right_outer(d_branch_two, down_matrix) * gelu_slope(pre_act)).astype(HALF)
    d_hidden_two = right_outer(d_pre, up_matrix)
    d_scale_two = d_hidden_two * normed_two
    d_middle = upstream + norm_backward(normed_two, inverse_two, d_hidden_two * (1.0 + scale_two))
    d_gate_one = d_middle * branch_one
    d_branch_one = (d_middle * gate_one).astype(HALF)
    d_attended = right_outer(d_branch_one, output_matrix).astype(HALF)
    delta = attention_delta(d_attended, attended)
    d_query_full, d_key_all, d_value_all = attend_backward(
        query, key_all, value_all, slot_ids, key_slots, log_total, delta, d_attended, scale
    )
    d_key_full, d_value_full = (
        lax.psum_scatter(
            d_key_all.astype(jnp.bfloat16), "blk", scatter_dimension=0, tiled=True
        ).astype(jnp.float32),
        lax.psum_scatter(
            d_value_all.astype(jnp.bfloat16), "blk", scatter_dimension=0, tiled=True
        ).astype(jnp.float32),
    )
    d_query = d_query_full.astype(HALF)
    d_keys = d_key_full.astype(HALF)
    d_values = d_value_full.astype(HALF)
    d_projected = jnp.concatenate([d_query, d_keys, d_values], axis=1)
    d_hidden_one = right_outer(d_projected, joint_matrix)
    d_scale_one = d_hidden_one * normed_one
    d_inputs = d_middle + norm_backward(normed_one, inverse_one, d_hidden_one * (1.0 + scale_one))
    d_per_token = jnp.concatenate(
        [d_hidden_one, d_scale_one, d_gate_one, d_hidden_two, d_scale_two, d_gate_two], axis=1
    )
    d_mod_local = lax.dot_general(
        member,
        d_per_token,
        (((0,), (0,)), ((), ())),
        precision=HIGHEST,
        preferred_element_type=FLOAT,
    )
    d_modulation = lax.psum(d_mod_local.astype(jnp.bfloat16), "blk").astype(jnp.float32)
    sigmoid_cond = jax.nn.sigmoid(condition_full)
    adaptive_float = adaptive_matrix.astype(FLOAT)
    d_condition = (
        lax.dot_general(
            d_modulation,
            adaptive_float,
            (((1,), (1,)), ((), ())),
            precision=HIGHEST,
            preferred_element_type=FLOAT,
        )
        * sigmoid_cond
        * (1.0 + condition_full * (1.0 - sigmoid_cond))
    )
    adaptive_grad = lax.dot_general(
        cond_act.astype(FLOAT),
        d_modulation,
        (((0,), (0,)), ((), ())),
        precision=HIGHEST,
        preferred_element_type=FLOAT,
    )
    local = (
        adaptive_grad * first_block,
        left_outer(hidden_one, d_projected),
        left_outer(attended_half, d_branch_one),
        left_outer(hidden_two, d_pre),
        left_outer(activated, d_branch_two),
        jnp.sum(d_modulation, axis=0) * first_block,
        jnp.sum(d_query.astype(FLOAT), axis=0),
        jnp.sum(d_values.astype(FLOAT), axis=0),
        jnp.sum(d_branch_one.astype(FLOAT), axis=0),
        jnp.sum(d_pre.astype(FLOAT), axis=0),
        jnp.sum(d_branch_two.astype(FLOAT), axis=0),
    )
    return (result, d_inputs, d_condition, local)


def body(
    tokens,
    cotangent,
    condition,
    lengths,
    adaptive_weight,
    joint_weight,
    output_weight,
    up_weight,
    down_weight,
    adaptive_bias,
    query_bias,
    value_bias,
    output_bias,
    up_bias,
    down_bias,
):
    micro = tokens.shape[1]
    blocks = lax.axis_size("blk")
    first_block = jnp.where(lax.axis_index("blk") == 0, 1.0, 0.0).astype(FLOAT)
    results = []
    token_grads = []
    condition_grads = []
    sums = None
    for step in range(micro):
        columns = (
            lax.all_gather(adaptive_weight, "blk", axis=1, tiled=True),
            lax.all_gather(joint_weight, "blk", axis=1, tiled=True),
            lax.all_gather(output_weight, "blk", axis=1, tiled=True),
            lax.all_gather(up_weight, "blk", axis=1, tiled=True),
            lax.all_gather(down_weight, "blk", axis=1, tiled=True),
            lax.all_gather(adaptive_bias, "blk", axis=0, tiled=True),
            lax.all_gather(query_bias, "blk", axis=0, tiled=True),
            lax.all_gather(value_bias, "blk", axis=0, tiled=True),
            lax.all_gather(output_bias, "blk", axis=0, tiled=True),
            lax.all_gather(up_bias, "blk", axis=0, tiled=True),
            lax.all_gather(down_bias, "blk", axis=0, tiled=True),
        )
        whole = (
            lax.all_gather(columns[0], "dp", axis=0, tiled=True),
            lax.all_gather(columns[1], "dp", axis=0, tiled=True),
            lax.all_gather(columns[2], "dp", axis=0, tiled=True),
            lax.all_gather(columns[3], "dp", axis=0, tiled=True),
            lax.all_gather(columns[4], "dp", axis=0, tiled=True),
        )
        full = tuple(whole) + tuple(columns[5:])
        result, d_inputs, d_condition, local = run_pack(
            full,
            tokens[0, step],
            cotangent[0, step],
            condition[0, step],
            lengths[0, step],
            blocks,
            first_block,
        )
        results.append(result)
        token_grads.append(d_inputs)
        condition_grads.append(d_condition)
        shares = (
            lax.psum_scatter(
                lax.psum_scatter(
                    local[0].astype(jnp.bfloat16), "dp", scatter_dimension=0, tiled=True
                ),
                "blk",
                scatter_dimension=1,
                tiled=True,
            ).astype(jnp.float32),
            lax.psum_scatter(
                lax.psum_scatter(
                    local[1].astype(jnp.bfloat16), "dp", scatter_dimension=0, tiled=True
                ),
                "blk",
                scatter_dimension=1,
                tiled=True,
            ).astype(jnp.float32),
            lax.psum_scatter(
                lax.psum_scatter(
                    local[2].astype(jnp.bfloat16), "dp", scatter_dimension=0, tiled=True
                ),
                "blk",
                scatter_dimension=1,
                tiled=True,
            ).astype(jnp.float32),
            lax.psum_scatter(
                lax.psum_scatter(
                    local[3].astype(jnp.bfloat16), "dp", scatter_dimension=0, tiled=True
                ),
                "blk",
                scatter_dimension=1,
                tiled=True,
            ).astype(jnp.float32),
            lax.psum_scatter(
                lax.psum_scatter(
                    local[4].astype(jnp.bfloat16), "dp", scatter_dimension=0, tiled=True
                ),
                "blk",
                scatter_dimension=1,
                tiled=True,
            ).astype(jnp.float32),
            lax.psum_scatter(
                lax.psum(local[5].astype(jnp.bfloat16), "dp"),
                "blk",
                scatter_dimension=0,
                tiled=True,
            ).astype(jnp.float32),
            lax.psum_scatter(
                lax.psum(local[6].astype(jnp.bfloat16), "dp"),
                "blk",
                scatter_dimension=0,
                tiled=True,
            ).astype(jnp.float32),
            lax.psum_scatter(
                lax.psum(local[7].astype(jnp.bfloat16), "dp"),
                "blk",
                scatter_dimension=0,
                tiled=True,
            ).astype(jnp.float32),
            lax.psum_scatter(
                lax.psum(local[8].astype(jnp.bfloat16), "dp"),
                "blk",
                scatter_dimension=0,
                tiled=True,
            ).astype(jnp.float32),
            lax.psum_scatter(
                lax.psum(local[9].astype(jnp.bfloat16), "dp"),
                "blk",
                scatter_dimension=0,
                tiled=True,
            ).astype(jnp.float32),
            lax.psum_scatter(
                lax.psum(local[10].astype(jnp.bfloat16), "dp"),
                "blk",
                scatter_dimension=0,
                tiled=True,
            ).astype(jnp.float32),
        )
        sums = (
            shares
            if sums is None
            else tuple((first + second for first, second in zip(sums, shares)))
        )
    block_output = jnp.stack(results, axis=0)[None]
    tokens_grad = jnp.stack(token_grads, axis=0)[None]
    condition_grad = jnp.stack(condition_grads, axis=0)[None]
    return (
        block_output,
        tokens_grad,
        condition_grad,
        sums[0],
        sums[1],
        sums[2],
        sums[3],
        sums[4],
        sums[5],
        sums[6],
        sums[7],
        sums[8],
        sums[9],
        sums[10],
    )


def solution(mesh):
    in_specs = (
        P("dp", None, "blk", None),
        P("dp", None, "blk", None),
        P("dp", None, None, None),
        P("dp", None, None),
        P("dp", "blk"),
        P("dp", "blk"),
        P("dp", "blk"),
        P("dp", "blk"),
        P("dp", "blk"),
        P("blk"),
        P("blk"),
        P("blk"),
        P("blk"),
        P("blk"),
        P("blk"),
    )
    out_specs = (
        P("dp", None, "blk", None),
        P("dp", None, "blk", None),
        P("dp", None, None, None),
        P("dp", "blk"),
        P("dp", "blk"),
        P("dp", "blk"),
        P("dp", "blk"),
        P("dp", "blk"),
        P("blk"),
        P("blk"),
        P("blk"),
        P("blk"),
        P("blk"),
        P("blk"),
    )
    return jax.shard_map(body, mesh=mesh, in_specs=in_specs, out_specs=out_specs, check_vma=False)
```

profile of v0, /device:TPU:0, one launch (start us, length us, event | category | flops | bytes accessed | tf_op | source)
XLA Modules:
  0.0 3540.3 jit_solution(2274096412259992264)
XLA Ops:
  44.8 102.4 %all-gather.15.cloned.1.call-done = bf16[1152,6912]{1,0:T(8,128)(2,1)} async-done(((bf16[72,6912]{1,0:T(8,128)(2,1)}), bf16[1152,6912]{1,0:T(8,128)(2,1)}) %all-gather.15.cloned.1.call-update) | async-done | bytes 15925264 | tf_op jit(solution)/shard_map/all_gather | solution.py:314
  178.4 41.9 %all-gather.17.cloned.1.call-done = bf16[1152,3456]{1,0:T(8,128)(2,1)} async-done(((bf16[72,3456]{1,0:T(8,128)(2,1)}), bf16[1152,3456]{1,0:T(8,128)(2,1)}) %all-gather.17.cloned.1.call-update) | async-done | bytes 7962640 | tf_op jit(solution)/shard_map/all_gather | solution.py:315
  371.3 121.2 %while.80 = (s32[]{:T(128)}, f32[16,1024]{1,0:T(8,128)S(1)}, f32[16,1024]{1,0:T(8,128)S(1)}, s32[1024]{0:T(1024)S(1)}, s32[4,512]{1,0:T(4,128)S(1)}, /*index=5*/...) while((s32[]{:T(128)}, f32[16,1024]{1,0:T(8,128)S(1)}, ...), condition=%wide.region_19.20_spmd.clone, body=%wide.region_16.19_spmd.clone.sunk | while | flops 1267286016 | bytes 73082992 | solution.py:87
  523.3 65.7 %while.81 = (s32[]{:T(128)}, f32[1024,16,72]{0,2,1:T(8,128)}, bf16[4,512,16,72]{1,3,2,0:T(8,128)(2,1)}, s32[1024]{0:T(1024)S(1)}, s32[4,512]{1,0:T(4,128)S(1)}, ...) while((s32[]{:T(128)}, f32[1024,16,72]{0,2,1:T(8,128)}, ...), condition=%wide.region_21.22_spmd.clone, body=%wide.region_20.21_spmd.clone.sunk | while | flops 2452357120 | bytes 15281786 | solution.py:100
  628.3 21.8 convolution_add_fusion.2
  650.1 28.0 fusion.217
  731.1 306.2 %while.83 = (s32[]{:T(128)}, f32[1024,16,72]{0,2,1:T(8,128)}, bf16[4,512,16,72]{1,3,2,0:T(8,128)(2,1)}, bf16[4,512,16,72]{1,3,2,0:T(8,128)(2,1)}, bf16[4,512,16,...) while((s32[]{:T(128)}, f32[1024,16,72]{0,2,1:T(8,128)}, ...), condition=%wide.region_35.36_spmd.clone, body=%wide.region_34.35_spmd.clone.sunk | while | flops 6128336896 | bytes 247015616 | solution.py:138
  1061.7 45.4 %reduce-scatter.55.cloned.1.call-done = bf16[1024,1152]{0,1:T(8,128)(2,1)} async-done(((bf16[2048,1152]{0,1:T(8,128)(2,1)}), bf16[1024,1152]{0,1:T(8,128)(2,1)}) %reduce-scatter.55.cloned.1.call-update) | async-done | bytes 2359312 | tf_op jit(solution)/shard_map/reduce_scatter | solution.py:217
  1107.1 63.0 %reduce-scatter.53.cloned.1.call-done = bf16[1024,1152]{0,1:T(8,128)(2,1)} async-done(((bf16[2048,1152]{0,1:T(8,128)(2,1)}), bf16[1024,1152]{0,1:T(8,128)(2,1)}) %reduce-scatter.53.cloned.1.call-update) | async-done | bytes 2359312 | tf_op jit(solution)/shard_map/reduce_scatter | solution.py:214
  1223.3 53.6 %all-gather.21.cloned.1.call-done = bf16[2048,1152]{1,0:T(8,128)(2,1)} async-done(((bf16[1024,1152]{1,0:T(8,128)(2,1)}), bf16[2048,1152]{1,0:T(8,128)(2,1)}) %all-gather.21.cloned.1.call-update) | async-done | bytes 4718608 | tf_op jit(solution)/shard_map/all_gather | solution.py:186
  1307.4 120.3 %while.78 = (s32[]{:T(128)}, f32[16,1024]{1,0:T(8,128)S(1)}, f32[16,1024]{1,0:T(8,128)S(1)}, s32[1024]{0:T(1024)S(1)}, s32[4,512]{1,0:T(4,128)S(1)}, /*index=5*/...) while((s32[]{:T(128)}, f32[16,1024]{1,0:T(8,128)S(1)}, ...), condition=%wide.region_7.8_spmd.clone, body=%wide.region_4.7_spmd.clone.sunk | while | flops 1267286016 | bytes 73082992 | solution.py:87
  1458.2 64.5 %while.79 = (s32[]{:T(128)}, f32[1024,16,72]{0,2,1:T(8,128)}, bf16[4,512,16,72]{1,3,2,0:T(8,128)(2,1)}, s32[1024]{0:T(1024)S(1)}, s32[4,512]{1,0:T(4,128)S(1)}, ...) while((s32[]{:T(128)}, f32[1024,16,72]{0,2,1:T(8,128)}, ...), condition=%wide.region_9.10_spmd.clone, body=%wide.region_8.9_spmd.clone.sunk | while | flops 2452357120 | bytes 15281786 | solution.py:100
  1561.2 20.8 convolution_add_fusion.3
  1582.0 31.0 fusion.218
  1660.5 306.4 %while.82 = (s32[]{:T(128)}, f32[1024,16,72]{0,2,1:T(8,128)}, bf16[4,512,16,72]{1,3,2,0:T(8,128)(2,1)}, bf16[4,512,16,72]{1,3,2,0:T(8,128)(2,1)}, bf16[4,512,16,...) while((s32[]{:T(128)}, f32[1024,16,72]{0,2,1:T(8,128)}, ...), condition=%wide.region_27.28_spmd.clone, body=%wide.region_26.27_spmd.clone.sunk | while | flops 6128336896 | bytes 247015616 | solution.py:138
  1770.8 20.6 fusion.356
  1847.5 20.6 fusion.356
  1995.3 23.2 convolution_convert_fusion
  2053.7 45.9 %reduce-scatter.49.cloned.1.call-done = bf16[1024,1152]{0,1:T(8,128)(2,1)} async-done(((bf16[2048,1152]{0,1:T(8,128)(2,1)}), bf16[1024,1152]{0,1:T(8,128)(2,1)}) %reduce-scatter.49.cloned.1.call-update) | async-done | bytes 2359312 | tf_op jit(solution)/shard_map/reduce_scatter | solution.py:214
  2205.1 22.5 convolution_convert_fusion.1
  2266.6 24.4 reduce-scatter.71.cloned.1.call-done
  2293.3 65.5 %reduce-scatter.93.cloned.1.call-done = bf16[72,1152]{1,0:T(8,128)(2,1)} async-done(((bf16[1152,1152]{1,0:T(8,128)(2,1)}), bf16[72,1152]{1,0:T(8,128)(2,1)}) %reduce-scatter.93.cloned.1.call-update) | async-done | bytes 165904
  2360.7 101.8 %reduce-scatter.91.cloned.1.call-done = bf16[72,3456]{1,0:T(8,128)(2,1)} async-done(((bf16[1152,3456]{1,0:T(8,128)(2,1)}), bf16[72,3456]{1,0:T(8,128)(2,1)}) %reduce-scatter.91.cloned.1.call-update) | async-done | bytes 497680
  2507.4 105.6 %reduce-scatter.69.cloned.1.call-done = bf16[288,1152]{1,0:T(8,128)(2,1)} async-done(((bf16[4608,1152]{1,0:T(8,128)(2,1)}), bf16[288,1152]{1,0:T(8,128)(2,1)}) %reduce-scatter.69.cloned.1.call-update) | async-done | bytes 663568 | tf_op jit(solution)/shard_map/reduce_scatter | solution.py:367
  2615.5 122.1 %reduce-scatter.65.cloned.1.call-done = bf16[72,4608]{1,0:T(8,128)(2,1)} async-done(((bf16[1152,4608]{1,0:T(8,128)(2,1)}), bf16[72,4608]{1,0:T(8,128)(2,1)}) %reduce-scatter.65.cloned.1.call-update) | async-done | bytes 663568 | tf_op jit(solution)/shard_map/reduce_scatter | solution.py:359
  2753.7 123.4 %reduce-scatter.61.cloned.1.call-done = bf16[72,4608]{1,0:T(8,128)(2,1)} async-done(((bf16[1152,4608]{1,0:T(8,128)(2,1)}), bf16[72,4608]{1,0:T(8,128)(2,1)}) %reduce-scatter.61.cloned.1.call-update) | async-done | bytes 663568 | tf_op jit(solution)/shard_map/reduce_scatter | solution.py:359
  2944.6 95.4 %reduce-scatter.89.cloned.1.call-done = bf16[72,3456]{1,0:T(8,128)(2,1)} async-done(((bf16[1152,3456]{1,0:T(8,128)(2,1)}), bf16[72,3456]{1,0:T(8,128)(2,1)}) %reduce-scatter.89.cloned.1.call-update) | async-done | bytes 497680
  3052.7 60.7 %all-reduce.20 = (bf16[3456]{0:T(1024)(128)(2,1)S(1)}, bf16[3456]{0:T(1024)(128)(2,1)S(1)}, bf16[576]{0:T(1024)(128)(2,1)S(1)}, bf16[576]{0:T(1024)(128)(2,1)S(1...) all-reduce(bf16[3456]{0:T(1024)(128)(2,1)S(1)} %dynamic-slice.15, ...), channel_id=1, replica_groups=mesh['dp'=16,'blk'=2] {'dp'}, use_global_device_ids=true, to_apply=%region_66.67 | all-reduce | flops 16128 | bytes 64512 | tf_op jit(solution)/shard_map/psum | solution.py:375
  3115.2 101.3 %reduce-scatter.57.cloned.1.call-done = bf16[72,6912]{1,0:T(8,128)(2,1)} async-done(((bf16[1152,6912]{1,0:T(8,128)(2,1)}), bf16[72,6912]{1,0:T(8,128)(2,1)}) %reduce-scatter.57.cloned.1.call-update) | async-done | bytes 995344 | tf_op jit(solution)/shard_map/reduce_scatter | solution.py:335
  3242.1 149.5 %reduce-scatter.59.cloned.1.call-done = bf16[72,6912]{1,0:T(8,128)(2,1)} async-done(((bf16[1152,6912]{1,0:T(8,128)(2,1)}), bf16[72,6912]{1,0:T(8,128)(2,1)}) %reduce-scatter.59.cloned.1.call-update) | async-done | bytes 995344 | tf_op jit(solution)/shard_map/reduce_scatter | solution.py:335
  3471.7 28.3 reduce-scatter.73.cloned.1.call-done
  3501.5 29.1 reduce-scatter.75.cloned.1.call-done
  (724 shorter events, 1971.6 us)
Async XLA Ops:
  7.2 140.0 %all-gather.15.cloned.1.call-start = ((), (), s32[]{:S(2)}) async-start(), calls=%async_computation.24 | async-start | bytes 16920576 | tf_op jit(solution)/shard_map/all_gather | solution.py:314
  25.2 195.1 %all-gather.17.cloned.1.call-start = ((), (), s32[]{:S(2)}) async-start(), calls=%async_computation.25 | async-start | bytes 8460288 | tf_op jit(solution)/shard_map/all_gather | solution.py:315
  35.2 305.7 %all-gather.31.cloned.1.call-start = ((), (), s32[]{:S(2)}) async-start(), calls=%async_computation.32 | async-start | bytes 7077888 | tf_op jit(solution)/shard_map/all_gather | solution.py:186
  239.3 253.2 %all-gather.29.cloned.1.call-start = ((), (), s32[]{:S(2)}) async-start(), calls=%async_computation.31 | async-start | bytes 7077888 | tf_op jit(solution)/shard_map/all_gather | solution.py:187
  256.2 335.6 %all-gather.23.cloned.1.call-start = ((), (), s32[]{:S(2)}) async-start(), calls=%async_computation.28 | async-start | bytes 2820096 | tf_op jit(solution)/shard_map/all_gather | solution.py:316
  264.7 344.0 %all-gather.25.cloned.1.call-start = ((), (), s32[]{:S(2)}) async-start(), calls=%async_computation.29 | async-start | bytes 11280384 | tf_op jit(solution)/shard_map/all_gather | solution.py:317
  282.3 345.9 %all-gather.27.cloned.1.call-start = ((), (), s32[]{:S(2)}) async-start(), calls=%async_computation.30 | async-start | bytes 11280384 | tf_op jit(solution)/shard_map/all_gather | solution.py:318
  303.0 804.1 %reduce-scatter.55.cloned.1.call-start = ((), (), s32[]{:S(2)}) async-start(), calls=%async_computation.36 | async-start | bytes 7077888 | tf_op jit(solution)/shard_map/reduce_scatter | solution.py:217
  1057.7 219.1 %all-gather.21.cloned.1.call-start = ((), (), s32[]{:S(2)}) async-start(), calls=%async_computation.27 | async-start | bytes 7077888 | tf_op jit(solution)/shard_map/all_gather | solution.py:186
  1214.0 213.6 %all-gather.19.cloned.1.call-start = ((), (), s32[]{:S(2)}) async-start(), calls=%async_computation.26 | async-start | bytes 7077888 | tf_op jit(solution)/shard_map/all_gather | solution.py:187
  1223.2 830.5 %reduce-scatter.51.cloned.1.call-start = ((), (), s32[]{:S(2)}) async-start(), calls=%async_computation.34 | async-start | bytes 7077888 | tf_op jit(solution)/shard_map/reduce_scatter | solution.py:217
  1987.3 259.3 %reduce-scatter.95.cloned.1.call-start = ((), (), s32[]{:S(2)}) async-start(), calls=%async_computation.56 | async-start | bytes 2820096
  1995.3 295.7 %reduce-scatter.71.cloned.1.call-start = ((), (), s32[]{:S(2)}) async-start(), calls=%async_computation.44 | async-start | bytes 11280384 | tf_op jit(solution)/shard_map/reduce_scatter | solution.py:367
  2018.6 340.3 %reduce-scatter.93.cloned.1.call-start = ((), (), s32[]{:S(2)}) async-start(), calls=%async_computation.55 | async-start | bytes 2820096
  2026.7 435.9 %reduce-scatter.91.cloned.1.call-start = ((), (), s32[]{:S(2)}) async-start(), calls=%async_computation.54 | async-start | bytes 8460288
  2049.0 439.2 %all-reduce.26.cloned.1.call-start = ((), (), s32[]{:S(2)}) async-start(), calls=%async_computation.57 | async-start | bytes 442368 | tf_op jit(solution)/shard_map/psum | solution.py:238
  2205.1 408.0 %reduce-scatter.69.cloned.1.call-start = ((), (), s32[]{:S(2)}) async-start(), calls=%async_computation.43 | async-start | bytes 11280384 | tf_op jit(solution)/shard_map/reduce_scatter | solution.py:367
  2227.6 509.9 %reduce-scatter.65.cloned.1.call-start = ((), (), s32[]{:S(2)}) async-start(), calls=%async_computation.41 | async-start | bytes 11280384 | tf_op jit(solution)/shard_map/reduce_scatter | solution.py:359
  2246.5 505.8 %reduce-scatter.83.cloned.1.call-start = ((), (), s32[]{:S(2)}) async-start(), calls=%async_computation.50 | async-start | bytes 442368
  2248.6 628.6 %reduce-scatter.61.cloned.1.call-start = ((), (), s32[]{:S(2)}) async-start(), calls=%async_computation.39 | async-start | bytes 11280384 | tf_op jit(solution)/shard_map/reduce_scatter | solution.py:359
  2266.5 631.9 %reduce-scatter.87.cloned.1.call-start = ((), (), s32[]{:S(2)}) async-start(), calls=%async_computation.52 | async-start | bytes 1327104
  2293.3 619.9 %reduce-scatter.81.cloned.1.call-start = ((), (), s32[]{:S(2)}) async-start(), calls=%async_computation.49 | async-start | bytes 442368
  2360.7 574.0 %reduce-scatter.79.cloned.1.call-start = ((), (), s32[]{:S(2)}) async-start(), calls=%async_computation.48 | async-start | bytes 1327104
  2464.8 575.2 %reduce-scatter.89.cloned.1.call-start = ((), (), s32[]{:S(2)}) async-start(), calls=%async_computation.53 | async-start | bytes 8460288
  2478.5 737.9 %reduce-scatter.57.cloned.1.call-start = ((), (), s32[]{:S(2)}) async-start(), calls=%async_computation.37 | async-start | bytes 16920576 | tf_op jit(solution)/shard_map/reduce_scatter | solution.py:335
  2496.9 894.7 %reduce-scatter.59.cloned.1.call-start = ((), (), s32[]{:S(2)}) async-start(), calls=%async_computation.38 | async-start | bytes 16920576 | tf_op jit(solution)/shard_map/reduce_scatter | solution.py:335
  2507.4 904.2 %reduce-scatter.85.cloned.1.call-start = ((), (), s32[]{:S(2)}) async-start(), calls=%async_computation.51 | async-start | bytes 1327104
  2615.4 814.4 %reduce-scatter.67.cloned.1.call-start = ((), (), s32[]{:S(2)}) async-start(), calls=%async_computation.42 | async-start | bytes 995328 | tf_op jit(solution)/shard_map/reduce_scatter | solution.py:358
  2737.6 710.7 %reduce-scatter.63.cloned.1.call-start = ((), (), s32[]{:S(2)}) async-start(), calls=%async_computation.40 | async-start | bytes 995328 | tf_op jit(solution)/shard_map/reduce_scatter | solution.py:358
  2877.2 592.5 %reduce-scatter.77.cloned.1.call-start = ((), (), s32[]{:S(2)}) async-start(), calls=%async_computation.47 | async-start | bytes 1327104
  3042.3 457.7 %reduce-scatter.73.cloned.1.call-start = ((), (), s32[]{:S(2)}) async-start(), calls=%async_computation.45 | async-start | bytes 2654208
  3219.0 311.6 %reduce-scatter.75.cloned.1.call-start = ((), (), s32[]{:S(2)}) async-start(), calls=%async_computation.46 | async-start | bytes 2654208
  (146 other events, 5488.0 us)
Sparse Core Ops, SparseCore 0:
  25.3 121.8 all-gather.14
  149.9 70.3 all-gather.16
  239.4 78.1 all-gather.30
  319.1 62.6 all-gather.28
  384.3 43.3 all-gather.22
  429.8 87.3 all-gather.24
  520.1 86.8 all-gather.26
  1047.6 59.4 reduce-scatter.54
  1110.1 59.9 reduce-scatter.52
  1214.2 62.6 all-gather.20
  1278.4 62.6 all-gather.18
  1977.1 59.9 reduce-scatter.50
  2039.5 59.9 reduce-scatter.48
  2103.3 63.8 reduce-scatter.94
  2171.7 119.1 reduce-scatter.70
  2295.2 63.6 reduce-scatter.92
  2362.8 99.7 reduce-scatter.90
  2465.5 22.5 all-reduce.25
  2492.7 120.3 reduce-scatter.68
  2617.5 119.9 reduce-scatter.64
  2756.9 120.2 reduce-scatter.60
  2880.1 18.2 reduce-scatter.86
  2916.1 18.5 reduce-scatter.78
  2939.2 100.8 reduce-scatter.88
  3044.0 172.3 reduce-scatter.56
  3220.6 171.0 reduce-scatter.58
  3393.9 17.6 reduce-scatter.84
  3413.7 16.0 reduce-scatter.66
  3432.2 16.0 reduce-scatter.62
  3451.1 18.5 reduce-scatter.76
  3471.8 28.2 reduce-scatter.72
  3502.4 28.2 reduce-scatter.74
  (2 shorter events, 23.7 us)
where the time goes:
time: 3550 us; the launch traced here: 3540 us
  waiting for transfers between devices  1440 us (41%)
  matrix products  1350 us (38%)
  other arithmetic  296 us (8%)
  local copies, waits for them, and re-layouts  279 us (8%)
  blocking collectives  157 us (4%)
    unnamed x46, waiting for transfers between devices  415 us
    dot_general x16, matrix products, block_scores(): jnp.einsum('qhd,khd->hqk', query_heads, key_part, preferred_element_type=...  265 us
    reduce_scatter x2, waiting for transfers between devices, body(): lax.psum_scatter(local[0].astype(jnp.bfloat16), 'dp', scatter_dimension=0...  251 us
    reduce_scatter x2, waiting for transfers between devices, body(): lax.psum_scatter(local[3].astype(jnp.bfloat16), 'dp', scatter_dimension=0...  245 us
    dot_general x8, matrix products, one_block(): jnp.einsum('qhd,khd->hqk', grad_heads, value_part, preferred_element_type...  165 us
    unnamed x325, local copies, waits for them, and re-layouts  150 us
    dot_general x10, matrix products, matmul(): return jnp.dot(left, right, preferred_element_type=FLOAT)  141 us
    dot_general x8, matrix products, right_outer(): lax.dot_general(left, right, (((1,), (1,)), ((), ())), preferred_element_...  136 us
  transfers between devices with their start and end apart: 34, of which 26 were waited for; matrix products, arithmetic and copies ran while one was open for 25% of the time, Pallas kernels for 0%

commit v1 on v0

--- a/solution.py
+++ b/solution.py
@@ -1,6 +1,10 @@
+import functools
+
 import jax
 import jax.numpy as jnp
 from jax import lax
+from jax.experimental import pallas as pl
+from jax.experimental.pallas import tpu as pltpu
 from jax.sharding import PartitionSpec as P
 
 HEADS = 16
@@ -272,7 +276,7 @@
     return (result, d_inputs, d_condition, local)
 
 
-def body(
+def general_body(
     tokens,
     cotangent,
     condition,
@@ -434,6 +438,1238 @@
     )
 
 
+HEAD = 72
+WINDOW = 256
+EXPONENT = HEAD**-0.5 * 1.4426950408889634
+
+
+def head_window(head, width):
+    start = jnp.minimum(lax.div(head * HEAD, 128) * 128, width - WINDOW)
+    return pl.ds(pl.multiple_of(start, 128), WINDOW), head * HEAD - start
+
+
+def head_lanes(offset, rows):
+    lane = lax.broadcasted_iota(jnp.int32, (rows, WINDOW), 1)
+    return (lane >= offset) & (lane < offset + HEAD)
+
+
+def for_images(info, unit, image):
+    @pl.when(info[8 + unit] == 1)
+    def _():
+        image(info[unit], 512, 256)
+
+    @pl.when(info[8 + unit] == 0)
+    def _():
+        def step(index, carry):
+            image(info[unit + index], 128, 128)
+            return carry
+
+        lax.fori_loop(0, 4, step, 0)
+
+
+def image_rows(start, strip, half, index, block):
+    place = index * block
+    place = start + (place if place < strip else half + place - strip)
+    return pl.ds(pl.multiple_of(place, 128), block)
+
+
+def both_strips(ref, start, strip, half, window):
+    return jnp.concatenate(
+        [ref[pl.ds(start, strip), window], ref[pl.ds(half + start, strip), window]], axis=0
+    )
+
+
+def attend_forward_kernel(info, q_ref, k_ref, v_ref, o_ref, total_ref, *, group):
+    half, width = q_ref.shape[0] // 2, q_ref.shape[1]
+
+    def image(start, strip, block):
+        start = pl.multiple_of(start, 128)
+        work = []
+        for member in range(group):
+            head = pl.program_id(1) * group + member
+            window, offset = head_window(head, width)
+            keys = both_strips(k_ref, start, strip, half, window)
+            keys = jnp.where(head_lanes(offset, 2 * strip), keys, jnp.zeros_like(keys))
+            values = both_strips(v_ref, start, strip, half, window).T
+            for index in range(2 * strip // block):
+                rows = image_rows(start, strip, half, index, block)
+                work.append((head, window, offset, keys, values, rows))
+
+        def scores_of(item):
+            return right_outer(item[3], q_ref[item[5], item[1]])
+
+        coming = scores_of(work[0])
+        for index, item in enumerate(work):
+            head, window, offset, keys, values, rows = item
+            scores = coming
+            if index + 1 < len(work):
+                coming = scores_of(work[index + 1])
+            top = jnp.max(scores, axis=0, keepdims=True)
+            expo = jnp.exp2((scores - top) * EXPONENT)
+            mass = jnp.sum(expo, axis=0, keepdims=True)
+            out = (matmul(values, expo.astype(HALF)) * (1.0 / mass)).T.astype(HALF)
+            o_ref[rows, window] = jnp.where(head_lanes(offset, block), out, o_ref[rows, window])
+            total_ref[head, :, rows] = top * EXPONENT + jnp.log2(mass)
+
+    for_images(info, pl.program_id(0), image)
+
+
+def attend_backward_kernel(
+    info, q_ref, k_ref, v_ref, do_ref, total_ref, dq_ref, dk_ref, dv_ref, *, group
+):
+    half, width = q_ref.shape[0] // 2, q_ref.shape[1]
+    scale = HEAD**-0.5
+
+    def image(start, strip, block):
+        start = pl.multiple_of(start, 128)
+        work = []
+        sums = {}
+        for member in range(group):
+            head = pl.program_id(1) * group + member
+            window, offset = head_window(head, width)
+            keys = both_strips(k_ref, start, strip, half, window)
+            values = both_strips(v_ref, start, strip, half, window)
+            inside = head_lanes(offset, 2 * strip)
+            head_keys = jnp.where(inside, keys, jnp.zeros_like(keys))
+            head_values = jnp.where(inside, values, jnp.zeros_like(values))
+            turned = keys.T
+            for index in range(2 * strip // block):
+                rows = image_rows(start, strip, half, index, block)
+                work.append((head, window, offset, head_keys, head_values, turned, rows))
+
+        def begin(item):
+            head, window, offset, keys, values, turned, rows = item
+            return (
+                right_outer(keys, q_ref[rows, window]),
+                right_outer(values, do_ref[rows, window]),
+            )
+
+        def middle(item, scores, d_weights):
+            weights = jnp.exp2(scores * EXPONENT - total_ref[item[0], :, item[6]])
+            product = weights * d_weights
+            delta = jnp.sum(product, axis=0, keepdims=True)
+            return weights.astype(HALF), (product - weights * delta).astype(HALF)
+
+        def finish(item, weights, d_scores):
+            head, window, offset, keys, values, turned, rows = item
+            d_keys = matmul(d_scores, q_ref[rows, window])
+            d_values = matmul(weights, do_ref[rows, window])
+            d_query = (matmul(turned, d_scores).T * scale).astype(HALF)
+            dq_ref[rows, window] = jnp.where(
+                head_lanes(offset, block), d_query, dq_ref[rows, window]
+            )
+            if id(keys) in sums:
+                d_keys, d_values = sums[id(keys)][0] + d_keys, sums[id(keys)][1] + d_values
+            sums[id(keys)] = (d_keys, d_values)
+
+        coming = begin(work[0])
+        late = None
+        for index, item in enumerate(work):
+            now = coming
+            if index + 1 < len(work):
+                coming = begin(work[index + 1])
+            if late is not None:
+                finish(*late)
+            late = (item,) + middle(item, *now)
+        finish(*late)
+        for item in work[:: 2 * strip // block]:
+            head, window, offset, keys = item[:4]
+            d_keys, d_values = sums[id(keys)]
+            lanes = head_lanes(offset, strip)
+            for ref, value in (
+                (dk_ref, (d_keys * scale).astype(HALF)),
+                (dv_ref, d_values.astype(HALF)),
+            ):
+                for first, part in ((start, value[:strip]), (half + start, value[strip:])):
+                    rows = pl.ds(pl.multiple_of(first, 128), strip)
+                    ref[rows, window] = jnp.where(lanes, part, ref[rows, window])
+
+    for_images(info, pl.program_id(0), image)
+
+
+def attention_call(kernel, name, info, arrays, outputs, group, flops):
+    def whole(array):
+        return pl.BlockSpec(
+            array.shape,
+            lambda unit, head, info: (0,) * len(array.shape),
+            pipeline_mode=pl.Buffered(1),
+        )
+
+    return pl.pallas_call(
+        functools.partial(kernel, group=group),
+        grid_spec=pltpu.PrefetchScalarGridSpec(
+            num_scalar_prefetch=1,
+            grid=(2, HEADS // group),
+            in_specs=[whole(array) for array in arrays],
+            out_specs=[whole(array) for array in outputs],
+        ),
+        out_shape=outputs,
+        compiler_params=pltpu.CompilerParams(vmem_limit_bytes=60 * 2**20),
+        cost_estimate=pl.CostEstimate(
+            flops=flops, bytes_accessed=30 * 2**20, transcendentals=HEADS * 2**21
+        ),
+        name=name,
+    )(info, *arrays)
+
+
+def attend_pack(info, query, keys, values):
+    rows, width = query.shape
+    outputs = [
+        jax.ShapeDtypeStruct((rows, width), HALF),
+        jax.ShapeDtypeStruct((HEADS, 1, rows), FLOAT),
+    ]
+    return attention_call(
+        attend_forward_kernel, "attend", info, [query, keys, values], outputs, 4, 70 * 10**9
+    )
+
+
+def attend_pack_backward(info, query, keys, values, grad, total):
+    outputs = [jax.ShapeDtypeStruct(query.shape, HALF)] * 3
+    arrays = [query, keys, values, grad, total]
+    return attention_call(
+        attend_backward_kernel, "attend_backward", info, arrays, outputs, 2, 140 * 10**9
+    )
+
+
+BLOCK = 256
+PART = 128
+STRIP = 32
+
+
+def resident(array):
+    return pl.BlockSpec(
+        array.shape, lambda *step: (0,) * len(array.shape), pipeline_mode=pl.Buffered(1)
+    )
+
+
+def by_rows(array):
+    size = BLOCK if len(array.shape) == 2 else BLOCK // PART
+    zeros = (0,) * (len(array.shape) - 1)
+    return pl.BlockSpec((size,) + array.shape[1:], lambda step: (step,) + zeros)
+
+
+def dense_call(kernel, name, inputs, outputs, scratch=(), flops=0):
+    rows = 2048
+    size = sum(array.size * array.dtype.itemsize for array, _ in inputs + outputs)
+    return pl.pallas_call(
+        kernel,
+        grid=(rows // BLOCK,),
+        in_specs=[spec for _, spec in inputs],
+        out_specs=[spec for _, spec in outputs],
+        out_shape=[shape for shape, _ in outputs],
+        scratch_shapes=list(scratch),
+        compiler_params=pltpu.CompilerParams(vmem_limit_bytes=60 * 2**20),
+        cost_estimate=pl.CostEstimate(flops=flops, bytes_accessed=size, transcendentals=0),
+        name=name,
+    )(*[array for array, _ in inputs])
+
+
+def shape_of(*dims, kind=None):
+    return jax.ShapeDtypeStruct(dims, kind or FLOAT)
+
+
+def strips():
+    return [
+        (pl.ds(begin, STRIP), begin // PART, begin % PART == 0) for begin in range(0, BLOCK, STRIP)
+    ]
+
+
+def row_norm(values):
+    center = values - jnp.mean(values, axis=1, keepdims=True)
+    inverse = lax.rsqrt(jnp.mean(center * center, axis=1, keepdims=True) + EPSILON)
+    return center * inverse, inverse
+
+
+def fold(values):
+    return jnp.sum(values.reshape(-1, 8, values.shape[1]), axis=0)
+
+
+class Sums:
+    def __init__(self):
+        self.held = {}
+
+    def add(self, ref, part, first, values):
+        folded = fold(values)
+        key = id(ref), part
+        if not first:
+            folded = self.held[key][1] + folded
+        self.held[key] = (ref, folded)
+
+    def store(self):
+        for (_, part), (ref, value) in self.held.items():
+            ref[part] = jnp.sum(value, axis=0, keepdims=True)
+
+
+TILE_ROWS = 32
+TILE_COLUMNS = 256
+
+
+def tiles(rows, columns):
+    return [
+        (row, column)
+        for row in range(0, rows, TILE_ROWS)
+        for column in range(0, columns, TILE_COLUMNS)
+    ]
+
+
+def up_kernel(x_ref, w_ref, bias_ref, act_ref, slope_ref, *, chunk):
+    x = x_ref[...]
+    halves, _, columns = w_ref.shape
+    work = [(half, begin) for half in range(halves) for begin in range(0, columns, chunk)]
+
+    def product(item):
+        return matmul(x, w_ref[item[0], :, pl.ds(item[1], chunk)])
+
+    coming = product(work[0])
+    for index, (half, begin) in enumerate(work):
+        now = coming
+        if index + 1 < len(work):
+            coming = product(work[index + 1])
+        for row, column in tiles(BLOCK, chunk):
+            rows = pl.ds(row, TILE_ROWS)
+            place = pl.ds(half * columns + begin + column, TILE_COLUMNS)
+            value = now[row : row + TILE_ROWS, column : column + TILE_COLUMNS] + bias_ref[:, place]
+            square = value * value
+            gate = 0.5 + 0.5 * jnp.tanh(
+                value * (GELU_SCALE + (GELU_SCALE * 0.044715) * square)
+            )
+            active = value * gate
+            bend = 2.0 * GELU_SCALE + (6.0 * GELU_SCALE * 0.044715) * square
+            act_ref[rows, place] = active.astype(HALF)
+            slope_ref[rows, place] = (gate + active * (1.0 - gate) * bend).astype(HALF)
+
+
+def up_call(hidden, weight, bias, chunk=768):
+    rows, width = hidden.shape
+    wide = 2 * weight.shape[2]
+    out = shape_of(rows, wide, kind=HALF)
+    return dense_call(
+        functools.partial(up_kernel, chunk=chunk),
+        "up",
+        [(hidden, by_rows(hidden)), (weight, resident(weight)), (bias, resident(bias))],
+        [(out, by_rows(out)), (out, by_rows(out))],
+        flops=2 * rows * width * wide,
+    )
+
+
+def down_grad_kernel(cot_ref, gate_ref, slope_ref, w_ref, d_branch_ref, d_pre_ref, sum_ref, wide_ref, *, chunk):
+    for rows, part, _ in strips():
+        d_branch_ref[rows, :] = (cot_ref[rows, :].astype(FLOAT) * gate_ref[part]).astype(HALF)
+    x = d_branch_ref[...]
+    sum_ref[0] = jnp.sum(fold(x.astype(FLOAT)), axis=0, keepdims=True)
+    wide = w_ref.shape[0]
+    work = list(range(0, wide, chunk))
+
+    def product(begin):
+        return right_outer(x, w_ref[pl.ds(begin, chunk), :])
+
+    coming = product(work[0])
+    for index, begin in enumerate(work):
+        now = coming
+        if index + 1 < len(work):
+            coming = product(work[index + 1])
+        for column in range(0, chunk, TILE_COLUMNS):
+            place = pl.ds(begin + column, TILE_COLUMNS)
+            total = None
+            for row in range(0, BLOCK, TILE_ROWS):
+                rows = pl.ds(row, TILE_ROWS)
+                value = now[row : row + TILE_ROWS, column : column + TILE_COLUMNS]
+                value = (value * slope_ref[rows, place].astype(FLOAT)).astype(HALF)
+                d_pre_ref[rows, place] = value
+                folded = fold(value.astype(FLOAT))
+                total = folded if total is None else total + folded
+            wide_ref[0, :, place] = jnp.sum(total, axis=0, keepdims=True)
+
+
+def down_grad_call(cotangent, gate, slope, weight, chunk=768):
+    rows, width = cotangent.shape
+    wide = weight.shape[0]
+    steps = rows // BLOCK
+    d_branch, d_pre = shape_of(rows, width, kind=HALF), shape_of(rows, wide, kind=HALF)
+    total, wide_total = shape_of(steps, 1, width), shape_of(steps, 1, wide)
+
+    def per_step(shape):
+        return pl.BlockSpec((1,) + shape.shape[1:], lambda step: (step, 0, 0))
+
+    return dense_call(
+        functools.partial(down_grad_kernel, chunk=chunk),
+        "down_grad",
+        [
+            (cotangent, by_rows(cotangent)),
+            (gate, by_rows(gate)),
+            (slope, by_rows(slope)),
+            (weight, resident(weight)),
+        ],
+        [
+            (d_branch, by_rows(d_branch)),
+            (d_pre, by_rows(d_pre)),
+            (total, per_step(total)),
+            (wide_total, per_step(wide_total)),
+        ],
+        flops=2 * rows * width * wide,
+    )
+
+
+def project_kernel(x_ref, shift_ref, scale_ref, w_ref, bias_ref, hidden_ref, q_ref, k_ref, v_ref):
+    for rows, part, _ in strips():
+        normed, _ = row_norm(x_ref[rows, :].astype(FLOAT))
+        hidden_ref[rows, :] = (normed * (1.0 + scale_ref[part]) + shift_ref[part]).astype(HALF)
+    hidden = hidden_ref[...]
+    width = hidden.shape[1]
+    for index, ref in enumerate((q_ref, k_ref, v_ref)):
+        place = pl.ds(index * width, width)
+        ref[...] = (matmul(hidden, w_ref[:, place]) + bias_ref[:, place]).astype(HALF)
+
+
+def project_call(tokens, shift, scale, weight, bias):
+    rows, width = tokens.shape
+    out = shape_of(rows, width, kind=HALF)
+    return dense_call(
+        project_kernel,
+        "project",
+        [
+            (tokens, by_rows(tokens)),
+            (shift, by_rows(shift)),
+            (scale, by_rows(scale)),
+            (weight, resident(weight)),
+            (bias, resident(bias)),
+        ],
+        [(out, by_rows(out))] * 4,
+        flops=6 * rows * width * width,
+    )
+
+
+def mix_kernel(
+    attended_ref, x_ref, gate_ref, shift_ref, scale_ref, w_ref, bias_ref, branch_ref, hidden_ref
+):
+    branch_ref[...] = matmul(attended_ref[...], w_ref[...]) + bias_ref[...]
+    for rows, part, _ in strips():
+        middle = x_ref[rows, :].astype(FLOAT) + gate_ref[part] * branch_ref[rows, :]
+        normed, _ = row_norm(middle)
+        hidden_ref[rows, :] = (normed * (1.0 + scale_ref[part]) + shift_ref[part]).astype(HALF)
+
+
+def mix_call(attended, tokens, gate, shift, scale, weight, bias):
+    rows, width = tokens.shape
+    branch, hidden = shape_of(rows, width), shape_of(rows, width, kind=HALF)
+    return dense_call(
+        mix_kernel,
+        "mix",
+        [
+            (attended, by_rows(attended)),
+            (tokens, by_rows(tokens)),
+            (gate, by_rows(gate)),
+            (shift, by_rows(shift)),
+            (scale, by_rows(scale)),
+            (weight, resident(weight)),
+            (bias, resident(bias)),
+        ],
+        [(branch, by_rows(branch)), (hidden, by_rows(hidden))],
+        flops=2 * rows * width * width,
+    )
+
+
+def finish_kernel(
+    act_ref, x_ref, branch_ref, cot_ref, gate_one_ref, gate_two_ref, w_ref, bias_ref,
+    own_ref, other_ref, sum_ref, branch_two,
+):
+    branch_two[...] = matmul(act_ref[...], w_ref[...]) + bias_ref[...]
+    step = pl.program_id(0)
+    sums = Sums()
+    for rows, part, first in strips():
+        middle = x_ref[rows, :].astype(FLOAT) + gate_one_ref[part] * branch_ref[rows, :]
+        two = branch_two[rows, :]
+        sums.add(sum_ref, part, first, cot_ref[rows, :].astype(FLOAT) * two)
+        branch_two[rows, :] = middle + gate_two_ref[part] * two
+    sums.store()
+    store_strip(step, branch_two, own_ref, other_ref)
+
+
+def store_strip(step, value_ref, own_ref, other_ref):
+    half = pl.num_programs(0) // 2
+
+    @pl.when(step < half)
+    def _():
+        own_ref[...] = value_ref[...]
+
+    @pl.when(step >= half)
+    def _():
+        other_ref[...] = value_ref[...].astype(HALF)
+
+
+def strip_specs(rows, width):
+    half = rows // BLOCK // 2
+    own, other = shape_of(rows // 2, width), shape_of(rows // 2, width, kind=HALF)
+    return [
+        (own, pl.BlockSpec((BLOCK, width), lambda step: (jnp.minimum(step, half - 1), 0))),
+        (other, pl.BlockSpec((BLOCK, width), lambda step: (jnp.maximum(step - half, 0), 0))),
+    ]
+
+
+def finish_call(active, tokens, branch, cotangent, gate_one, gate_two, weight, bias):
+    rows, width = tokens.shape
+    sums = shape_of(rows // PART, 1, width)
+    return dense_call(
+        finish_kernel,
+        "finish",
+        [
+            (active, by_rows(active)),
+            (tokens, by_rows(tokens)),
+            (branch, by_rows(branch)),
+            (cotangent, by_rows(cotangent)),
+            (gate_one, by_rows(gate_one)),
+            (gate_two, by_rows(gate_two)),
+            (weight, resident(weight)),
+            (bias, resident(bias)),
+        ],
+        strip_specs(rows, width) + [(sums, by_rows(sums))],
+        scratch=[pltpu.VMEM((BLOCK, width), FLOAT)],
+        flops=2 * rows * active.shape[1] * width,
+    )
+
+
+def norm_pull(normed, inverse, grad):
+    mean_grad = jnp.mean(grad, axis=1, keepdims=True)
+    mean_cross = jnp.mean(grad * normed, axis=1, keepdims=True)
+    return inverse * (grad - mean_grad - normed * mean_cross)
+
+
+def mix_grad_kernel(
+    d_pre_ref, x_ref, branch_ref, cot_ref, gate_ref, scale_ref, up_ref, out_ref,
+    d_middle_ref, d_branch_ref, d_attended_ref, shift_sum, scale_sum, gate_sum, bias_sum, hidden,
+):
+    columns = up_ref.shape[2]
+    hidden[...] = right_outer(d_pre_ref[:, :columns], up_ref[0]) + right_outer(
+        d_pre_ref[:, columns:], up_ref[1]
+    )
+    sums = Sums()
+    for rows, part, first in strips():
+        branch, grad = branch_ref[rows, :], hidden[rows, :]
+        gate = gate_ref[part]
+        normed, inverse = row_norm(x_ref[rows, :].astype(FLOAT) + gate * branch)
+        sums.add(shift_sum, part, first, grad)
+        sums.add(scale_sum, part, first, grad * normed)
+        d_middle = cot_ref[rows, :].astype(FLOAT) + norm_pull(
+            normed, inverse, grad * (1.0 + scale_ref[part])
+        )
+        d_middle_ref[rows, :] = d_middle
+        sums.add(gate_sum, part, first, d_middle * branch)
+        d_branch = (d_middle * gate).astype(HALF)
+        d_branch_ref[rows, :] = d_branch
+        sums.add(bias_sum, part, first, d_branch.astype(FLOAT))
+    sums.store()
+    d_attended_ref[...] = right_outer(d_branch_ref[...], out_ref[...]).astype(HALF)
+
+
+def mix_grad_call(d_pre, tokens, branch, cotangent, gate, scale, up, out):
+    rows, width = tokens.shape
+    half, sums = shape_of(rows, width, kind=HALF), shape_of(rows // PART, 1, width)
+    d_middle = shape_of(rows, width)
+    return dense_call(
+        mix_grad_kernel,
+        "mix_grad",
+        [
+            (d_pre, by_rows(d_pre)),
+            (tokens, by_rows(tokens)),
+            (branch, by_rows(branch)),
+            (cotangent, by_rows(cotangent)),
+            (gate, by_rows(gate)),
+            (scale, by_rows(scale)),
+            (up, resident(up)),
+            (out, resident(out)),
+        ],
+        [(d_middle, by_rows(d_middle)), (half, by_rows(half)), (half, by_rows(half))]
+        + [(sums, by_rows(sums))] * 4,
+        scratch=[pltpu.VMEM((BLOCK, width), FLOAT)],
+        flops=2 * rows * width * (d_pre.shape[1] + width),
+    )
+
+
+def project_grad_kernel(
+    dq_ref, dk_ref, dv_ref, x_ref, d_middle_ref, scale_ref, w_ref,
+    own_ref, other_ref, shift_sum, scale_sum, query_sum, value_sum, hidden,
+):
+    grads = jnp.concatenate([dq_ref[...], dk_ref[...], dv_ref[...]], axis=1)
+    hidden[...] = right_outer(grads, w_ref[...])
+    sums = Sums()
+    for rows, part, first in strips():
+        grad = hidden[rows, :]
+        normed, inverse = row_norm(x_ref[rows, :].astype(FLOAT))
+        sums.add(shift_sum, part, first, grad)
+        sums.add(scale_sum, part, first, grad * normed)
+        sums.add(query_sum, part, first, dq_ref[rows, :].astype(FLOAT))
+        sums.add(value_sum, part, first, dv_ref[rows, :].astype(FLOAT))
+        hidden[rows, :] = d_middle_ref[rows, :] + norm_pull(
+            normed, inverse, grad * (1.0 + scale_ref[part])
+        )
+    sums.store()
+    store_strip(pl.program_id(0), hidden, own_ref, other_ref)
+
+
+def project_grad_call(d_query, d_keys, d_values, tokens, d_middle, scale, weight):
+    rows, width = tokens.shape
+    sums = shape_of(rows // PART, 1, width)
+    return dense_call(
+        project_grad_kernel,
+        "project_grad",
+        [
+            (d_query, by_rows(d_query)),
+            (d_keys, by_rows(d_keys)),
+            (d_values, by_rows(d_values)),
+            (tokens, by_rows(tokens)),
+            (d_middle, by_rows(d_middle)),
+            (scale, by_rows(scale)),
+            (weight, resident(weight)),
+        ],
+        strip_specs(rows, width) + [(sums, by_rows(sums))] * 4,
+        scratch=[pltpu.VMEM((BLOCK, width), FLOAT)],
+        flops=6 * rows * width * width,
+    )
+
+
+MESH = pl.DeviceIdType.MESH
+
+
+class Place:
+    def __init__(self):
+        me = lax.axis_index("dp")
+        self.me, self.y = me, lax.axis_index("blk")
+        self.z, self.x, self.core = me // 4, (me // 2) % 2, me % 2
+
+    def at(self, z_step, x_step, core_step):
+        z = (self.z + 4 - z_step) % 4
+        return z * 4 + ((self.x + x_step) % 2) * 2 + (self.core + core_step) % 2
+
+    def half(self, y_step):
+        return (self.y + y_step) % 2
+
+    def partner(self, kind):
+        if kind == "y":
+            return {"blk": 1 - self.y}
+        if kind == "z":
+            return {"dp": (self.me + 4) % 16}
+        if kind == "back":
+            return {"dp": (self.me + 12) % 16}
+        if kind == "x":
+            return {"dp": self.at(0, 1, 0)}
+        return {"dp": self.at(0, 0, 1)}
+
+    def greet(self):
+        barrier = pltpu.get_barrier_semaphore()
+        for kind in ("y", "z", "back", "x", "core"):
+            pl.semaphore_signal(
+                barrier, inc=1, device_id=self.partner(kind), device_id_type=MESH
+            )
+        pl.semaphore_wait(barrier, 5)
+
+
+class Copies:
+    def __init__(self, place, send_sems, recv_sems):
+        self.place, self.send_sems, self.recv_sems = place, send_sems, recv_sems
+        self.made = {}
+
+    def send(self, key, source, target):
+        index = len(self.made)
+        copy = pltpu.make_async_remote_copy(
+            src_ref=source,
+            dst_ref=target,
+            send_sem=self.send_sems.at[index],
+            recv_sem=self.recv_sems.at[index],
+            device_id=self.place.partner(key[0]),
+            device_id_type=MESH,
+        )
+        self.made[key] = copy
+        copy.start()
+
+    def receive(self, key):
+        self.made[key].wait_recv()
+
+    def finish(self):
+        for copy in self.made.values():
+            copy.wait_send()
+
+
+def head_kernel(
+    shard_ref,
+    condition_ref,
+    adaptive_ref,
+    bias_ref,
+    tokens_ref,
+    whole_ref,
+    modulation_ref,
+    act_ref,
+    other_ref,
+    conditions,
+    parts,
+    from_core,
+    from_x,
+    from_z,
+    share,
+    from_y,
+    local_sem,
+    send_sems,
+    recv_sems,
+):
+    place = Place()
+    copies = Copies(place, send_sems, recv_sems)
+    place.greet()
+
+    own = pltpu.make_async_copy(
+        shard_ref, whole_ref.at[place.half(0), place.me], local_sem.at[0]
+    )
+    own.start()
+    conditions[place.me] = condition_ref[...]
+
+    def condition(kind, z_step, x_step):
+        slot = conditions.at[place.at(z_step, x_step, 0)]
+        copies.send((kind, "condition", z_step, x_step), slot, slot)
+
+    def weight(kind, y_step, z_step, x_step):
+        slot = whole_ref.at[place.half(y_step), place.at(z_step, x_step, 0)]
+        mine = y_step == 0 and z_step == 0 and x_step == 0
+        copies.send((kind, "weight", y_step, z_step, x_step), shard_ref if mine else slot, slot)
+
+    def forward_condition(z_step):
+        for x_step in range(2):
+            copies.receive(("z", "condition", z_step - 1, x_step))
+            if z_step < 3:
+                condition("z", z_step, x_step)
+            condition("core", z_step, x_step)
+
+    def forward(z_step, y_step):
+        copies.receive(("z", "weight", y_step, z_step - 1, 0))
+        if z_step < 3:
+            weight("z", y_step, z_step, 0)
+        weight("x", y_step, z_step, 0)
+        weight("core", y_step, z_step, 0)
+
+    condition("x", 0, 0)
+    condition("z", 0, 0)
+    condition("core", 0, 0)
+    weight("y", 0, 0, 0)
+    weight("z", 0, 0, 0)
+    weight("x", 0, 0, 0)
+    weight("core", 0, 0, 0)
+    copies.send(("y", "tokens"), tokens_ref.at[place.half(1)], other_ref)
+    copies.receive(("x", "condition", 0, 0))
+    condition("z", 0, 1)
+    condition("core", 0, 1)
+    forward_condition(1)
+    copies.receive(("y", "weight", 0, 0, 0))
+    weight("z", 1, 0, 0)
+    weight("x", 1, 0, 0)
+    weight("core", 1, 0, 0)
+    forward_condition(2)
+    forward(1, 0)
+    forward_condition(3)
+    forward(1, 1)
+    for z_step in range(4):
+        for x_step in range(2):
+            copies.receive(("core", "condition", z_step, x_step))
+
+    adaptive = adaptive_ref[...]
+    count, rows = conditions.shape[0], conditions.shape[2]
+    for index in range(count):
+        values = conditions[index, place.me].astype(FLOAT)
+        act_ref[index] = (values / (1.0 + jnp.exp(-values))).astype(HALF)
+
+    def products(z_step, core_step):
+        for x_step in range(2):
+            target = place.at((4 - z_step) % 4, x_step, core_step)
+            product = matmul(act_ref[target], adaptive)
+            parts[core_step, z_step, x_step] = product.astype(HALF)
+
+    def add(first, second):
+        return first.astype(FLOAT) + second.astype(FLOAT)
+
+    for z_step in (3, 2, 1, 0):
+        products(z_step, 1)
+        copies.send(("core", "part", z_step), parts.at[1, z_step], from_core.at[z_step])
+    forward(2, 0)
+    for z_step in (3, 2, 1, 0):
+        products(z_step, 0)
+    forward(2, 1)
+    for z_step in (3, 2, 1, 0):
+        copies.receive(("core", "part", z_step))
+        total = add(parts[0, z_step], from_core[z_step])
+        if z_step < 3:
+            copies.receive(("z", "part", z_step + 1))
+            total = total + from_z[z_step].astype(FLOAT)
+        parts[0, z_step] = total.astype(HALF)
+        if z_step > 0:
+            copies.send(("z", "part", z_step), parts.at[0, z_step], from_z.at[z_step - 1])
+        if z_step == 2:
+            forward(3, 0)
+        if z_step == 1:
+            forward(3, 1)
+    copies.send(("x", "part"), parts.at[0, 0, 1], from_x)
+
+    def last(z_step):
+        for y_step in range(2):
+            copies.receive(("x", "weight", y_step, z_step, 0))
+            weight("core", y_step, z_step, 1)
+
+    last(0)
+    last(1)
+    images = rows // 2
+    copies.receive(("x", "part"))
+    total = add(parts[0, 0, 0], from_x[...]) + bias_ref[...]
+    share[0] = total[:images]
+    share[1] = total[images:]
+    copies.send(("y", "part"), share.at[place.half(1)], from_y)
+    modulation_ref[place.half(0)] = share[place.half(0)]
+    last(2)
+    last(3)
+    copies.receive(("y", "part"))
+    modulation_ref[place.half(1)] = from_y[...]
+    for z_step in range(4):
+        for x_step in range(2):
+            for y_step in range(2):
+                copies.receive(("core", "weight", y_step, z_step, x_step))
+    copies.receive(("y", "tokens"))
+    own.wait()
+    copies.finish()
+
+
+def head(shard, condition, adaptive_weight, adaptive_bias, tokens):
+    micro, images, width = condition.shape
+    features = adaptive_weight.shape[0]
+    rows = micro * images
+    condition = condition.reshape(rows, width // features, features).transpose(1, 0, 2)
+    columns = adaptive_weight.shape[1]
+    count = 16
+    vmem = pl.BlockSpec(memory_space=pltpu.VMEM)
+    anywhere = pl.BlockSpec(memory_space=pl.ANY)
+    return pl.pallas_call(
+        head_kernel,
+        out_shape=[
+            jax.ShapeDtypeStruct((2, count) + shard.shape, HALF),
+            jax.ShapeDtypeStruct((2, images, columns), FLOAT),
+            jax.ShapeDtypeStruct((count, rows, features), HALF),
+            jax.ShapeDtypeStruct(tokens.shape[1:], HALF),
+        ],
+        in_specs=[anywhere, vmem, vmem, vmem, anywhere],
+        out_specs=[anywhere, vmem, vmem, anywhere],
+        scratch_shapes=[
+            pltpu.VMEM((count,) + condition.shape, HALF),
+            pltpu.VMEM((2, 4, 2, rows, columns), HALF),
+            pltpu.VMEM((4, 2, rows, columns), HALF),
+            pltpu.VMEM((rows, columns), HALF),
+            pltpu.VMEM((3, 2, rows, columns), HALF),
+            pltpu.VMEM((2, images, columns), FLOAT),
+            pltpu.VMEM((images, columns), FLOAT),
+            pltpu.SemaphoreType.DMA((1,)),
+            pltpu.SemaphoreType.DMA((64,)),
+            pltpu.SemaphoreType.DMA((64,)),
+        ],
+        compiler_params=pltpu.CompilerParams(
+            collective_id=1, has_side_effects=True, vmem_limit_bytes=48 * 2**20
+        ),
+        cost_estimate=pl.CostEstimate(flops=0, bytes_accessed=200 * 2**20, transcendentals=0),
+        name="head",
+    )(shard, condition, adaptive_weight, adaptive_bias.astype(FLOAT)[None], tokens)
+
+
+def tail_kernel(
+    grad_ref,
+    half_ref,
+    vector_ref,
+    strip_ref,
+    share_ref,
+    all_ref,
+    total_ref,
+    other_ref,
+    own,
+    from_core,
+    from_x,
+    from_z,
+    from_y,
+    pair,
+    pair_from_y,
+    vector,
+    vector_from,
+    vector_z,
+    local_sems,
+    send_sems,
+    recv_sems,
+):
+    place = Place()
+    copies = Copies(place, send_sems, recv_sems)
+    place.greet()
+
+    def grad(y_step, z_step, x_step, core_step):
+        return grad_ref.at[place.half(y_step), place.at((4 - z_step) % 4, x_step, core_step)]
+
+    def modulation(kind, z_step, x_step):
+        slot = all_ref.at[place.at(z_step, x_step, 0)]
+        copies.send((kind, "modulation", z_step, x_step), slot, slot)
+
+    copies.send(("y", "half"), half_ref.at[place.half(1)], pair_from_y)
+    copies.send(("core", "vector"), vector_ref, vector_from.at[0])
+    order = [(z_step, y_step) for z_step in (3, 2, 1, 0) for y_step in (1, 0)]
+    loads = {}
+    for x_step in (1, 0):
+        for z_step, y_step in order:
+            copies.send(
+                ("core", x_step, z_step, y_step),
+                grad(y_step, z_step, x_step, 1),
+                from_core.at[x_step, z_step, y_step],
+            )
+            load = pltpu.make_async_copy(
+                grad(y_step, z_step, x_step, 0),
+                own.at[x_step, z_step, y_step],
+                local_sems.at[len(loads)],
+            )
+            load.start()
+            loads[x_step, z_step, y_step] = load
+
+    copies.receive(("core", "vector"))
+    vector[0] = vector_ref[...] + vector_from[0]
+    copies.send(("x", "vector"), vector.at[0], vector_from.at[1])
+    pair[place.half(0)] = half_ref[place.half(0)]
+    copies.receive(("y", "half"))
+    pair[place.half(1)] = pair_from_y[...]
+    all_ref[place.me] = pair[...].reshape(all_ref.shape[1:]).astype(HALF)
+    modulation("x", 0, 0)
+    modulation("z", 0, 0)
+    modulation("core", 0, 0)
+
+    def summed(x_step, z_step, y_step):
+        loads[x_step, z_step, y_step].wait()
+        copies.receive(("core", x_step, z_step, y_step))
+        first = own[x_step, z_step, y_step].astype(FLOAT)
+        return first + from_core[x_step, z_step, y_step].astype(FLOAT)
+
+    def send_x(z_step):
+        for y_step in (1, 0):
+            own[1, z_step, y_step] = summed(1, z_step, y_step).astype(HALF)
+            copies.send(
+                ("x", z_step, y_step), own.at[1, z_step, y_step], from_x.at[z_step, y_step]
+            )
+
+    def forward_modulation(z_step):
+        for x_step in range(2):
+            copies.receive(("z", "modulation", z_step - 1, x_step))
+            if z_step < 3:
+                modulation("z", z_step, x_step)
+            modulation("core", z_step, x_step)
+
+    def vector_ring(z_step):
+        slot = vector_z.at[(place.z + 4 - z_step) % 4]
+        copies.send(("z", "vector", z_step), slot, slot)
+
+    send_x(3)
+    copies.receive(("x", "vector"))
+    vector[1] = vector[0] + vector_from[1]
+    copies.send(("y", "vector"), vector.at[1], vector_from.at[2])
+    copies.send(("y", "strip"), strip_ref, other_ref)
+    copies.receive(("x", "modulation", 0, 0))
+    modulation("z", 0, 1)
+    modulation("core", 0, 1)
+    send_x(2)
+    copies.receive(("y", "vector"))
+    vector_z[place.z] = vector[1] + vector_from[2]
+    vector_ring(0)
+    forward_modulation(1)
+    send_x(1)
+    copies.receive(("z", "vector", 0))
+    vector_ring(1)
+    forward_modulation(2)
+    send_x(0)
+    copies.receive(("z", "vector", 1))
+    vector_ring(2)
+    forward_modulation(3)
+    for z_step, y_step in order:
+        total = summed(0, z_step, y_step)
+        copies.receive(("x", z_step, y_step))
+        total = total + from_x[z_step, y_step].astype(FLOAT)
+        if z_step < 3:
+            copies.receive(("z", z_step + 1, y_step))
+            total = total + from_z[z_step, y_step].astype(FLOAT)
+        if z_step == 0 and y_step == 0:
+            copies.receive(("y",))
+            share_ref[...] = total + from_y[...].astype(FLOAT)
+            continue
+        own[0, z_step, y_step] = total.astype(HALF)
+        if z_step > 0:
+            copies.send(
+                ("z", z_step, y_step), own.at[0, z_step, y_step], from_z.at[z_step - 1, y_step]
+            )
+        else:
+            copies.send(("y",), own.at[0, 0, 1], from_y)
+    copies.receive(("z", "vector", 2))
+    total_ref[...] = (vector_z[0] + vector_z[1]) + (vector_z[2] + vector_z[3])
+    for z_step in range(4):
+        for x_step in range(2):
+            copies.receive(("core", "modulation", z_step, x_step))
+    copies.receive(("y", "strip"))
+    copies.finish()
+
+
+def tail(grad, half, vector, strip):
+    slot = grad.shape[2:]
+    count = grad.shape[1]
+    images, columns = half.shape[1:]
+    vmem = pl.BlockSpec(memory_space=pltpu.VMEM)
+    anywhere = pl.BlockSpec(memory_space=pl.ANY)
+    return pl.pallas_call(
+        tail_kernel,
+        out_shape=[
+            jax.ShapeDtypeStruct(slot, FLOAT),
+            jax.ShapeDtypeStruct((count, 2 * images, columns), HALF),
+            jax.ShapeDtypeStruct(vector.shape, FLOAT),
+            jax.ShapeDtypeStruct(strip.shape, HALF),
+        ],
+        in_specs=[anywhere, vmem, vmem, anywhere],
+        out_specs=[vmem, vmem, vmem, anywhere],
+        scratch_shapes=[
+            pltpu.VMEM((2, 4, 2) + slot, HALF),
+            pltpu.VMEM((2, 4, 2) + slot, HALF),
+            pltpu.VMEM((4, 2) + slot, HALF),
+            pltpu.VMEM((3, 2) + slot, HALF),
+            pltpu.VMEM(slot, HALF),
+            pltpu.VMEM(half.shape, FLOAT),
+            pltpu.VMEM(half.shape[1:], FLOAT),
+            pltpu.VMEM((2,) + vector.shape, FLOAT),
+            pltpu.VMEM((3,) + vector.shape, FLOAT),
+            pltpu.VMEM((4,) + vector.shape, FLOAT),
+            pltpu.SemaphoreType.DMA((16,)),
+            pltpu.SemaphoreType.DMA((64,)),
+            pltpu.SemaphoreType.DMA((64,)),
+        ],
+        compiler_params=pltpu.CompilerParams(
+            collective_id=2, has_side_effects=True, vmem_limit_bytes=48 * 2**20
+        ),
+        cost_estimate=pl.CostEstimate(flops=0, bytes_accessed=200 * 2**20, transcendentals=0),
+        name="tail",
+    )(grad, half, vector, strip)
+
+
+def swap_blk(value):
+    return lax.ppermute(value, "blk", [(0, 1), (1, 0)])
+
+
+def gather_weight(shard):
+    halves = lax.all_gather(shard, ("blk", "dp"), axis=0, tiled=True)
+    rows = halves.shape[0] // 2
+    return jnp.concatenate([halves[:rows], halves[rows:]], axis=1)
+
+
+def share_columns(total, me_blk):
+    half = total.shape[1] // 2
+    keep = lax.dynamic_slice_in_dim(total, me_blk * half, half, 1)
+    send = lax.dynamic_slice_in_dim(total, (1 - me_blk) * half, half, 1)
+    return keep.astype(FLOAT) + swap_blk(send).astype(FLOAT)
+
+
+def order_blk(first, mine, other, axis):
+    return jnp.concatenate(
+        [jnp.where(first, mine, other), jnp.where(first, other, mine)], axis=axis
+    )
+
+
+def pair_body(
+    tokens,
+    cotangent,
+    condition,
+    lengths,
+    adaptive_weight,
+    joint_weight,
+    output_weight,
+    up_weight,
+    down_weight,
+    adaptive_bias,
+    query_bias,
+    value_bias,
+    output_bias,
+    up_bias,
+    down_bias,
+):
+    me_dp, me_blk = lax.axis_index("dp"), lax.axis_index("blk")
+    first = me_blk == 0
+    strip_rows, width = tokens.shape[2:]
+    rows = 2 * strip_rows
+    parts = strip_rows // 128
+    images = lengths.shape[2]
+
+    def mine_of(pair):
+        return lax.dynamic_index_in_dim(pair, me_blk, 0, keepdims=False)
+
+    def other_of(pair):
+        return lax.dynamic_index_in_dim(pair, 1 - me_blk, 0, keepdims=False)
+
+    cut = joint_weight.shape[1]
+    halves, modulation, act_part, tokens_other = head(
+        jnp.concatenate([joint_weight, output_weight], axis=1),
+        condition[0],
+        adaptive_weight,
+        adaptive_bias,
+        tokens[0],
+    )
+    modulation = jnp.concatenate([modulation[0], modulation[1]], axis=1)
+
+    bias_mine = jnp.concatenate([query_bias, value_bias, output_bias, down_bias, up_bias])
+    bias_other = swap_blk(bias_mine)
+    small = width // 2
+
+    def bias_of(begin, size):
+        return order_blk(
+            first, bias_mine[begin : begin + size], bias_other[begin : begin + size], 0
+        ).astype(FLOAT)
+
+    query_vector, value_vector = bias_of(0, small), bias_of(small, small)
+    output_vector, down_vector = bias_of(2 * small, small), bias_of(3 * small, small)
+    up_vector = bias_of(4 * small, up_bias.shape[0])
+
+    halves, up_weight, down_weight = lax.optimization_barrier((halves, up_weight, down_weight))
+    halves = halves.reshape(2, width, -1)
+    joint = jnp.concatenate([halves[0, :, :cut], halves[1, :, :cut]], axis=1)
+    output_matrix = jnp.concatenate([halves[0, :, cut:], halves[1, :, cut:]], axis=1)
+    up_halves = lax.all_gather(up_weight, ("blk", "dp"), axis=0, tiled=True)
+    up_halves = up_halves.reshape(2, width, -1)
+    cotangent_other = swap_blk(other_of(cotangent[0]))
+
+    strip = mine_of(lengths[0]) // 2
+    ends = jnp.cumsum(strip)
+    starts = ends - strip
+    begin = jnp.arange(parts, dtype=jnp.int32)[:, None] * 128
+    inside = (begin >= starts[None, :]) & (begin < ends[None, :])
+    member = jnp.tile(inside.astype(FLOAT), (2, 1))
+    long = strip == 512
+    used = strip > 0
+    rank = jnp.where(
+        long,
+        jnp.cumsum(long) - 1,
+        jnp.where(used, jnp.sum(long) + jnp.cumsum(used & ~long) - 1, images + 8),
+    )
+    info = jnp.sum(
+        jnp.where(rank[:, None] == jnp.arange(8)[None, :], starts[:, None], 0), axis=0
+    )
+    kinds = jnp.where(jnp.arange(8) < jnp.sum(long), 1, 0)
+    info = jnp.concatenate([info, kinds]).astype(jnp.int32)
+
+    per_part = jnp.dot(member, modulation, precision=HIGHEST, preferred_element_type=FLOAT)
+    per_part = per_part.reshape(2 * parts, 1, 6, width)
+    shift_one, scale_one, gate_one, shift_two, scale_two, gate_two = (
+        per_part[:, :, index] for index in range(6)
+    )
+
+    inputs = jnp.concatenate([mine_of(tokens[0]), tokens_other], axis=0)
+    joint_vector = jnp.concatenate([query_vector, jnp.zeros_like(query_vector), value_vector])
+    hidden_one, query, keys, values = project_call(
+        inputs, shift_one, scale_one, joint, joint_vector[None]
+    )
+    query, down_weight = lax.optimization_barrier((query, down_weight))
+    down_matrix = gather_weight(down_weight)
+    attended, total = attend_pack(info, query, keys, values)
+    branch_one, hidden_two = mix_call(
+        attended, inputs, gate_one, shift_two, scale_two, output_matrix, output_vector[None]
+    )
+    activated, slope = up_call(hidden_two, up_halves, up_vector[None])
+
+    upstream = jnp.concatenate([mine_of(cotangent[0]), cotangent_other], axis=0)
+    d_branch_two, d_pre, down_sum, up_sum = down_grad_call(
+        upstream, gate_two, slope, down_matrix
+    )
+    d_pre, down_grad = lax.optimization_barrier(
+        (d_pre, left_outer(activated, d_branch_two).astype(HALF))
+    )
+    down_total = lax.psum_scatter(down_grad, "dp", scatter_dimension=0, tiled=True)
+    d_pre, up_grad = lax.optimization_barrier(
+        (d_pre, left_outer(hidden_two, d_pre).astype(HALF))
+    )
+    up_total = lax.psum_scatter(up_grad, "dp", scatter_dimension=0, tiled=True)
+    result, result_send, d_gate_two = finish_call(
+        activated, inputs, branch_one, upstream, gate_one, gate_two, down_matrix, down_vector[None]
+    )
+    d_pre, result_send = lax.optimization_barrier((d_pre, result_send))
+    result_other = swap_blk(result_send)
+    d_middle, d_branch_one, d_attended, d_shift_two, d_scale_two, d_gate_one, output_sum = (
+        mix_grad_call(
+            d_pre, inputs, branch_one, upstream, gate_one, scale_two, up_halves, output_matrix
+        )
+    )
+    d_attended, output_grad, down_total = lax.optimization_barrier(
+        (d_attended, left_outer(attended, d_branch_one).astype(HALF), down_total)
+    )
+    down_share = share_columns(down_total, me_blk)
+    d_query, d_keys, d_values = attend_pack_backward(
+        info, query, keys, values, d_attended, total
+    )
+    d_query, up_total, result_other = lax.optimization_barrier((d_query, up_total, result_other))
+    up_share = share_columns(up_total, me_blk)
+    d_projected = jnp.concatenate([d_query, d_keys, d_values], axis=1)
+    joint_grad = left_outer(hidden_one, d_projected).astype(HALF)
+    d_inputs, d_inputs_send, d_shift_one, d_scale_one, query_sum, value_sum = project_grad_call(
+        d_query, d_keys, d_values, inputs, d_middle, scale_one, joint
+    )
+
+    def part_rows(value):
+        return value.reshape(2 * parts, width)
+
+    d_parts = [d_shift_one, d_scale_one, d_gate_one, d_shift_two, d_scale_two, d_gate_two]
+    d_parts = jnp.concatenate([part_rows(value) for value in d_parts], axis=1)
+    d_modulation = lax.dot_general(
+        member,
+        d_parts,
+        (((0,), (0,)), ((), ())),
+        precision=HIGHEST,
+        preferred_element_type=FLOAT,
+    )
+    vectors = [query_sum, value_sum, output_sum, down_sum, up_sum]
+    sums = jnp.concatenate([jnp.sum(value, axis=(0, 1)) for value in vectors])
+    narrow = output_weight.shape[1]
+    grad_halves = jnp.stack(
+        [
+            jnp.concatenate([joint_grad[:, :cut], output_grad[:, :narrow]], axis=1),
+            jnp.concatenate([joint_grad[:, cut:], output_grad[:, narrow:]], axis=1),
+        ]
+    )
+    shard_rows = adaptive_weight.shape[0]
+    share, d_mod_all, sums, d_inputs_other = tail(
+        grad_halves.reshape(2, 16, shard_rows, -1),
+        d_modulation.reshape(images, 2, -1).transpose(1, 0, 2),
+        sums.reshape(-1, 128),
+        d_inputs_send,
+    )
+    joint_share, output_share = share[:, :cut], share[:, cut:]
+    sums = sums.reshape(-1)
+    d_mod_all = d_mod_all.reshape(-1, d_mod_all.shape[2])
+    adaptive_share = left_outer(act_part.reshape(-1, shard_rows), d_mod_all)
+    adaptive_vector_share = jnp.sum(d_mod_all.astype(FLOAT), axis=0)
+    d_act = right_outer(d_mod_all, adaptive_weight)
+    d_act = d_act.reshape(16, 2 * images, shard_rows)
+    d_act = lax.all_to_all(d_act, "dp", 0, 0)
+    d_act = d_act + swap_blk(d_act)
+    d_act = d_act.transpose(1, 0, 2).reshape(2, images, width)
+    condition_full = condition[0].astype(FLOAT)
+    sigmoid_cond = jax.nn.sigmoid(condition_full)
+    d_condition = d_act * sigmoid_cond * (1.0 + condition_full * (1.0 - sigmoid_cond))
+
+    def share_of(begin, size):
+        return lax.dynamic_slice_in_dim(sums, begin + me_blk * (size // 2), size // 2, 0)
+
+    def both(mine, other):
+        return order_blk(first, mine[None], other.astype(FLOAT)[None], 0)[None]
+
+    return (
+        both(result, result_other),
+        both(d_inputs, d_inputs_other),
+        d_condition[None],
+        adaptive_share,
+        joint_share,
+        output_share,
+        up_share,
+        down_share,
+        adaptive_vector_share,
+        share_of(0, width),
+        share_of(width, width),
+        share_of(2 * width, width),
+        share_of(4 * width, 2 * up_bias.shape[0]),
+        share_of(3 * width, width),
+    )
+
+
 def solution(mesh):
     in_specs = (
         P("dp", None, "blk", None),
@@ -468,4 +1704,6 @@
         P("blk"),
         P("blk"),
     )
+    paired = mesh.shape["dp"] == 16 and mesh.shape["blk"] == 2
+    body = pair_body if paired else general_body
     return jax.shard_map(body, mesh=mesh, in_specs=in_specs, out_specs=out_specs, check_vma=False)

time: 3550 us -> 828 us (0.23)
  waiting for transfers between devices: 1440 us -> 4.06 us
  matrix products: 1350 us -> 102 us
  Pallas kernels: 0 us -> 582 us
  local copies, waits for them, and re-layouts: 279 us -> 40.6 us
  other arithmetic: 296 us -> 66.5 us
  blocking collectives: 157 us -> 0 us
    dot_general x74 -> x2, matrix products: 1090 us -> 0.9 us  [the longest x1 0.56 us: pair_body(): jnp.dot(member, modulation, precision=HIGHEST, preferred_element_type=FLOAT)]
    reduce_scatter x12 -> x2, waiting for transfers between devices: 815 us -> 0.01 us  [the longest x1 0.01 us: pair_body(): lax.psum_scatter(down_grad, 'dp', scatter_dimension=0, tiled=True)]
    pallas_call x0 -> x11, Pallas kernels: none -> 582 us  [the longest x7 246 us: dense_call(): pl.pallas_call(kernel, grid=(rows // BLOCK,), in_specs=[spec for _, spec...]
    unnamed x46 -> x4, waiting for transfers between devices: 415 us -> 0.07 us
    all_gather x9 -> x2, waiting for transfers between devices: 198 us -> 0.01 us  [the longest x1 0.01 us: pair_body(): up_halves = lax.all_gather(up_weight, ('blk', 'dp'), axis=0, tiled=True)]
    reduce_sum x25 -> x8, other arithmetic: 168 us -> 4.6 us  [the longest x5 2.99 us: pair_body(): sums = jnp.concatenate([jnp.sum(value, axis=(0, 1)) for value in vectors])]
    unnamed x325 -> x77, local copies, waits for them, and re-layouts: 150 us -> 6.37 us
    dot_general x8 -> x1, matrix products: 136 us -> 1.29 us  [right_outer(): lax.dot_general(left, right, (((1,), (1,)), ((), ())), preferred_element_...]
  transfers between devices with their start and end apart: 34 -> 11, of which waited for: 26 -> 1; matrix products, arithmetic and copies ran while one was open for 25% -> 13% of each run, Pallas kernels for 0% -> 44%
where the time goes in v1:
time: 828 us; the launch traced here: 819 us
  Pallas kernels  582 us (70%)
  matrix products  102 us (12%)
  other arithmetic  66.5 us (8%)
  local copies, waits for them, and re-layouts  40.6 us (5%)
  between operations  14.9 us (2%)
  starting transfers between devices  9.37 us (1%)
    pallas_call x7, Pallas kernels, dense_call(): pl.pallas_call(kernel, grid=(rows // BLOCK,), in_specs=[spec for _, spec...  246 us
    pallas_call x2, Pallas kernels, attention_call(): pl.pallas_call(functools.partial(kernel, group=group), grid_spec=pltpu.Pr...  180 us
    dot_general x5, matrix products, left_outer(): lax.dot_general(left, right, (((0,), (0,)), ((), ())), preferred_element_...  99.4 us
    pallas_call x1, Pallas kernels, head(): pl.pallas_call(head_kernel, out_shape=[jax.ShapeDtypeStruct((2, count) +...  84.9 us
    pallas_call x1, Pallas kernels, tail(): pl.pallas_call(tail_kernel, out_shape=[jax.ShapeDtypeStruct(slot, FLOAT),...  71.2 us
  transfers between devices with their start and end apart: 11, of which 1 were waited for; matrix products, arithmetic and copies ran while one was open for 13% of the time, Pallas kernels for 44%

profile of v1, /device:TPU:0, one launch (start us, length us, event | category | flops | bytes accessed | tf_op | source)
XLA Modules:
  0.0 819.3 jit_solution(10495290855831156130)
XLA Ops:
  11.1 84.9 %head.1 = (bf16[2,16,72,2304]{3,2,1,0:T(8,128)(2,1)}, f32[2,8,3456]{2,1,0:T(8,128)S(1)}, bf16[16,16,72]{2,1,0:T(8,128)(2,1)S(1)}, bf16[1024,1152]{1,0:T(8,128)(2,1)S(1)}) custom-call(bf16[72,2304]{1,0:T(8,128)(2,1)S(1)} %pad_maximum_fusion.8.shard_ref, bf16[16,16,72]{2,1,0:T(8,128)(2,1)S(1)} %bitcast.126, bf16[72,3456]{1,0:T(8,128)(2,1)S(1)} %copy-done.2, ...), custom_call_target="tpu_custom_call" | custom-call | bytes 209715200 | tf_op jit(solution)/shard_map/head/pallas_call | solution.py:1243
  100.8 2.8 pad_maximum_fusion.5.x_ref
  105.4 3.6 slice_bitcast_fusion.1
  109.0 9.0 %pad_maximum_fusion.2.w_ref = bf16[1152,3456]{1,0:T(8,128)(2,1)} fusion(bf16[1152,1728]{1,0:T(8,128)(2,1)} %get-tuple-element.139, bf16[1152,1728]{1,0:T(8,128)(2,1)} %get-tuple-element.138), kind=kLoop, calls=%fused_computation.12 | loop fusion | flops 15925248 | bytes 15925248 | tf_op jit(solution)/shard_map/concatenate | solution.py:1526
  120.9 28.3 %project.1 = (bf16[2048,1152]{1,0:T(8,128)(2,1)}, bf16[2048,1152]{1,0:T(8,128)(2,1)}, bf16[2048,1152]{1,0:T(8,128)(2,1)}, bf16[2048,1152]{1,0:T(8,128)(2,1)}) custom-call(bf16[2048,1152]{1,0:T(8,128)(2,1)} %pad_maximum_fusion.5.x_ref, f32[16,1,1152]{2,1,0:T(1,128)} %bitcast.139, f32[16,1,1152]{2,1,0:T(1,128)} %get-tuple-element.183.scale_ref, ...), custom_call_target="tpu_custom_call" | custom-call | flops 16307453952 | bytes 31716864 | tf_op jit(solution)/shard_map/project/pallas_call | solution.py:654
  149.4 4.2 dynamic-slice_bitcast_fusion.1
  158.1 3.4 slice_bitcast_fusion.3
  163.9 63.6 %attend.1 = (bf16[2048,1152]{1,0:T(8,128)(2,1)}, f32[16,1,2048]{2,1,0:T(1,128)}) custom-call(s32[16]{0:T(128)} %pad_add_fusion.info, bf16[2048,1152]{1,0:T(8,128)(2,1)} %get-tuple-element.78.q_ref, bf16[2048,1152]{1,0:T(8,128)(2,1)} %get-tuple-element.79.k_ref, bf16[2048,1152]{1,0:T(8,128)(2,1)} %get-tuple-element.80.v_ref), custom_call_target="tpu_custom_call" | custom-call | flops 70000001024 | bytes 31457280 | tf_op jit(solution)/shard_map/attend/pallas_call | solution.py:598
  228.3 14.9 %mix.1 = (f32[2048,1152]{1,0:T(8,128)}, bf16[2048,1152]{1,0:T(8,128)(2,1)}) custom-call(bf16[2048,1152]{1,0:T(8,128)(2,1)} %get-tuple-element.81.attended_ref, bf16[2048,1152]{1,0:T(8,128)(2,1)} %pad_maximum_fusion.5.x_ref, f32[16,1,1152]{2,1,0:T(1,128)} %get-tuple-element.181.gate_ref.gate_one_ref, f32[16,1,1152]{2,1,0:T(1,128)} %get-tuple-element.182.shift_ref, ...), custom_call_target="tpu_custom_call" | custom-call | flops 5435817984 | bytes 26472960 | tf_op jit(solution)/shard_map/mix/pallas_call | solution.py:654
  243.8 4.1 pad_maximum_fusion.6.cot_ref
  247.9 46.4 %up.1 = (bf16[2048,4608]{1,0:T(8,128)(2,1)}, bf16[2048,4608]{1,0:T(8,128)(2,1)}) custom-call(bf16[2048,1152]{1,0:T(8,128)(2,1)} %get-tuple-element.82.x_ref, bf16[2,1152,2304]{2,1,0:T(8,128)(2,1)} %bitcast.141, f32[1,4608]{1,0:T(1,128)} %maximum_convert_fusion.bias_ref), custom_call_target="tpu_custom_call" | custom-call | flops 21743271936 | bytes 53102592 | tf_op jit(solution)/shard_map/up/pallas_call | solution.py:654
  294.3 5.2 fusion.20
  299.5 7.7 pad_maximum_fusion.w_ref
  307.2 34.8 %down_grad.1 = (bf16[2048,1152]{1,0:T(8,128)(2,1)}, bf16[2048,4608]{1,0:T(8,128)(2,1)}, f32[8,1,1152]{2,1,0:T(1,128)}, f32[8,1,4608]{2,1,0:T(1,128)}) custom-call(bf16[2048,1152]{1,0:T(8,128)(2,1)} %pad_maximum_fusion.6.cot_ref, f32[16,1,1152]{2,1,0:T(1,128)} %get-tuple-element.180.gate_two_ref.gate_ref, bf16[2048,4608]{1,0:T(8,128)(2,1)} %get-tuple-element.88.slope_ref, ...), custom_call_target="tpu_custom_call" | custom-call | flops 21743271936 | bytes 58060800 | tf_op jit(solution)/shard_map/down_grad/pallas_call | solution.py:654
  342.0 30.9 %convolution_convert_fusion.1 = bf16[4608,1152]{1,0:T(8,128)(2,1)} fusion(bf16[2048,4608]{1,0:T(8,128)(2,1)} %get-tuple-element.84.act_ref, bf16[2048,1152]{1,0:T(8,128)(2,1)} %get-tuple-element.90), kind=kOutput, calls=%fused_computation.1 | convolution fusion | flops 21748580352 | bytes 34209792 | tf_op jit(solution)/shard_map/dot_general | solution.py:25
  374.3 30.1 %convolution_convert_fusion = bf16[1152,4608]{1,0:T(8,128)(2,1)} fusion(bf16[2048,1152]{1,0:T(8,128)(2,1)} %get-tuple-element.82.x_ref, bf16[2048,4608]{1,0:T(8,128)(2,1)} %get-tuple-element.94.d_pre_ref), kind=kOutput, calls=%fused_computation | convolution fusion | flops 21748580352 | bytes 34209792 | tf_op jit(solution)/shard_map/dot_general | solution.py:25
  404.4 34.3 %finish.1 = (f32[1024,1152]{1,0:T(8,128)}, bf16[1024,1152]{1,0:T(8,128)(2,1)}, f32[16,1,1152]{2,1,0:T(1,128)}) custom-call(bf16[2048,4608]{1,0:T(8,128)(2,1)} %get-tuple-element.84.act_ref, bf16[2048,1152]{1,0:T(8,128)(2,1)} %pad_maximum_fusion.5.x_ref, f32[2048,1152]{1,0:T(8,128)} %get-tuple-element.85.branch_ref, ...), custom_call_target="tpu_custom_call" | custom-call | flops 21743271936 | bytes 55669248 | tf_op jit(solution)/shard_map/finish/pallas_call | solution.py:654
  438.7 55.8 %mix_grad.1 = (f32[2048,1152]{1,0:T(8,128)}, bf16[2048,1152]{1,0:T(8,128)(2,1)}, bf16[2048,1152]{1,0:T(8,128)(2,1)}, f32[16,1,1152]{2,1,0:T(1,128)}, f32[16,1,11...) custom-call(bf16[2048,4608]{1,0:T(8,128)(2,1)} %get-tuple-element.94.d_pre_ref, ...), custom_call_target="tpu_custom_call" | custom-call | flops 27179089920 | bytes 70336512 | tf_op jit(solution)/shard_map/mix_grad/pallas_call | solution.py:654
  497.4 12.1 %convolution_convert_fusion.3 = bf16[1152,1152]{1,0:T(8,128)(2,1)} fusion(bf16[2048,1152]{1,0:T(8,128)(2,1)} %get-tuple-element.81.attended_ref, bf16[2048,1152]{1,0:T(8,128)(2,1)} %get-tuple-element.96), kind=kOutput, calls=%fused_computation.13 | convolution fusion | flops 5437145088 | bytes 12091392 | tf_op jit(solution)/shard_map/dot_general | solution.py:25
  509.4 116.2 %attend_backward.1 = (bf16[2048,1152]{1,0:T(8,128)(2,1)}, bf16[2048,1152]{1,0:T(8,128)(2,1)}, bf16[2048,1152]{1,0:T(8,128)(2,1)}) custom-call(s32[16]{0:T(128)} %pad_add_fusion.info, bf16[2048,1152]{1,0:T(8,128)(2,1)} %get-tuple-element.78.q_ref, bf16[2048,1152]{1,0:T(8,128)(2,1)} %get-tuple-element.79.k_ref, bf16[2048,1152]{1,0:T(8,128)(2,1)} %get-tuple-element.80.v_ref, ...), custom_call_target="tpu_custom_call" | custom-call | flops 140000002048 | bytes 31457280 | tf_op jit(solution)/shard_map/attend_backward/pallas_call | solution.py:598
  625.7 32.0 %project_grad.1 = (f32[1024,1152]{1,0:T(8,128)}, bf16[1024,1152]{1,0:T(8,128)(2,1)}, f32[16,1,1152]{2,1,0:T(1,128)}, f32[16,1,1152]{2,1,0:T(1,128)}, f32[16,1,1152]{2,1,0:T(1,128)}, /*index=5*/f32[16,1,1152]{2,1,0:T(1,128)}) custom-call(bf16[2048,1152]{1,0:T(8,128)(2,1)} %get-tuple-element.104.dq_ref, bf16[2048,1152]{1,0:T(8,128)(2,1)} %get-tuple-element.105.dk_ref, ...), custom_call_target="tpu_custom_call" | custom-call | flops 16307453952 | bytes 43720704 | tf_op jit(solution)/shard_map/project_grad/pallas_call | solution.py:654
  657.7 25.0 %convolution_convert_fusion.2 = bf16[1152,3456]{1,0:T(8,128)(2,1)} fusion(bf16[2048,1152]{1,0:T(8,128)(2,1)} %get-tuple-element.109, bf16[2048,1152]{1,0:T(8,128)(2,1)} %get-tuple-element.106.dv_ref, bf16[2048,1152]{1,0:T(8,128)(2,1)} %get-tuple-element.105.dk_ref, bf16[2048,1152]{1,0:T(8,128)(2,1)} %get-tuple-element.104.dq_ref), kind=kOutput, calls=%fused_computation.2 | convolution fusion | flops 16353902592 | bytes 26836992 | tf_op jit(solution)/shard_map/dot_general | solution.py:25
  682.8 4.6 fusion.21
  690.4 2.4 pad_maximum_fusion.3
  695.3 5.2 pad_maximum_fusion.1.grad_ref
  700.5 71.2 %tail.1 = (f32[72,2304]{1,0:T(8,128)S(1)}, bf16[16,16,3456]{2,1,0:T(8,128)(2,1)S(1)}, f32[72,128]{1,0:T(8,128)S(1)}, bf16[1024,1152]{1,0:T(8,128)(2,1)S(1)}) custom-call(bf16[2,16,72,2304]{3,2,1,0:T(8,128)(2,1)} %pad_maximum_fusion.1.grad_ref, f32[2,8,3456]{2,1,0:T(8,128)S(1)} %convolution_bitcast_fusion.1.half_ref, f32[72,128]{1,0:T(8,128)S(1)} %bitcast.127, ...), custom_call_target="tpu_custom_call" | custom-call | bytes 209715200 | tf_op jit(solution)/shard_map/tail/pallas_call | solution.py:1415
  781.1 3.5 all-to-all-start
  784.7 3.7 fusion.5
  788.4 4.3 maximum_bitcast_fusion
  793.4 3.1 fusion.7
  796.5 4.3 maximum_bitcast_fusion.1
  803.6 4.0 collective-permute-done.3
  (169 shorter events, 48.9 us)
Async XLA Ops:
  7.2 88.8 %copy-start.26 = (bf16[576]{0:T(1024)(128)(2,1)S(1)}, bf16[576]{0:T(1024)(128)(2,1)}, u32[]{:S(2)}) copy-start(bf16[576]{0:T(1024)(128)(2,1)} %param.29) | copy-start | bytes 3460
  7.2 88.8 %copy-start.25 = (bf16[2304]{0:T(1024)(128)(2,1)S(1)}, bf16[2304]{0:T(1024)(128)(2,1)}, u32[]{:S(2)}) copy-start(bf16[2304]{0:T(1024)(128)(2,1)} %param.28) | copy-start | bytes 13828
  7.2 88.8 %copy-start.29 = (bf16[576]{0:T(1024)(128)(2,1)S(1)}, bf16[576]{0:T(1024)(128)(2,1)}, u32[]{:S(2)}) copy-start(bf16[576]{0:T(1024)(128)(2,1)} %param.27) | copy-start | bytes 3460
  7.2 88.8 %copy-start.28 = (bf16[576]{0:T(1024)(128)(2,1)S(1)}, bf16[576]{0:T(1024)(128)(2,1)}, u32[]{:S(2)}) copy-start(bf16[576]{0:T(1024)(128)(2,1)} %param.26) | copy-start | bytes 3460
  7.2 88.8 %copy-start.27 = (bf16[576]{0:T(1024)(128)(2,1)S(1)}, bf16[576]{0:T(1024)(128)(2,1)}, u32[]{:S(2)}) copy-start(bf16[576]{0:T(1024)(128)(2,1)} %param.25) | copy-start | bytes 3460
  7.2 90.6 %copy-start.32 = (s32[1,2,8]{2,1,0:T(2,128)S(1)}, s32[1,2,8]{2,1,0:T(2,128)}, u32[]{:S(2)}) copy-start(s32[1,2,8]{2,1,0:T(2,128)} %param.18) | copy-start | bytes 196
  7.2 240.7 %all-gather.3.cloned.1.call-start = ((), (), s32[]{:S(2)}) async-start(), calls=%async_computation.3 | async-start | bytes 10948608 | tf_op jit(solution)/shard_map/all_gather | solution.py:1528
  96.0 198.4 %all-gather.5.cloned.1.call-start = ((), (), s32[]{:S(2)}) async-start(), calls=%async_computation.4 | async-start | bytes 12165120 | tf_op jit(solution)/shard_map/all_gather | solution.py:1453
  96.2 23.4 %collective-permute-start = (bf16[4608]{0:T(1024)(128)(2,1)S(1)}, bf16[4608]{0:T(1024)(128)(2,1)S(1)}, u32[]{:S(2)}, u32[]{:S(2)}) collective-permute-start(bf16[4608]{0:T(1024)(128)(2,1)S(1)} %concatenate.105), channel_id=1, source_target_pairs={{0,1},{1,0},{2,3},{3,2},{4,5},{5,4},{6,7},{7,6},{8,9},{9,8},{10,11... | collective-permute-start | bytes 27656 | tf_op jit(solution)/shard_map/ppermute | solution.py:1449
  98.8 6.6 copy-start.5
  149.2 360.3 %reduce-scatter.3.cloned.1.call-start = ((), (), s32[]{:S(2)}) async-start(), calls=%async_computation.5 | async-start | bytes 11280384 | tf_op jit(solution)/shard_map/reduce_scatter | solution.py:1577
  153.6 90.2 %collective-permute-start.1 = (bf16[1024,1152]{1,0:T(8,128)(2,1)}, bf16[1024,1152]{1,0:T(8,128)(2,1)}, u32[]{:S(2)}, u32[]{:S(2)}) collective-permute-start(bf16[1024,1152]{1,0:T(8,128)(2,1)} %get-tuple-element.147), channel_id=1, source_target_pairs={{0,1},{1,0},{2,3},{3,2},{4,5},{5,4},{6,7},{7,6},{8,9},{9,8},{10,11... | collective-permute-start | bytes 7077896 | tf_op jit(solution)/shard_map/ppermute | solution.py:1449
  372.9 252.7 %reduce-scatter.5.cloned.1.call-start = ((), (), s32[]{:S(2)}) async-start(), calls=%async_computation.6 | async-start | bytes 11280384 | tf_op jit(solution)/shard_map/reduce_scatter | solution.py:1581
  438.7 55.8 %copy-start.22 = (f32[8,1,1152]{2,1,0:T(1,128)S(1)}, f32[8,1,1152]{2,1,0:T(1,128)}, u32[]{:S(2)}) copy-start(f32[8,1,1152]{2,1,0:T(1,128)} %get-tuple-element.120) | copy-start | bytes 110596
  438.7 56.4 %copy-start.9 = (f32[8,1,4608]{2,1,0:T(1,128)S(1)}, f32[8,1,4608]{2,1,0:T(1,128)}, u32[]{:S(2)}) copy-start(f32[8,1,4608]{2,1,0:T(1,128)} %get-tuple-element.121) | copy-start | bytes 442372
  497.4 128.3 %collective-permute-start.2 = (bf16[1024,1152]{1,0:T(8,128)(2,1)}, bf16[1024,1152]{1,0:T(8,128)(2,1)}, u32[]{:S(2)}, u32[]{:S(2)}) collective-permute-start(bf16[1024,1152]{1,0:T(8,128)(2,1)} %get-tuple-element.102), channel_id=1, source_target_pairs={{0,1},{1,0},{2,3},{3,2},{4,5},{5,4},{6,7},{7,6},{8,9},{9,8},{10,11... | collective-permute-start | bytes 7077896 | tf_op jit(solution)/shard_map/ppermute | solution.py:1449
  657.6 25.0 %copy-start.13 = (f32[16,1,1152]{2,1,0:T(1,128)S(1)}, f32[16,1,1152]{2,1,0:T(1,128)}, u32[]{:S(2)}) copy-start(f32[16,1,1152]{2,1,0:T(1,128)} %get-tuple-element.117) | copy-start | bytes 221188
  657.7 25.0 %copy-start.12 = (f32[16,1,1152]{2,1,0:T(1,128)S(1)}, f32[16,1,1152]{2,1,0:T(1,128)}, u32[]{:S(2)}) copy-start(f32[16,1,1152]{2,1,0:T(1,128)} %get-tuple-element.118) | copy-start | bytes 221188
  682.8 4.8 copy-start.16
  682.8 4.8 copy-start.15
  682.8 4.8 copy-start.14
  682.8 4.8 copy-start.21
  682.8 5.2 copy-start.6
  700.5 74.3 %copy-start.7 = (bf16[288,1152]{1,0:T(8,128)(2,1)S(1)}, bf16[288,1152]{1,0:T(8,128)(2,1)}, u32[]{:S(2)}) copy-start(bf16[288,1152]{1,0:T(8,128)(2,1)} %reduce-scatter.3.cloned.1.call-done) | copy-start | bytes 1990660
  700.5 76.3 %copy-start.8 = (bf16[72,4608]{1,0:T(8,128)(2,1)S(1)}, bf16[72,4608]{1,0:T(8,128)(2,1)}, u32[]{:S(2)}) copy-start(bf16[72,4608]{1,0:T(8,128)(2,1)} %reduce-scatter.5.cloned.1.call-done) | copy-start | bytes 1990660
  700.5 78.0 %copy-start.3 = (bf16[72,3456]{1,0:T(8,128)(2,1)S(1)}, bf16[72,3456]{1,0:T(8,128)(2,1)}, u32[]{:S(2)}) copy-start(bf16[72,3456]{1,0:T(8,128)(2,1)} %adaptive_ref.1) | copy-start | bytes 1492996
  775.7 32.7 %collective-permute-start.5 = (bf16[288,576]{1,0:T(8,128)(2,1)}, bf16[288,576]{1,0:T(8,128)(2,1)}, u32[]{:S(2)}, u32[]{:S(2)}) collective-permute-start(bf16[288,576]{1,0:T(8,128)(2,1)} %constant_dynamic-slice_fusion), channel_id=1, source_target_pairs={{0,1},{1,0},{2,3},{3,2},{4,5},{5,4},{6,7},{7,6},{8,9},{9,8},{10,11... | collective-permute-start | bytes 995336 | tf_op jit(solution)/shard_map/ppermute | solution.py:1449
  777.6 32.9 %collective-permute-start.4 = (bf16[72,2304]{1,0:T(8,128)(2,1)}, bf16[72,2304]{1,0:T(8,128)(2,1)}, u32[]{:S(2)}, u32[]{:S(2)}) collective-permute-start(bf16[72,2304]{1,0:T(8,128)(2,1)} %constant_dynamic-slice_fusion.1), channel_id=1, source_target_pairs={{0,1},{1,0},{2,3},{3,2},{4,5},{5,4},{6,7},{7,6},{8,9},{9,8},{10,11... | collective-permute-start | bytes 995336 | tf_op jit(solution)/shard_map/ppermute | solution.py:1449
  781.1 20.6 %all-to-all-start = ((f32[16,16,72]{2,1,0:T(8,128)}), f32[16,16,72]{2,1,0:T(8,128)S(1)}, u32[]{:S(2)}, u32[]{:S(2)}) async-start(f32[16,16,72]{2,1,0:T(8,128)} %fusion.9), calls=%async_computation.2 | async-start | bytes 262144 | tf_op jit(solution)/shard_map/all_to_all | solution.py:1642
  788.4 5.0 copy-start.1
  796.5 11.2 %copy-start.10 = (bf16[1,2,8,1152]{3,2,1,0:T(8,128)(2,1)S(1)}, bf16[1,2,8,1152]{3,2,1,0:T(8,128)(2,1)}, u32[]{:S(2)}) copy-start(bf16[1,2,8,1152]{3,2,1,0:T(8,128)(2,1)} %param.17) | copy-start | bytes 110596
  801.7 5.8 collective-permute-start.3
  (12 other events, 30.3 us)
Sparse Core Ops, SparseCore 0:
  96.1 96.2 all-gather.2
  195.3 94.0 all-gather.4
  373.1 117.6 reduce-scatter.2
  494.6 119.9 reduce-scatter.4

commit v2 on v1

--- a/solution.py
+++ b/solution.py
@@ -439,8 +439,10 @@
 
 
 HEAD = 72
+EXPONENT = HEAD**-0.5 * 1.4426950408889634
+
+
 WINDOW = 256
-EXPONENT = HEAD**-0.5 * 1.4426950408889634
 
 
 def head_window(head, width):
@@ -448,8 +450,19 @@
     return pl.ds(pl.multiple_of(start, 128), WINDOW), head * HEAD - start
 
 
-def head_lanes(offset, rows):
-    lane = lax.broadcasted_iota(jnp.int32, (rows, WINDOW), 1)
+def head_windows(group):
+    heads = []
+    for pair in range(group // 2):
+        pair = pl.program_id(1) * (group // 2) + pair
+        late = jnp.where(pair >= HEADS // 4, 1, 0)
+        for head, size in ((2 * pair + late, 128), (2 * pair + 1 - late, 256)):
+            start = lax.div(head * HEAD, 128) * 128
+            heads.append((head, pl.ds(pl.multiple_of(start, 128), size), head * HEAD - start, size))
+    return heads
+
+
+def head_lanes(offset, rows, size):
+    lane = lax.broadcasted_iota(jnp.int32, (rows, size), 1)
     return (lane >= offset) & (lane < offset + HEAD)
 
 
@@ -489,7 +502,7 @@
             head = pl.program_id(1) * group + member
             window, offset = head_window(head, width)
             keys = both_strips(k_ref, start, strip, half, window)
-            keys = jnp.where(head_lanes(offset, 2 * strip), keys, jnp.zeros_like(keys))
+            keys = jnp.where(head_lanes(offset, 2 * strip, WINDOW), keys, jnp.zeros_like(keys))
             values = both_strips(v_ref, start, strip, half, window).T
             for index in range(2 * strip // block):
                 rows = image_rows(start, strip, half, index, block)
@@ -508,59 +521,69 @@
             expo = jnp.exp2((scores - top) * EXPONENT)
             mass = jnp.sum(expo, axis=0, keepdims=True)
             out = (matmul(values, expo.astype(HALF)) * (1.0 / mass)).T.astype(HALF)
-            o_ref[rows, window] = jnp.where(head_lanes(offset, block), out, o_ref[rows, window])
+            o_ref[rows, window] = jnp.where(head_lanes(offset, block, WINDOW), out, o_ref[rows, window])
             total_ref[head, :, rows] = top * EXPONENT + jnp.log2(mass)
 
     for_images(info, pl.program_id(0), image)
 
 
 def attend_backward_kernel(
-    info, q_ref, k_ref, v_ref, do_ref, total_ref, dq_ref, dk_ref, dv_ref, *, group
+    info, q_ref, k_ref, v_ref, do_ref, total_ref, delta_ref, dq_ref, dk_ref, dv_ref, *, group
 ):
-    half, width = q_ref.shape[0] // 2, q_ref.shape[1]
+    half = q_ref.shape[0] // 2
     scale = HEAD**-0.5
 
     def image(start, strip, block):
         start = pl.multiple_of(start, 128)
+        count = 2 * strip // block
         work = []
-        sums = {}
-        for member in range(group):
-            head = pl.program_id(1) * group + member
-            window, offset = head_window(head, width)
+        for head, window, offset, size in head_windows(group):
             keys = both_strips(k_ref, start, strip, half, window)
             values = both_strips(v_ref, start, strip, half, window)
-            inside = head_lanes(offset, 2 * strip)
+            inside = head_lanes(offset, 2 * strip, size)
             head_keys = jnp.where(inside, keys, jnp.zeros_like(keys))
             head_values = jnp.where(inside, values, jnp.zeros_like(values))
             turned = keys.T
-            for index in range(2 * strip // block):
+            lanes = head_lanes(offset, block, size)
+            for index in range(count):
                 rows = image_rows(start, strip, half, index, block)
-                work.append((head, window, offset, head_keys, head_values, turned, rows))
+                work.append((head, window, lanes, head_keys, head_values, turned, rows))
 
         def begin(item):
-            head, window, offset, keys, values, turned, rows = item
+            head, window, lanes, keys, values, turned, rows = item
             return (
                 right_outer(keys, q_ref[rows, window]),
                 right_outer(values, do_ref[rows, window]),
             )
 
         def middle(item, scores, d_weights):
-            weights = jnp.exp2(scores * EXPONENT - total_ref[item[0], :, item[6]])
-            product = weights * d_weights
-            delta = jnp.sum(product, axis=0, keepdims=True)
-            return weights.astype(HALF), (product - weights * delta).astype(HALF)
+            head, rows = item[0], item[6]
+            weights = jnp.exp2(scores * EXPONENT - total_ref[head, :, rows])
+            d_scores = weights * (d_weights - delta_ref[head, :, rows])
+            return weights.astype(HALF), d_scores.astype(HALF)
+
+        kept = []
 
         def finish(item, weights, d_scores):
-            head, window, offset, keys, values, turned, rows = item
-            d_keys = matmul(d_scores, q_ref[rows, window])
-            d_values = matmul(weights, do_ref[rows, window])
+            head, window, lanes, keys, values, turned, rows = item
             d_query = (matmul(turned, d_scores).T * scale).astype(HALF)
-            dq_ref[rows, window] = jnp.where(
-                head_lanes(offset, block), d_query, dq_ref[rows, window]
-            )
-            if id(keys) in sums:
-                d_keys, d_values = sums[id(keys)][0] + d_keys, sums[id(keys)][1] + d_values
-            sums[id(keys)] = (d_keys, d_values)
+            dq_ref[rows, window] = jnp.where(lanes, d_query, dq_ref[rows, window])
+            kept.append((weights, d_scores))
+            if len(kept) < count:
+                return
+            weights = jnp.concatenate([part for part, _ in kept], axis=1)
+            d_scores = jnp.concatenate([part for _, part in kept], axis=1)
+            kept.clear()
+            d_keys = matmul(d_scores, both_strips(q_ref, start, strip, half, window))
+            d_values = matmul(weights, both_strips(do_ref, start, strip, half, window))
+            for ref, value in (
+                (dk_ref, (d_keys * scale).astype(HALF)),
+                (dv_ref, d_values.astype(HALF)),
+            ):
+                for index in range(count):
+                    rows = image_rows(start, strip, half, index, block)
+                    part = value[index * block : (index + 1) * block]
+                    ref[rows, window] = jnp.where(lanes, part, ref[rows, window])
 
         coming = begin(work[0])
         late = None
@@ -572,17 +595,6 @@
                 finish(*late)
             late = (item,) + middle(item, *now)
         finish(*late)
-        for item in work[:: 2 * strip // block]:
-            head, window, offset, keys = item[:4]
-            d_keys, d_values = sums[id(keys)]
-            lanes = head_lanes(offset, strip)
-            for ref, value in (
-                (dk_ref, (d_keys * scale).astype(HALF)),
-                (dv_ref, d_values.astype(HALF)),
-            ):
-                for first, part in ((start, value[:strip]), (half + start, value[strip:])):
-                    rows = pl.ds(pl.multiple_of(first, 128), strip)
-                    ref[rows, window] = jnp.where(lanes, part, ref[rows, window])
 
     for_images(info, pl.program_id(0), image)
 
@@ -623,11 +635,11 @@
     )
 
 
-def attend_pack_backward(info, query, keys, values, grad, total):
+def attend_pack_backward(info, query, keys, values, grad, total, delta):
     outputs = [jax.ShapeDtypeStruct(query.shape, HALF)] * 3
-    arrays = [query, keys, values, grad, total]
+    arrays = [query, keys, values, grad, total, delta]
     return attention_call(
-        attend_backward_kernel, "attend_backward", info, arrays, outputs, 2, 140 * 10**9
+        attend_backward_kernel, "attend_backward", info, arrays, outputs, 4, 140 * 10**9
     )
 
 
@@ -645,23 +657,30 @@
 def by_rows(array):
     size = BLOCK if len(array.shape) == 2 else BLOCK // PART
     zeros = (0,) * (len(array.shape) - 1)
-    return pl.BlockSpec((size,) + array.shape[1:], lambda step: (step,) + zeros)
-
-
-def dense_call(kernel, name, inputs, outputs, scratch=(), flops=0):
-    rows = 2048
+    return pl.BlockSpec((size,) + array.shape[1:], lambda step, *scalars: (step,) + zeros)
+
+
+def dense_call(kernel, name, rows, inputs, outputs, scratch=(), flops=0, strip=None):
     size = sum(array.size * array.dtype.itemsize for array, _ in inputs + outputs)
+    scalars = [] if strip is None else [strip.reshape(1).astype(jnp.int32)]
+
+    def run(*refs):
+        kernel(*refs[len(scalars) :])
+
     return pl.pallas_call(
-        kernel,
-        grid=(rows // BLOCK,),
-        in_specs=[spec for _, spec in inputs],
-        out_specs=[spec for _, spec in outputs],
+        run,
+        grid_spec=pltpu.PrefetchScalarGridSpec(
+            num_scalar_prefetch=len(scalars),
+            grid=(rows // BLOCK,),
+            in_specs=[spec for _, spec in inputs],
+            out_specs=[spec for _, spec in outputs],
+            scratch_shapes=list(scratch),
+        ),
         out_shape=[shape for shape, _ in outputs],
-        scratch_shapes=list(scratch),
         compiler_params=pltpu.CompilerParams(vmem_limit_bytes=60 * 2**20),
         cost_estimate=pl.CostEstimate(flops=flops, bytes_accessed=size, transcendentals=0),
         name=name,
-    )(*[array for array, _ in inputs])
+    )(*scalars, *[array for array, _ in inputs])
 
 
 def shape_of(*dims, kind=None):
@@ -733,10 +752,11 @@
             gate = 0.5 + 0.5 * jnp.tanh(
                 value * (GELU_SCALE + (GELU_SCALE * 0.044715) * square)
             )
-            active = value * gate
+            active = (value * gate).astype(HALF)
+            gate, square = gate.astype(HALF), square.astype(HALF)
             bend = 2.0 * GELU_SCALE + (6.0 * GELU_SCALE * 0.044715) * square
-            act_ref[rows, place] = active.astype(HALF)
-            slope_ref[rows, place] = (gate + active * (1.0 - gate) * bend).astype(HALF)
+            act_ref[rows, place] = active
+            slope_ref[rows, place] = gate + active * (1.0 - gate) * bend
 
 
 def up_call(hidden, weight, bias, chunk=768):
@@ -746,16 +766,15 @@
     return dense_call(
         functools.partial(up_kernel, chunk=chunk),
         "up",
+        rows,
         [(hidden, by_rows(hidden)), (weight, resident(weight)), (bias, resident(bias))],
         [(out, by_rows(out)), (out, by_rows(out))],
         flops=2 * rows * width * wide,
     )
 
 
-def down_grad_kernel(cot_ref, gate_ref, slope_ref, w_ref, d_branch_ref, d_pre_ref, sum_ref, wide_ref, *, chunk):
-    for rows, part, _ in strips():
-        d_branch_ref[rows, :] = (cot_ref[rows, :].astype(FLOAT) * gate_ref[part]).astype(HALF)
-    x = d_branch_ref[...]
+def down_grad_kernel(x_ref, slope_ref, w_ref, d_pre_ref, sum_ref, wide_ref, *, chunk):
+    x = x_ref[...]
     sum_ref[0] = jnp.sum(fold(x.astype(FLOAT)), axis=0, keepdims=True)
     wide = w_ref.shape[0]
     work = list(range(0, wide, chunk))
@@ -781,27 +800,26 @@
             wide_ref[0, :, place] = jnp.sum(total, axis=0, keepdims=True)
 
 
-def down_grad_call(cotangent, gate, slope, weight, chunk=768):
-    rows, width = cotangent.shape
+def down_grad_call(d_branch, slope, weight, chunk=768):
+    rows, width = d_branch.shape
     wide = weight.shape[0]
     steps = rows // BLOCK
-    d_branch, d_pre = shape_of(rows, width, kind=HALF), shape_of(rows, wide, kind=HALF)
+    d_pre = shape_of(rows, wide, kind=HALF)
     total, wide_total = shape_of(steps, 1, width), shape_of(steps, 1, wide)
 
     def per_step(shape):
-        return pl.BlockSpec((1,) + shape.shape[1:], lambda step: (step, 0, 0))
+        return pl.BlockSpec((1,) + shape.shape[1:], lambda step, *scalars: (step, 0, 0))
 
     return dense_call(
         functools.partial(down_grad_kernel, chunk=chunk),
         "down_grad",
+        rows,
         [
-            (cotangent, by_rows(cotangent)),
-            (gate, by_rows(gate)),
+            (d_branch, by_rows(d_branch)),
             (slope, by_rows(slope)),
             (weight, resident(weight)),
         ],
         [
-            (d_branch, by_rows(d_branch)),
             (d_pre, by_rows(d_pre)),
             (total, per_step(total)),
             (wide_total, per_step(wide_total)),
@@ -827,6 +845,7 @@
     return dense_call(
         project_kernel,
         "project",
+        rows,
         [
             (tokens, by_rows(tokens)),
             (shift, by_rows(shift)),
@@ -855,6 +874,7 @@
     return dense_call(
         mix_kernel,
         "mix",
+        rows,
         [
             (attended, by_rows(attended)),
             (tokens, by_rows(tokens)),
@@ -899,19 +919,80 @@
 
 def strip_specs(rows, width):
     half = rows // BLOCK // 2
-    own, other = shape_of(rows // 2, width), shape_of(rows // 2, width, kind=HALF)
+    both, other = shape_of(2, rows // 2, width), shape_of(rows // 2, width, kind=HALF)
+
+    def own_place(step, strip):
+        return strip[0], jnp.minimum(step, half - 1), 0
+
+    def other_place(step, strip):
+        return jnp.maximum(step - half, 0), 0
+
     return [
-        (own, pl.BlockSpec((BLOCK, width), lambda step: (jnp.minimum(step, half - 1), 0))),
-        (other, pl.BlockSpec((BLOCK, width), lambda step: (jnp.maximum(step - half, 0), 0))),
+        (both, pl.BlockSpec((None, BLOCK, width), own_place)),
+        (other, pl.BlockSpec((BLOCK, width), other_place)),
     ]
 
 
-def finish_call(active, tokens, branch, cotangent, gate_one, gate_two, weight, bias):
+def join_kernel(own_ref, other_ref, gate_ref, both_ref, d_branch_ref):
+    first = pl.program_id(0) < pl.num_programs(0) // 2
+    both_ref[...] = jnp.where(first, own_ref[...].astype(FLOAT), other_ref[...].astype(FLOAT)).astype(HALF)
+    for rows, part, _ in strips():
+        d_branch_ref[rows, :] = (both_ref[rows, :].astype(FLOAT) * gate_ref[part]).astype(HALF)
+
+
+def join_call(pair, other, gate, strip):
+    half, width = other.shape
+    steps = half // BLOCK
+    out = shape_of(2 * half, width, kind=HALF)
+    own_spec = pl.BlockSpec(
+        (None, BLOCK, width), lambda step, strip: (strip[0], jnp.minimum(step, steps - 1), 0)
+    )
+    other_spec = pl.BlockSpec(
+        (BLOCK, width), lambda step, strip: (jnp.maximum(step - steps, 0), 0)
+    )
+    return dense_call(
+        join_kernel,
+        "join",
+        2 * half,
+        [(pair, own_spec), (other, other_spec), (gate, by_rows(gate))],
+        [(out, by_rows(out)), (out, by_rows(out))],
+        strip=strip,
+    )
+
+
+def fill_kernel(strip, both_ref, other_ref, out_ref):
+    out_ref[...] = other_ref[...].astype(FLOAT)
+
+
+def fill_call(both, other, strip):
+    rows, width = other.shape
+    return pl.pallas_call(
+        fill_kernel,
+        grid_spec=pltpu.PrefetchScalarGridSpec(
+            num_scalar_prefetch=1,
+            grid=(rows // BLOCK,),
+            in_specs=[
+                pl.BlockSpec(memory_space=pl.ANY),
+                pl.BlockSpec((BLOCK, width), lambda step, strip: (step, 0)),
+            ],
+            out_specs=pl.BlockSpec(
+                (None, BLOCK, width), lambda step, strip: (1 - strip[0], step, 0)
+            ),
+        ),
+        out_shape=jax.ShapeDtypeStruct(both.shape, both.dtype),
+        input_output_aliases={1: 0},
+        cost_estimate=pl.CostEstimate(flops=0, bytes_accessed=8 * 2**20, transcendentals=0),
+        name="fill",
+    )(strip.reshape(1).astype(jnp.int32), both, other)
+
+
+def finish_call(active, tokens, branch, cotangent, gate_one, gate_two, weight, bias, strip):
     rows, width = tokens.shape
     sums = shape_of(rows // PART, 1, width)
     return dense_call(
         finish_kernel,
         "finish",
+        rows,
         [
             (active, by_rows(active)),
             (tokens, by_rows(tokens)),
@@ -925,6 +1006,7 @@
         strip_specs(rows, width) + [(sums, by_rows(sums))],
         scratch=[pltpu.VMEM((BLOCK, width), FLOAT)],
         flops=2 * rows * active.shape[1] * width,
+        strip=strip,
     )
 
 
@@ -935,8 +1017,8 @@
 
 
 def mix_grad_kernel(
-    d_pre_ref, x_ref, branch_ref, cot_ref, gate_ref, scale_ref, up_ref, out_ref,
-    d_middle_ref, d_branch_ref, d_attended_ref, shift_sum, scale_sum, gate_sum, bias_sum, hidden,
+    d_pre_ref, attended_ref, x_ref, branch_ref, cot_ref, gate_ref, scale_ref, up_ref, out_ref,
+    d_middle_ref, d_branch_ref, d_attended_ref, delta_ref, shift_sum, scale_sum, gate_sum, bias_sum, hidden,
 ):
     columns = up_ref.shape[2]
     hidden[...] = right_outer(d_pre_ref[:, :columns], up_ref[0]) + right_outer(
@@ -958,18 +1040,31 @@
         d_branch_ref[rows, :] = d_branch
         sums.add(bias_sum, part, first, d_branch.astype(FLOAT))
     sums.store()
-    d_attended_ref[...] = right_outer(d_branch_ref[...], out_ref[...]).astype(HALF)
-
-
-def mix_grad_call(d_pre, tokens, branch, cotangent, gate, scale, up, out):
+    d_attended = right_outer(d_branch_ref[...], out_ref[...]).astype(HALF)
+    d_attended_ref[...] = d_attended
+    product = d_attended.astype(FLOAT) * attended_ref[...].astype(FLOAT)
+    heads, width = HEADS, product.shape[1]
+    lane = lax.broadcasted_iota(jnp.int32, (heads, width), 1)
+    head = lax.broadcasted_iota(jnp.int32, (heads, width), 0) * HEAD
+    member = jnp.where((lane >= head) & (lane < head + HEAD), 1.0, 0.0).astype(HALF)
+    high = product.astype(HALF)
+    low = (product - high.astype(FLOAT)).astype(HALF)
+    delta = right_outer(member, high) + right_outer(member, low)
+    for index in range(heads):
+        delta_ref[index] = delta[index : index + 1]
+
+
+def mix_grad_call(d_pre, attended, tokens, branch, cotangent, gate, scale, up, out):
     rows, width = tokens.shape
     half, sums = shape_of(rows, width, kind=HALF), shape_of(rows // PART, 1, width)
-    d_middle = shape_of(rows, width)
+    d_middle, delta = shape_of(rows, width), shape_of(HEADS, 1, rows)
     return dense_call(
         mix_grad_kernel,
         "mix_grad",
+        rows,
         [
             (d_pre, by_rows(d_pre)),
+            (attended, by_rows(attended)),
             (tokens, by_rows(tokens)),
             (branch, by_rows(branch)),
             (cotangent, by_rows(cotangent)),
@@ -979,6 +1074,7 @@
             (out, resident(out)),
         ],
         [(d_middle, by_rows(d_middle)), (half, by_rows(half)), (half, by_rows(half))]
+        + [(delta, pl.BlockSpec((HEADS, 1, BLOCK), lambda step, *scalars: (0, 0, step)))]
         + [(sums, by_rows(sums))] * 4,
         scratch=[pltpu.VMEM((BLOCK, width), FLOAT)],
         flops=2 * rows * width * (d_pre.shape[1] + width),
@@ -1006,12 +1102,13 @@
     store_strip(pl.program_id(0), hidden, own_ref, other_ref)
 
 
-def project_grad_call(d_query, d_keys, d_values, tokens, d_middle, scale, weight):
+def project_grad_call(d_query, d_keys, d_values, tokens, d_middle, scale, weight, strip):
     rows, width = tokens.shape
     sums = shape_of(rows // PART, 1, width)
     return dense_call(
         project_grad_kernel,
         "project_grad",
+        rows,
         [
             (d_query, by_rows(d_query)),
             (d_keys, by_rows(d_keys)),
@@ -1024,6 +1121,7 @@
         strip_specs(rows, width) + [(sums, by_rows(sums))] * 4,
         scratch=[pltpu.VMEM((BLOCK, width), FLOAT)],
         flops=6 * rows * width * width,
+        strip=strip,
     )
 
 
@@ -1090,15 +1188,21 @@
 
 
 def head_kernel(
-    shard_ref,
+    joint_ref,
+    output_ref,
     condition_ref,
     adaptive_ref,
     bias_ref,
     tokens_ref,
-    whole_ref,
+    whole_joint_ref,
+    whole_output_ref,
     modulation_ref,
     act_ref,
     other_ref,
+    joint_from_y,
+    output_from_y,
+    joint_slot,
+    output_slot,
     conditions,
     parts,
     from_core,
@@ -1106,28 +1210,31 @@
     from_z,
     share,
     from_y,
-    local_sem,
+    local_sems,
     send_sems,
     recv_sems,
 ):
     place = Place()
     copies = Copies(place, send_sems, recv_sems)
     place.greet()
-
-    own = pltpu.make_async_copy(
-        shard_ref, whole_ref.at[place.half(0), place.me], local_sem.at[0]
-    )
-    own.start()
     conditions[place.me] = condition_ref[...]
 
     def condition(kind, z_step, x_step):
         slot = conditions.at[place.at(z_step, x_step, 0)]
         copies.send((kind, "condition", z_step, x_step), slot, slot)
 
-    def weight(kind, y_step, z_step, x_step):
-        slot = whole_ref.at[place.half(y_step), place.at(z_step, x_step, 0)]
-        mine = y_step == 0 and z_step == 0 and x_step == 0
-        copies.send((kind, "weight", y_step, z_step, x_step), shard_ref if mine else slot, slot)
+    def weight(kind, z_step, x_step):
+        for name, slot, whole in (
+            ("joint", joint_slot, whole_joint_ref),
+            ("output", output_slot, whole_output_ref),
+        ):
+            target = whole.at[place.at(z_step, x_step, 0)]
+            mine = z_step == 0 and x_step == 0
+            copies.send((kind, name, z_step, x_step), slot if mine else target, target)
+
+    def arrived(kind, z_step, x_step):
+        copies.receive((kind, "joint", z_step, x_step))
+        copies.receive((kind, "output", z_step, x_step))
 
     def forward_condition(z_step):
         for x_step in range(2):
@@ -1136,33 +1243,44 @@
                 condition("z", z_step, x_step)
             condition("core", z_step, x_step)
 
-    def forward(z_step, y_step):
-        copies.receive(("z", "weight", y_step, z_step - 1, 0))
+    def forward(z_step):
+        arrived("z", z_step - 1, 0)
         if z_step < 3:
-            weight("z", y_step, z_step, 0)
-        weight("x", y_step, z_step, 0)
-        weight("core", y_step, z_step, 0)
-
+            weight("z", z_step, 0)
+        weight("x", z_step, 0)
+        weight("core", z_step, 0)
+
+    copies.send(("y", "joint"), joint_ref, joint_from_y)
+    copies.send(("y", "output"), output_ref, output_from_y)
     condition("x", 0, 0)
     condition("z", 0, 0)
     condition("core", 0, 0)
-    weight("y", 0, 0, 0)
-    weight("z", 0, 0, 0)
-    weight("x", 0, 0, 0)
-    weight("core", 0, 0, 0)
     copies.send(("y", "tokens"), tokens_ref.at[place.half(1)], other_ref)
     copies.receive(("x", "condition", 0, 0))
     condition("z", 0, 1)
     condition("core", 0, 1)
     forward_condition(1)
-    copies.receive(("y", "weight", 0, 0, 0))
-    weight("z", 1, 0, 0)
-    weight("x", 1, 0, 0)
-    weight("core", 1, 0, 0)
+
+    owns = []
+    for name, mine, other, slot, whole in (
+        ("joint", joint_ref, joint_from_y, joint_slot, whole_joint_ref),
+        ("output", output_ref, output_from_y, output_slot, whole_output_ref),
+    ):
+        copies.receive(("y", name))
+        first, second = mine[...].astype(FLOAT), other[...].astype(FLOAT)
+        low = place.y == 0
+        slot[...] = jnp.concatenate(
+            [jnp.where(low, first, second), jnp.where(low, second, first)], axis=1
+        ).astype(HALF)
+        own = pltpu.make_async_copy(slot, whole.at[place.me], local_sems.at[len(owns)])
+        own.start()
+        owns.append(own)
+    weight("z", 0, 0)
+    weight("x", 0, 0)
+    weight("core", 0, 0)
     forward_condition(2)
-    forward(1, 0)
     forward_condition(3)
-    forward(1, 1)
+    forward(1)
     for z_step in range(4):
         for x_step in range(2):
             copies.receive(("core", "condition", z_step, x_step))
@@ -1173,22 +1291,24 @@
         values = conditions[index, place.me].astype(FLOAT)
         act_ref[index] = (values / (1.0 + jnp.exp(-values))).astype(HALF)
 
-    def products(z_step, core_step):
-        for x_step in range(2):
-            target = place.at((4 - z_step) % 4, x_step, core_step)
-            product = matmul(act_ref[target], adaptive)
-            parts[core_step, z_step, x_step] = product.astype(HALF)
+    def products(core_step):
+        targets = [
+            place.at((4 - z_step) % 4, x_step, core_step)
+            for z_step in range(4)
+            for x_step in range(2)
+        ]
+        acts = jnp.concatenate([act_ref[target] for target in targets], axis=0)
+        product = matmul(acts, adaptive).astype(HALF)
+        parts[core_step] = product.reshape(parts.shape[1:])
 
     def add(first, second):
         return first.astype(FLOAT) + second.astype(FLOAT)
 
+    products(1)
     for z_step in (3, 2, 1, 0):
-        products(z_step, 1)
         copies.send(("core", "part", z_step), parts.at[1, z_step], from_core.at[z_step])
-    forward(2, 0)
-    for z_step in (3, 2, 1, 0):
-        products(z_step, 0)
-    forward(2, 1)
+    products(0)
+    forward(2)
     for z_step in (3, 2, 1, 0):
         copies.receive(("core", "part", z_step))
         total = add(parts[0, z_step], from_core[z_step])
@@ -1198,16 +1318,13 @@
         parts[0, z_step] = total.astype(HALF)
         if z_step > 0:
             copies.send(("z", "part", z_step), parts.at[0, z_step], from_z.at[z_step - 1])
-        if z_step == 2:
-            forward(3, 0)
         if z_step == 1:
-            forward(3, 1)
+            forward(3)
     copies.send(("x", "part"), parts.at[0, 0, 1], from_x)
 
     def last(z_step):
-        for y_step in range(2):
-            copies.receive(("x", "weight", y_step, z_step, 0))
-            weight("core", y_step, z_step, 1)
+        arrived("x", z_step, 0)
+        weight("core", z_step, 1)
 
     last(0)
     last(1)
@@ -1224,33 +1341,37 @@
     modulation_ref[place.half(1)] = from_y[...]
     for z_step in range(4):
         for x_step in range(2):
-            for y_step in range(2):
-                copies.receive(("core", "weight", y_step, z_step, x_step))
+            arrived("core", z_step, x_step)
     copies.receive(("y", "tokens"))
-    own.wait()
+    for own in owns:
+        own.wait()
     copies.finish()
 
 
-def head(shard, condition, adaptive_weight, adaptive_bias, tokens):
+def head(joint_weight, output_weight, condition, adaptive_weight, adaptive_bias, tokens):
     micro, images, width = condition.shape
-    features = adaptive_weight.shape[0]
+    features, columns = adaptive_weight.shape
     rows = micro * images
     condition = condition.reshape(rows, width // features, features).transpose(1, 0, 2)
-    columns = adaptive_weight.shape[1]
     count = 16
     vmem = pl.BlockSpec(memory_space=pltpu.VMEM)
     anywhere = pl.BlockSpec(memory_space=pl.ANY)
-    return pl.pallas_call(
+    slots = [(shard.shape[0], 2 * shard.shape[1]) for shard in (joint_weight, output_weight)]
+    joint, output, modulation, act, other = pl.pallas_call(
         head_kernel,
-        out_shape=[
-            jax.ShapeDtypeStruct((2, count) + shard.shape, HALF),
+        out_shape=[jax.ShapeDtypeStruct((count,) + slot, HALF) for slot in slots]
+        + [
             jax.ShapeDtypeStruct((2, images, columns), FLOAT),
             jax.ShapeDtypeStruct((count, rows, features), HALF),
             jax.ShapeDtypeStruct(tokens.shape[1:], HALF),
         ],
-        in_specs=[anywhere, vmem, vmem, vmem, anywhere],
-        out_specs=[anywhere, vmem, vmem, anywhere],
+        in_specs=[vmem] * 5 + [anywhere],
+        out_specs=[anywhere, anywhere, vmem, vmem, anywhere],
         scratch_shapes=[
+            pltpu.VMEM(joint_weight.shape, HALF),
+            pltpu.VMEM(output_weight.shape, HALF),
+            pltpu.VMEM(slots[0], HALF),
+            pltpu.VMEM(slots[1], HALF),
             pltpu.VMEM((count,) + condition.shape, HALF),
             pltpu.VMEM((2, 4, 2, rows, columns), HALF),
             pltpu.VMEM((4, 2, rows, columns), HALF),
@@ -1258,7 +1379,7 @@
             pltpu.VMEM((3, 2, rows, columns), HALF),
             pltpu.VMEM((2, images, columns), FLOAT),
             pltpu.VMEM((images, columns), FLOAT),
-            pltpu.SemaphoreType.DMA((1,)),
+            pltpu.SemaphoreType.DMA((2,)),
             pltpu.SemaphoreType.DMA((64,)),
             pltpu.SemaphoreType.DMA((64,)),
         ],
@@ -1267,7 +1388,21 @@
         ),
         cost_estimate=pl.CostEstimate(flops=0, bytes_accessed=200 * 2**20, transcendentals=0),
         name="head",
-    )(shard, condition, adaptive_weight, adaptive_bias.astype(FLOAT)[None], tokens)
+    )(
+        joint_weight,
+        output_weight,
+        condition,
+        adaptive_weight,
+        adaptive_bias.astype(FLOAT)[None],
+        tokens,
+    )
+    return (
+        joint.reshape(-1, joint.shape[2]),
+        output.reshape(-1, output.shape[2]),
+        modulation,
+        act,
+        other,
+    )
 
 
 def tail_kernel(
@@ -1283,6 +1418,7 @@
     from_core,
     from_x,
     from_z,
+    half_sum,
     from_y,
     pair,
     pair_from_y,
@@ -1297,8 +1433,8 @@
     copies = Copies(place, send_sems, recv_sems)
     place.greet()
 
-    def grad(y_step, z_step, x_step, core_step):
-        return grad_ref.at[place.half(y_step), place.at((4 - z_step) % 4, x_step, core_step)]
+    def grad(z_step, x_step, core_step):
+        return grad_ref.at[place.at((4 - z_step) % 4, x_step, core_step)]
 
     def modulation(kind, z_step, x_step):
         slot = all_ref.at[place.at(z_step, x_step, 0)]
@@ -1306,22 +1442,19 @@
 
     copies.send(("y", "half"), half_ref.at[place.half(1)], pair_from_y)
     copies.send(("core", "vector"), vector_ref, vector_from.at[0])
-    order = [(z_step, y_step) for z_step in (3, 2, 1, 0) for y_step in (1, 0)]
     loads = {}
     for x_step in (1, 0):
-        for z_step, y_step in order:
+        for z_step in (3, 2, 1, 0):
             copies.send(
-                ("core", x_step, z_step, y_step),
-                grad(y_step, z_step, x_step, 1),
-                from_core.at[x_step, z_step, y_step],
+                ("core", x_step, z_step),
+                grad(z_step, x_step, 1),
+                from_core.at[x_step, z_step],
             )
             load = pltpu.make_async_copy(
-                grad(y_step, z_step, x_step, 0),
-                own.at[x_step, z_step, y_step],
-                local_sems.at[len(loads)],
+                grad(z_step, x_step, 0), own.at[x_step, z_step], local_sems.at[len(loads)]
             )
             load.start()
-            loads[x_step, z_step, y_step] = load
+            loads[x_step, z_step] = load
 
     copies.receive(("core", "vector"))
     vector[0] = vector_ref[...] + vector_from[0]
@@ -1334,18 +1467,15 @@
     modulation("z", 0, 0)
     modulation("core", 0, 0)
 
-    def summed(x_step, z_step, y_step):
-        loads[x_step, z_step, y_step].wait()
-        copies.receive(("core", x_step, z_step, y_step))
-        first = own[x_step, z_step, y_step].astype(FLOAT)
-        return first + from_core[x_step, z_step, y_step].astype(FLOAT)
+    def summed(x_step, z_step):
+        loads[x_step, z_step].wait()
+        copies.receive(("core", x_step, z_step))
+        first = own[x_step, z_step].astype(FLOAT)
+        return first + from_core[x_step, z_step].astype(FLOAT)
 
     def send_x(z_step):
-        for y_step in (1, 0):
-            own[1, z_step, y_step] = summed(1, z_step, y_step).astype(HALF)
-            copies.send(
-                ("x", z_step, y_step), own.at[1, z_step, y_step], from_x.at[z_step, y_step]
-            )
+        own[1, z_step] = summed(1, z_step).astype(HALF)
+        copies.send(("x", z_step), own.at[1, z_step], from_x.at[z_step])
 
     def forward_modulation(z_step):
         for x_step in range(2):
@@ -1379,24 +1509,23 @@
     copies.receive(("z", "vector", 1))
     vector_ring(2)
     forward_modulation(3)
-    for z_step, y_step in order:
-        total = summed(0, z_step, y_step)
-        copies.receive(("x", z_step, y_step))
-        total = total + from_x[z_step, y_step].astype(FLOAT)
+    for z_step in (3, 2, 1, 0):
+        total = summed(0, z_step)
+        copies.receive(("x", z_step))
+        total = total + from_x[z_step].astype(FLOAT)
         if z_step < 3:
-            copies.receive(("z", z_step + 1, y_step))
-            total = total + from_z[z_step, y_step].astype(FLOAT)
-        if z_step == 0 and y_step == 0:
-            copies.receive(("y",))
-            share_ref[...] = total + from_y[...].astype(FLOAT)
-            continue
-        own[0, z_step, y_step] = total.astype(HALF)
+            copies.receive(("z", z_step + 1))
+            total = total + from_z[z_step].astype(FLOAT)
         if z_step > 0:
-            copies.send(
-                ("z", z_step, y_step), own.at[0, z_step, y_step], from_z.at[z_step - 1, y_step]
-            )
-        else:
-            copies.send(("y",), own.at[0, 0, 1], from_y)
+            own[0, z_step] = total.astype(HALF)
+            copies.send(("z", z_step), own.at[0, z_step], from_z.at[z_step - 1])
+    cut = share_ref.shape[1]
+    low, high = total[:, :cut], total[:, cut:]
+    half_sum[...] = jnp.where(place.y == 0, high, low).astype(HALF)
+    copies.send(("y",), half_sum, from_y)
+    share_ref[...] = jnp.where(place.y == 0, low, high)
+    copies.receive(("y",))
+    share_ref[...] = share_ref[...] + from_y[...].astype(FLOAT)
     copies.receive(("z", "vector", 2))
     total_ref[...] = (vector_z[0] + vector_z[1]) + (vector_z[2] + vector_z[3])
     for z_step in range(4):
@@ -1407,15 +1536,16 @@
 
 
 def tail(grad, half, vector, strip):
-    slot = grad.shape[2:]
-    count = grad.shape[1]
+    slot = grad.shape[1:]
+    count = grad.shape[0]
+    share = (slot[0], slot[1] // 2)
     images, columns = half.shape[1:]
     vmem = pl.BlockSpec(memory_space=pltpu.VMEM)
     anywhere = pl.BlockSpec(memory_space=pl.ANY)
     return pl.pallas_call(
         tail_kernel,
         out_shape=[
-            jax.ShapeDtypeStruct(slot, FLOAT),
+            jax.ShapeDtypeStruct(share, FLOAT),
             jax.ShapeDtypeStruct((count, 2 * images, columns), HALF),
             jax.ShapeDtypeStruct(vector.shape, FLOAT),
             jax.ShapeDtypeStruct(strip.shape, HALF),
@@ -1423,17 +1553,18 @@
         in_specs=[anywhere, vmem, vmem, anywhere],
         out_specs=[vmem, vmem, vmem, anywhere],
         scratch_shapes=[
-            pltpu.VMEM((2, 4, 2) + slot, HALF),
-            pltpu.VMEM((2, 4, 2) + slot, HALF),
-            pltpu.VMEM((4, 2) + slot, HALF),
-            pltpu.VMEM((3, 2) + slot, HALF),
-            pltpu.VMEM(slot, HALF),
+            pltpu.VMEM((2, 4) + slot, HALF),
+            pltpu.VMEM((2, 4) + slot, HALF),
+            pltpu.VMEM((4,) + slot, HALF),
+            pltpu.VMEM((3,) + slot, HALF),
+            pltpu.VMEM(share, HALF),
+            pltpu.VMEM(share, HALF),
             pltpu.VMEM(half.shape, FLOAT),
             pltpu.VMEM(half.shape[1:], FLOAT),
             pltpu.VMEM((2,) + vector.shape, FLOAT),
             pltpu.VMEM((3,) + vector.shape, FLOAT),
             pltpu.VMEM((4,) + vector.shape, FLOAT),
-            pltpu.SemaphoreType.DMA((16,)),
+            pltpu.SemaphoreType.DMA((8,)),
             pltpu.SemaphoreType.DMA((64,)),
             pltpu.SemaphoreType.DMA((64,)),
         ],
@@ -1447,12 +1578,6 @@
 
 def swap_blk(value):
     return lax.ppermute(value, "blk", [(0, 1), (1, 0)])
-
-
-def gather_weight(shard):
-    halves = lax.all_gather(shard, ("blk", "dp"), axis=0, tiled=True)
-    rows = halves.shape[0] // 2
-    return jnp.concatenate([halves[:rows], halves[rows:]], axis=1)
 
 
 def share_columns(total, me_blk):
@@ -1498,13 +1623,8 @@
     def other_of(pair):
         return lax.dynamic_index_in_dim(pair, 1 - me_blk, 0, keepdims=False)
 
-    cut = joint_weight.shape[1]
-    halves, modulation, act_part, tokens_other = head(
-        jnp.concatenate([joint_weight, output_weight], axis=1),
-        condition[0],
-        adaptive_weight,
-        adaptive_bias,
-        tokens[0],
+    joint, output_matrix, modulation, act_part, tokens_other = head(
+        joint_weight, output_weight, condition[0], adaptive_weight, adaptive_bias, tokens[0]
     )
     modulation = jnp.concatenate([modulation[0], modulation[1]], axis=1)
 
@@ -1521,12 +1641,10 @@
     output_vector, down_vector = bias_of(2 * small, small), bias_of(3 * small, small)
     up_vector = bias_of(4 * small, up_bias.shape[0])
 
-    halves, up_weight, down_weight = lax.optimization_barrier((halves, up_weight, down_weight))
-    halves = halves.reshape(2, width, -1)
-    joint = jnp.concatenate([halves[0, :, :cut], halves[1, :, :cut]], axis=1)
-    output_matrix = jnp.concatenate([halves[0, :, cut:], halves[1, :, cut:]], axis=1)
+    joint, up_weight, down_weight = lax.optimization_barrier((joint, up_weight, down_weight))
     up_halves = lax.all_gather(up_weight, ("blk", "dp"), axis=0, tiled=True)
     up_halves = up_halves.reshape(2, width, -1)
+    down_other = swap_blk(down_weight)
     cotangent_other = swap_blk(other_of(cotangent[0]))
 
     strip = mine_of(lengths[0]) // 2
@@ -1560,48 +1678,58 @@
         inputs, shift_one, scale_one, joint, joint_vector[None]
     )
     query, down_weight = lax.optimization_barrier((query, down_weight))
-    down_matrix = gather_weight(down_weight)
+    down_rows = order_blk(first, down_weight, down_other, 1)
+    down_matrix = lax.all_gather(down_rows, "dp", axis=0, tiled=True)
     attended, total = attend_pack(info, query, keys, values)
     branch_one, hidden_two = mix_call(
         attended, inputs, gate_one, shift_two, scale_two, output_matrix, output_vector[None]
     )
     activated, slope = up_call(hidden_two, up_halves, up_vector[None])
 
-    upstream = jnp.concatenate([mine_of(cotangent[0]), cotangent_other], axis=0)
-    d_branch_two, d_pre, down_sum, up_sum = down_grad_call(
-        upstream, gate_two, slope, down_matrix
-    )
-    d_pre, down_grad = lax.optimization_barrier(
-        (d_pre, left_outer(activated, d_branch_two).astype(HALF))
+    upstream, d_branch_two = join_call(cotangent[0], cotangent_other, gate_two, me_blk)
+    d_branch_two, down_grad = lax.optimization_barrier(
+        (d_branch_two, left_outer(activated, d_branch_two).astype(HALF))
     )
     down_total = lax.psum_scatter(down_grad, "dp", scatter_dimension=0, tiled=True)
+    d_pre, down_sum, up_sum = down_grad_call(d_branch_two, slope, down_matrix)
     d_pre, up_grad = lax.optimization_barrier(
         (d_pre, left_outer(hidden_two, d_pre).astype(HALF))
     )
     up_total = lax.psum_scatter(up_grad, "dp", scatter_dimension=0, tiled=True)
     result, result_send, d_gate_two = finish_call(
-        activated, inputs, branch_one, upstream, gate_one, gate_two, down_matrix, down_vector[None]
+        activated,
+        inputs,
+        branch_one,
+        upstream,
+        gate_one,
+        gate_two,
+        down_matrix,
+        down_vector[None],
+        me_blk,
     )
     d_pre, result_send = lax.optimization_barrier((d_pre, result_send))
     result_other = swap_blk(result_send)
-    d_middle, d_branch_one, d_attended, d_shift_two, d_scale_two, d_gate_one, output_sum = (
+    d_middle, d_branch_one, d_attended, delta, *part_totals = (
         mix_grad_call(
-            d_pre, inputs, branch_one, upstream, gate_one, scale_two, up_halves, output_matrix
+            d_pre, attended, inputs, branch_one, upstream, gate_one, scale_two, up_halves, output_matrix
         )
     )
+    d_shift_two, d_scale_two, d_gate_one, output_sum = part_totals
     d_attended, output_grad, down_total = lax.optimization_barrier(
         (d_attended, left_outer(attended, d_branch_one).astype(HALF), down_total)
     )
+    output_total = lax.psum_scatter(output_grad, "dp", scatter_dimension=0, tiled=True)
     down_share = share_columns(down_total, me_blk)
     d_query, d_keys, d_values = attend_pack_backward(
-        info, query, keys, values, d_attended, total
+        info, query, keys, values, d_attended, total, delta
     )
     d_query, up_total, result_other = lax.optimization_barrier((d_query, up_total, result_other))
     up_share = share_columns(up_total, me_blk)
+    result = fill_call(result, result_other, me_blk)
     d_projected = jnp.concatenate([d_query, d_keys, d_values], axis=1)
     joint_grad = left_outer(hidden_one, d_projected).astype(HALF)
     d_inputs, d_inputs_send, d_shift_one, d_scale_one, query_sum, value_sum = project_grad_call(
-        d_query, d_keys, d_values, inputs, d_middle, scale_one, joint
+        d_query, d_keys, d_values, inputs, d_middle, scale_one, joint, me_blk
     )
 
     def part_rows(value):
@@ -1618,21 +1746,16 @@
     )
     vectors = [query_sum, value_sum, output_sum, down_sum, up_sum]
     sums = jnp.concatenate([jnp.sum(value, axis=(0, 1)) for value in vectors])
-    narrow = output_weight.shape[1]
-    grad_halves = jnp.stack(
-        [
-            jnp.concatenate([joint_grad[:, :cut], output_grad[:, :narrow]], axis=1),
-            jnp.concatenate([joint_grad[:, cut:], output_grad[:, narrow:]], axis=1),
-        ]
-    )
+    joint_grad, output_total = lax.optimization_barrier((joint_grad, output_total))
+    output_share = share_columns(output_total, me_blk)
     shard_rows = adaptive_weight.shape[0]
-    share, d_mod_all, sums, d_inputs_other = tail(
-        grad_halves.reshape(2, 16, shard_rows, -1),
+    joint_share, d_mod_all, sums, d_inputs_other = tail(
+        joint_grad.reshape(16, shard_rows, -1),
         d_modulation.reshape(images, 2, -1).transpose(1, 0, 2),
         sums.reshape(-1, 128),
         d_inputs_send,
     )
-    joint_share, output_share = share[:, :cut], share[:, cut:]
+    d_inputs = fill_call(d_inputs, d_inputs_other, me_blk)
     sums = sums.reshape(-1)
     d_mod_all = d_mod_all.reshape(-1, d_mod_all.shape[2])
     adaptive_share = left_outer(act_part.reshape(-1, shard_rows), d_mod_all)
@@ -1649,12 +1772,9 @@
     def share_of(begin, size):
         return lax.dynamic_slice_in_dim(sums, begin + me_blk * (size // 2), size // 2, 0)
 
-    def both(mine, other):
-        return order_blk(first, mine[None], other.astype(FLOAT)[None], 0)[None]
-
     return (
-        both(result, result_other),
-        both(d_inputs, d_inputs_other),
+        result[None],
+        d_inputs[None],
         d_condition[None],
         adaptive_share,
         joint_share,

time: 828 us -> 765 us (0.924)
  other arithmetic: 66.5 us -> 19.7 us
  local copies, waits for them, and re-layouts: 40.6 us -> 17.8 us
    concatenate x7 -> x1, other arithmetic: 29.2 us -> 1.02 us  [order_blk(): jnp.concatenate([jnp.where(first, mine, other), jnp.where(first, other, m...]
    pallas_call x9 -> x12, Pallas kernels: 402 us -> 426 us  [the longest x8 260 us: dense_call(): pl.pallas_call(run, grid_spec=pltpu.PrefetchScalarGridSpec(num_scalar_pre...]
    pallas_call x2, Pallas kernels: 180 us -> 164 us  [attention_call(): pl.pallas_call(functools.partial(kernel, group=group), grid_spec=pltpu.Pr...]
    slice x5 -> x0, local copies, waits for them, and re-layouts: 13.7 us -> none  [the longest x1 5.16 us: gather_weight(): return jnp.concatenate([halves[:rows], halves[rows:]], axis=1)]
    broadcast_in_dim x2 -> x0, other arithmetic: 8.7 us -> none  [both(): return order_blk(first, mine[None], other.astype(FLOAT)[None], 0)[None]]
  transfers between devices with their start and end apart: 11 -> 14, of which waited for: 1 -> 1; matrix products, arithmetic and copies ran while one was open for 13% -> 17% of each run, Pallas kernels for 44% -> 57%
where the time goes in v2:
time: 765 us; the launch traced here: 758 us
  Pallas kernels  590 us (77%)
  matrix products  99.9 us (13%)
  other arithmetic  19.7 us (3%)
  local copies, waits for them, and re-layouts  17.8 us (2%)
  between operations  14.6 us (2%)
  starting transfers between devices  12.1 us (2%)
    pallas_call x8, Pallas kernels, dense_call(): pl.pallas_call(run, grid_spec=pltpu.PrefetchScalarGridSpec(num_scalar_pre...  260 us
    pallas_call x2, Pallas kernels, attention_call(): pl.pallas_call(functools.partial(kernel, group=group), grid_spec=pltpu.Pr...  164 us
    dot_general x5, matrix products, left_outer(): lax.dot_general(left, right, (((0,), (0,)), ((), ())), preferred_element_...  97.8 us
    pallas_call x1, Pallas kernels, head(): pl.pallas_call(head_kernel, out_shape=[jax.ShapeDtypeStruct((count,) + sl...  92.2 us
    pallas_call x1, Pallas kernels, tail(): pl.pallas_call(tail_kernel, out_shape=[jax.ShapeDtypeStruct(share, FLOAT)...  64.9 us
  transfers between devices with their start and end apart: 14, of which 1 were waited for; matrix products, arithmetic and copies ran while one was open for 17% of the time, Pallas kernels for 57%

profile of v2, /device:TPU:0, one launch (start us, length us, event | category | flops | bytes accessed | tf_op | source)
XLA Modules:
  0.0 758.5 jit_solution(3854656722270309673)
XLA Ops:
  11.8 92.2 %head.1 = (bf16[16,72,3456]{2,1,0:T(8,128)(2,1)}, bf16[16,72,1152]{2,1,0:T(8,128)(2,1)}, f32[2,8,3456]{2,1,0:T(8,128)S(1)}, bf16[16,16,72]{2,1,0:T(8,128)(2,1)S(1)}, bf16[1024,1152]{1,0:T(8,128)(2,1)S(1)}) custom-call(bf16[72,1728]{1,0:T(8,128)(2,1)S(1)} %copy-done.3, bf16[72,576]{1,0:T(8,128)(2,1)S(1)} %copy-done.4, bf16[16,16,72]{2,1,0:T(8,128)(2,1)S(1)} %bitcast.109, ...), custom_call_target="tpu_custom_call" | custom-call | bytes 209715200 | tf_op jit(solution)/shard_map/head/pallas_call | solution.py:1360
  104.2 1.3 collective-permute-start
  107.3 1.9 dynamic-slice_bitcast_fusion.1
  109.2 2.5 pad_maximum_fusion.refs_0_.refs_1_.refs_2_.refs_4_
  114.5 28.3 %project.1 = (bf16[2048,1152]{1,0:T(8,128)(2,1)}, bf16[2048,1152]{1,0:T(8,128)(2,1)}, bf16[2048,1152]{1,0:T(8,128)(2,1)}, bf16[2048,1152]{1,0:T(8,128)(2,1)}) custom-call(bf16[2048,1152]{1,0:T(8,128)(2,1)} %pad_maximum_fusion.refs_0_.refs_1_.refs_2_.refs_4_, f32[16,1,1152]{2,1,0:T(1,128)} %bitcast.122, f32[16,1,1152]{2,1,0:T(1,128)} %get-tuple-element.177.refs_2_.refs_6_, ...), custom_call_target="tpu_custom_call" | custom-call | flops 16307453952 | bytes 31716864 | tf_op jit(solution)/shard_map/project/pallas_call | solution.py:670
  144.2 1.9 dynamic-slice_bitcast_fusion
  146.1 1.4 collective-permute-start.1
  152.1 65.0 %attend.1 = (bf16[2048,1152]{1,0:T(8,128)(2,1)}, f32[16,1,2048]{2,1,0:T(1,128)}) custom-call(s32[16]{0:T(128)} %pad_add_fusion.info, bf16[2048,1152]{1,0:T(8,128)(2,1)} %get-tuple-element.83.q_ref, bf16[2048,1152]{1,0:T(8,128)(2,1)} %get-tuple-element.84.k_ref, bf16[2048,1152]{1,0:T(8,128)(2,1)} %get-tuple-element.85.v_ref), custom_call_target="tpu_custom_call" | custom-call | flops 70000001024 | bytes 31457280 | tf_op jit(solution)/shard_map/attend/pallas_call | solution.py:610
  217.8 15.2 %mix.1 = (f32[2048,1152]{1,0:T(8,128)}, bf16[2048,1152]{1,0:T(8,128)(2,1)}) custom-call(bf16[2048,1152]{1,0:T(8,128)(2,1)} %get-tuple-element.86.refs_0_.refs_1_, bf16[2048,1152]{1,0:T(8,128)(2,1)} %pad_maximum_fusion.refs_0_.refs_1_.refs_2_.refs_4_, f32[16,1,1152]{2,1,0:T(1,128)} %get-tuple-element.175.refs_2_.refs_5_, ...), custom_call_target="tpu_custom_call" | custom-call | flops 5435817984 | bytes 26472960 | tf_op jit(solution)/shard_map/mix/pallas_call | solution.py:670
  233.6 8.6 %join.1 = (bf16[2048,1152]{1,0:T(8,128)(2,1)}, bf16[2048,1152]{1,0:T(8,128)(2,1)}) custom-call(s32[1]{0:T(128)} %bitcast.refs_0_.strip, bf16[2,1024,1152]{2,1,0:T(8,128)(2,1)} %bitcast.114, bf16[1024,1152]{1,0:T(8,128)(2,1)} %collective-permute-done.1.refs_2_, f32[16,1,1152]{2,1,0:T(1,128)} %get-tuple-element.174.refs_3_.refs_6_), custom_call_target="tpu_custom_call" | custom-call | bytes 16588800 | tf_op jit(solution)/shard_map/join/pallas_call | solution.py:670
  242.1 42.9 %up.1 = (bf16[2048,4608]{1,0:T(8,128)(2,1)}, bf16[2048,4608]{1,0:T(8,128)(2,1)}) custom-call(bf16[2048,1152]{1,0:T(8,128)(2,1)} %get-tuple-element.88.refs_0_, bf16[2,1152,2304]{2,1,0:T(8,128)(2,1)} %bitcast.124, f32[1,4608]{1,0:T(1,128)} %maximum_convert_fusion.refs_2_), custom_call_target="tpu_custom_call" | custom-call | flops 21743271936 | bytes 53102592 | tf_op jit(solution)/shard_map/up/pallas_call | solution.py:670
  285.1 30.9 %convolution_convert_fusion.1 = bf16[4608,1152]{1,0:T(8,128)(2,1)} fusion(bf16[2048,4608]{1,0:T(8,128)(2,1)} %get-tuple-element.90.refs_1_, bf16[2048,1152]{1,0:T(8,128)(2,1)} %get-tuple-element.96.refs_0_), kind=kOutput, calls=%fused_computation.1 | convolution fusion | flops 21748580352 | bytes 34209792 | tf_op jit(solution)/shard_map/dot_general | solution.py:25
  317.4 36.6 %down_grad.1 = (bf16[2048,4608]{1,0:T(8,128)(2,1)}, f32[8,1,1152]{2,1,0:T(1,128)}, f32[8,1,4608]{2,1,0:T(1,128)}) custom-call(bf16[2048,1152]{1,0:T(8,128)(2,1)} %get-tuple-element.96.refs_0_, bf16[2048,4608]{1,0:T(8,128)(2,1)} %get-tuple-element.97.refs_1_, bf16[4608,1152]{1,0:T(8,128)(2,1)} %all-gather.5.cloned.1.call-done.refs_7_.refs_2_), custom_call_target="tpu_custom_call" | custom-call | flops 21743271936 | bytes 53268480 | tf_op jit(solution)/shard_map/down_grad/pallas_call | solution.py:670
  354.0 28.8 %convolution_convert_fusion = bf16[1152,4608]{1,0:T(8,128)(2,1)} fusion(bf16[2048,1152]{1,0:T(8,128)(2,1)} %get-tuple-element.88.refs_0_, bf16[2048,4608]{1,0:T(8,128)(2,1)} %get-tuple-element.101.refs_0_), kind=kOutput, calls=%fused_computation | convolution fusion | flops 21748580352 | bytes 34209792 | tf_op jit(solution)/shard_map/dot_general | solution.py:25
  382.8 34.5 %finish.1 = (f32[2,1024,1152]{2,1,0:T(8,128)}, bf16[1024,1152]{1,0:T(8,128)(2,1)}, f32[16,1,1152]{2,1,0:T(1,128)}) custom-call(s32[1]{0:T(128)} %bitcast.refs_0_.strip, bf16[2048,4608]{1,0:T(8,128)(2,1)} %get-tuple-element.90.refs_1_, bf16[2048,1152]{1,0:T(8,128)(2,1)} %pad_maximum_fusion.refs_0_.refs_1_.refs_2_.refs_4_, ...), custom_call_target="tpu_custom_call" | custom-call | flops 21743271936 | bytes 60387840 | tf_op jit(solution)/shard_map/finish/pallas_call | solution.py:670
  417.4 61.1 %mix_grad.1 = (f32[2048,1152]{1,0:T(8,128)}, bf16[2048,1152]{1,0:T(8,128)(2,1)}, bf16[2048,1152]{1,0:T(8,128)(2,1)}, f32[16,1,2048]{2,1,0:T(1,128)}, f32[16,1,11...) custom-call(bf16[2048,4608]{1,0:T(8,128)(2,1)} %get-tuple-element.101.refs_0_, ...), custom_call_target="tpu_custom_call" | custom-call | flops 27179089920 | bytes 75186176 | tf_op jit(solution)/shard_map/mix_grad/pallas_call | solution.py:670
  478.6 1.5 reduce_sum.80
  481.5 11.6 %convolution_convert_fusion.3 = bf16[1152,1152]{1,0:T(8,128)(2,1)} fusion(bf16[2048,1152]{1,0:T(8,128)(2,1)} %get-tuple-element.86.refs_0_.refs_1_, bf16[2048,1152]{1,0:T(8,128)(2,1)} %get-tuple-element.103), kind=kOutput, calls=%fused_computation.8 | convolution fusion | flops 5437145088 | bytes 12091392 | tf_op jit(solution)/shard_map/dot_general | solution.py:25
  493.1 99.5 %attend_backward.1 = (bf16[2048,1152]{1,0:T(8,128)(2,1)}, bf16[2048,1152]{1,0:T(8,128)(2,1)}, bf16[2048,1152]{1,0:T(8,128)(2,1)}) custom-call(s32[16]{0:T(128)} %pad_add_fusion.info, bf16[2048,1152]{1,0:T(8,128)(2,1)} %get-tuple-element.83.q_ref, bf16[2048,1152]{1,0:T(8,128)(2,1)} %get-tuple-element.84.k_ref, bf16[2048,1152]{1,0:T(8,128)(2,1)} %get-tuple-element.85.v_ref, ...), custom_call_target="tpu_custom_call" | custom-call | flops 140000002048 | bytes 31457280 | tf_op jit(solution)/shard_map/attend_backward/pallas_call | solution.py:610
  592.6 32.6 %project_grad.1 = (f32[2,1024,1152]{2,1,0:T(8,128)}, bf16[1024,1152]{1,0:T(8,128)(2,1)}, f32[16,1,1152]{2,1,0:T(1,128)}, f32[16,1,1152]{2,1,0:T(1,128)}, f32[16,1,1152]{2,1,0:T(1,128)}, /*index=5*/f32[16,1,1152]{2,1,0:T(1,128)}) custom-call(s32[1]{0:T(128)} %bitcast.refs_0_.strip, bf16[2048,1152]{1,0:T(8,128)(2,1)} %get-tuple-element.112.refs_1_, ...), custom_call_target="tpu_custom_call" | custom-call | flops 16307453952 | bytes 48439296 | tf_op jit(solution)/shard_map/project_grad/pallas_call | solution.py:670
  628.3 2.1 collective-permute-start.7
  630.4 4.5 fill.2
  635.2 25.0 %convolution_convert_fusion.2 = bf16[1152,3456]{1,0:T(8,128)(2,1)} fusion(bf16[2048,1152]{1,0:T(8,128)(2,1)} %get-tuple-element.117, bf16[2048,1152]{1,0:T(8,128)(2,1)} %get-tuple-element.114.refs_3_, bf16[2048,1152]{1,0:T(8,128)(2,1)} %get-tuple-element.113.refs_2_, bf16[2048,1152]{1,0:T(8,128)(2,1)} %get-tuple-element.112.refs_1_), kind=kOutput, calls=%fused_computation.2 | convolution fusion | flops 16353902592 | bytes 26836992 | tf_op jit(solution)/shard_map/dot_general | solution.py:25
  661.6 1.9 convert_add_fusion.1
  663.5 64.9 %tail.1 = (f32[72,1728]{1,0:T(8,128)S(1)}, bf16[16,16,3456]{2,1,0:T(8,128)(2,1)S(1)}, f32[72,128]{1,0:T(8,128)S(1)}, bf16[1024,1152]{1,0:T(8,128)(2,1)S(1)}) custom-call(bf16[16,72,3456]{2,1,0:T(8,128)(2,1)} %bitcast.117, f32[2,8,3456]{2,1,0:T(8,128)S(1)} %convolution_bitcast_fusion.1.half_ref, f32[72,128]{1,0:T(8,128)S(1)} %bitcast.110, ...), custom_call_target="tpu_custom_call" | custom-call | bytes 209715200 | tf_op jit(solution)/shard_map/tail/pallas_call | solution.py:1545
  728.4 1.4 copy-done
  729.8 1.3 fusion.5
  732.0 3.9 all-to-all-start
  735.9 1.4 convolution_bitcast_fusion
  737.4 1.4 collective-permute-start.5
  738.8 4.4 fill.3
  746.0 4.1 collective-permute-done.4
  (162 shorter events, 29.5 us)
Async XLA Ops:
  7.2 96.9 %copy-start.24 = (bf16[576]{0:T(1024)(128)(2,1)S(1)}, bf16[576]{0:T(1024)(128)(2,1)}, u32[]{:S(2)}) copy-start(bf16[576]{0:T(1024)(128)(2,1)} %param.29) | copy-start | bytes 3460
  7.2 96.9 %copy-start.25 = (bf16[576]{0:T(1024)(128)(2,1)S(1)}, bf16[576]{0:T(1024)(128)(2,1)}, u32[]{:S(2)}) copy-start(bf16[576]{0:T(1024)(128)(2,1)} %param.25) | copy-start | bytes 3460
  7.2 96.9 %copy-start.26 = (bf16[576]{0:T(1024)(128)(2,1)S(1)}, bf16[576]{0:T(1024)(128)(2,1)}, u32[]{:S(2)}) copy-start(bf16[576]{0:T(1024)(128)(2,1)} %param.26) | copy-start | bytes 3460
  7.2 96.9 %copy-start.27 = (bf16[576]{0:T(1024)(128)(2,1)S(1)}, bf16[576]{0:T(1024)(128)(2,1)}, u32[]{:S(2)}) copy-start(bf16[576]{0:T(1024)(128)(2,1)} %param.27) | copy-start | bytes 3460
  7.2 96.9 %copy-start.23 = (bf16[2304]{0:T(1024)(128)(2,1)S(1)}, bf16[2304]{0:T(1024)(128)(2,1)}, u32[]{:S(2)}) copy-start(bf16[2304]{0:T(1024)(128)(2,1)} %param.28) | copy-start | bytes 13828
  7.2 99.0 %copy-start.30 = (s32[1,2,8]{2,1,0:T(2,128)S(1)}, s32[1,2,8]{2,1,0:T(2,128)}, u32[]{:S(2)}) copy-start(s32[1,2,8]{2,1,0:T(2,128)} %param.18) | copy-start | bytes 196
  7.2 234.9 %all-gather.3.cloned.1.call-start = ((), (), s32[]{:S(2)}) async-start(), calls=%async_computation.4 | async-start | bytes 10948608 | tf_op jit(solution)/shard_map/all_gather | solution.py:1645
  11.8 93.7 %copy-start.8 = (bf16[288,576]{1,0:T(8,128)(2,1)S(1)}, bf16[288,576]{1,0:T(8,128)(2,1)}, u32[]{:S(2)}) copy-start(bf16[288,576]{1,0:T(8,128)(2,1)} %param.23) | copy-start | bytes 995332
  104.0 213.3 %all-gather.5.cloned.1.call-start = ((), (), s32[]{:S(2)}) async-start(), calls=%async_computation.5 | async-start | bytes 11280384 | tf_op jit(solution)/shard_map/all_gather | solution.py:1682
  104.2 9.0 %collective-permute-start = (bf16[4608]{0:T(1024)(128)(2,1)S(1)}, bf16[4608]{0:T(1024)(128)(2,1)S(1)}, u32[]{:S(2)}, u32[]{:S(2)}) collective-permute-start(bf16[4608]{0:T(1024)(128)(2,1)S(1)} %concatenate.78), channel_id=1, source_target_pairs={{0,1},{1,0},{2,3},{3,2},{4,5},{5,4},{6,7},{7,6},{8,9},{9,8},{10,11... | collective-permute-start | bytes 27656 | tf_op jit(solution)/shard_map/ppermute | solution.py:1580
  105.6 37.3 %collective-permute-start.2 = (bf16[288,576]{1,0:T(8,128)(2,1)S(1)}, bf16[288,576]{1,0:T(8,128)(2,1)S(1)}, u32[]{:S(2)}, u32[]{:S(2)}) collective-permute-start(bf16[288,576]{1,0:T(8,128)(2,1)S(1)} %copy-done.8), channel_id=1, source_target_pairs={{0,1},{1,0},{2,3},{3,2},{4,5},{5,4},{6,7},{7,6},{8,9},{9,8},{10,11... | collective-permute-start | bytes 995336 | tf_op jit(solution)/shard_map/ppermute | solution.py:1580
  144.0 349.1 %reduce-scatter.6.cloned.1.call-start = ((), (), s32[]{:S(2)}) async-start(), calls=%async_computation.6 | async-start | bytes 11280384 | tf_op jit(solution)/shard_map/reduce_scatter | solution.py:1693
  146.1 87.5 %collective-permute-start.1 = (bf16[1024,1152]{1,0:T(8,128)(2,1)S(1)}, bf16[1024,1152]{1,0:T(8,128)(2,1)}, u32[]{:S(2)}, u32[]{:S(2)}) collective-permute-start(bf16[1024,1152]{1,0:T(8,128)(2,1)S(1)} %dynamic-slice_bitcast_fusion), channel_id=1, source_target_pairs={{0,1},{1,0},{2,3},{3,2},{4,5},{5,4},{6,7},{7,6},{8,9},{9,8},{10,11... | collective-permute-start | bytes 7077896 | tf_op jit(solution)/shard_map/ppermute | solution.py:1580
  316.0 276.6 %reduce-scatter.8.cloned.1.call-start = ((), (), s32[]{:S(2)}) async-start(), calls=%async_computation.7 | async-start | bytes 11280384 | tf_op jit(solution)/shard_map/reduce_scatter | solution.py:1698
  417.3 62.8 %copy-start.20 = (f32[8,1,1152]{2,1,0:T(1,128)S(1)}, f32[8,1,1152]{2,1,0:T(1,128)}, u32[]{:S(2)}) copy-start(f32[8,1,1152]{2,1,0:T(1,128)} %get-tuple-element.129) | copy-start | bytes 110596
  417.3 63.4 %copy-start.10 = (f32[8,1,4608]{2,1,0:T(1,128)S(1)}, f32[8,1,4608]{2,1,0:T(1,128)}, u32[]{:S(2)}) copy-start(f32[8,1,4608]{2,1,0:T(1,128)} %get-tuple-element.130) | copy-start | bytes 442372
  417.3 246.2 %reduce-scatter.10.cloned.1.call-start = ((), (), s32[]{:S(2)}) async-start(), calls=%async_computation.8 | async-start | bytes 2820096
  478.5 114.1 %collective-permute-start.3 = (bf16[1024,1152]{1,0:T(8,128)(2,1)}, bf16[1024,1152]{1,0:T(8,128)(2,1)}, u32[]{:S(2)}, u32[]{:S(2)}) collective-permute-start(bf16[1024,1152]{1,0:T(8,128)(2,1)} %get-tuple-element.110), channel_id=1, source_target_pairs={{0,1},{1,0},{2,3},{3,2},{4,5},{5,4},{6,7},{7,6},{8,9},{9,8},{10,11... | collective-permute-start | bytes 7077896 | tf_op jit(solution)/shard_map/ppermute | solution.py:1580
  592.6 35.4 %copy-start.7 = (bf16[72,4608]{1,0:T(8,128)(2,1)S(1)}, bf16[72,4608]{1,0:T(8,128)(2,1)}, u32[]{:S(2)}) copy-start(bf16[72,4608]{1,0:T(8,128)(2,1)} %reduce-scatter.8.cloned.1.call-done) | copy-start | bytes 1990660
  592.6 35.5 %copy-start.6 = (bf16[288,1152]{1,0:T(8,128)(2,1)S(1)}, bf16[288,1152]{1,0:T(8,128)(2,1)}, u32[]{:S(2)}) copy-start(bf16[288,1152]{1,0:T(8,128)(2,1)} %reduce-scatter.6.cloned.1.call-done) | copy-start | bytes 1990660
  628.0 33.6 %collective-permute-start.6 = (bf16[72,2304]{1,0:T(8,128)(2,1)S(1)}, bf16[72,2304]{1,0:T(8,128)(2,1)}, u32[]{:S(2)}, u32[]{:S(2)}) collective-permute-start(bf16[72,2304]{1,0:T(8,128)(2,1)S(1)} %constant_dynamic-slice_fusion.1), channel_id=1, source_target_pairs={{0,1},{1,0},{2,3},{3,2},{4,5},{5,4},{6,7},{7,6},{8,9},{9,8},{10,11... | collective-permute-start | bytes 995336 | tf_op jit(solution)/shard_map/ppermute | solution.py:1580
  628.3 32.3 %collective-permute-start.7 = (bf16[288,576]{1,0:T(8,128)(2,1)S(1)}, bf16[288,576]{1,0:T(8,128)(2,1)S(1)}, u32[]{:S(2)}, u32[]{:S(2)}) collective-permute-start(bf16[288,576]{1,0:T(8,128)(2,1)S(1)} %constant_dynamic-slice_fusion), channel_id=1, source_target_pairs={{0,1},{1,0},{2,3},{3,2},{4,5},{5,4},{6,7},{7,6},{8,9},{9,8},{10,11... | collective-permute-start | bytes 995336 | tf_op jit(solution)/shard_map/ppermute | solution.py:1580
  630.4 4.7 copy-start.22
  630.4 4.7 copy-start.13
  635.1 25.1 %copy-start.19 = (f32[16,8,1]{0,1,2:T(8,128)S(1)}, f32[16,8,1]{0,1,2:T(8,128)}, u32[]{:S(2)}) copy-start(f32[16,8,1]{0,1,2:T(8,128)} %copy-done.18) | copy-start | bytes 1540
  635.1 25.4 %copy-start.12 = (f32[4608]{0:T(1024)S(1)}, f32[4608]{0:T(1024)}, u32[]{:S(2)}) copy-start(f32[4608]{0:T(1024)} %reduce_sum.82) | copy-start | bytes 55300
  663.5 66.3 %copy-start.2 = (bf16[72,3456]{1,0:T(8,128)(2,1)S(1)}, bf16[72,3456]{1,0:T(8,128)(2,1)}, u32[]{:S(2)}) copy-start(bf16[72,3456]{1,0:T(8,128)(2,1)} %adaptive_ref.1) | copy-start | bytes 1492996
  729.8 7.5 copy-start.9
  732.0 12.5 %all-to-all-start = ((f32[16,16,72]{2,1,0:T(8,128)}), f32[16,16,72]{2,1,0:T(8,128)S(1)}, u32[]{:S(2)}, u32[]{:S(2)}) async-start(f32[16,16,72]{2,1,0:T(8,128)} %fusion.5), calls=%async_computation.2 | async-start | bytes 262144 | tf_op jit(solution)/shard_map/all_to_all | solution.py:1765
  737.4 7.8 %collective-permute-start.5 = (bf16[72,576]{1,0:T(8,128)(2,1)S(1)}, bf16[72,576]{1,0:T(8,128)(2,1)S(1)}, u32[]{:S(2)}, u32[]{:S(2)}) collective-permute-start(bf16[72,576]{1,0:T(8,128)(2,1)S(1)} %constant_dynamic-slice_fusion.2), channel_id=1, source_target_pairs={{0,1},{1,0},{2,3},{3,2},{4,5},{5,4},{6,7},{7,6},{8,9},{9,8},{10,11... | collective-permute-start | bytes 248840 | tf_op jit(solution)/shard_map/ppermute | solution.py:1580
  738.8 11.5 %copy-start.11 = (bf16[1,2,8,1152]{3,2,1,0:T(8,128)(2,1)S(1)}, bf16[1,2,8,1152]{3,2,1,0:T(8,128)(2,1)}, u32[]{:S(2)}) copy-start(bf16[1,2,8,1152]{3,2,1,0:T(8,128)(2,1)} %param.17) | copy-start | bytes 110596
  744.5 5.6 collective-permute-start.4
  (13 other events, 33.9 us)
Sparse Core Ops, SparseCore 0:
  104.1 104.9 all-gather.2
  212.0 86.9 all-gather.4
  316.1 117.6 reduce-scatter.5
  437.7 120.0 reduce-scatter.7
  592.7 62.1 reduce-scatter.9

commit v3 on v2

--- a/solution.py
+++ b/solution.py
@@ -1308,7 +1308,6 @@
     for z_step in (3, 2, 1, 0):
         copies.send(("core", "part", z_step), parts.at[1, z_step], from_core.at[z_step])
     products(0)
-    forward(2)
     for z_step in (3, 2, 1, 0):
         copies.receive(("core", "part", z_step))
         total = add(parts[0, z_step], from_core[z_step])
@@ -1318,7 +1317,9 @@
         parts[0, z_step] = total.astype(HALF)
         if z_step > 0:
             copies.send(("z", "part", z_step), parts.at[0, z_step], from_z.at[z_step - 1])
-        if z_step == 1:
+        if z_step == 3:
+            forward(2)
+        if z_step == 2:
             forward(3)
     copies.send(("x", "part"), parts.at[0, 0, 1], from_x)
 

time: 765 us -> 762 us (level)
  no operation moved by 1% of the time
where the time goes in v3:
time: 762 us; the launch traced here: 755 us
  Pallas kernels  585 us (77%)
  matrix products  99.9 us (13%)
  other arithmetic  19.7 us (3%)
  local copies, waits for them, and re-layouts  17.8 us (2%)
  between operations  14.6 us (2%)
  starting transfers between devices  13.8 us (2%)
    pallas_call x8, Pallas kernels, dense_call(): pl.pallas_call(run, grid_spec=pltpu.PrefetchScalarGridSpec(num_scalar_pre...  260 us
    pallas_call x2, Pallas kernels, attention_call(): pl.pallas_call(functools.partial(kernel, group=group), grid_spec=pltpu.Pr...  164 us
    dot_general x5, matrix products, left_outer(): lax.dot_general(left, right, (((0,), (0,)), ((), ())), preferred_element_...  97.7 us
    pallas_call x1, Pallas kernels, head(): pl.pallas_call(head_kernel, out_shape=[jax.ShapeDtypeStruct((count,) + sl...  87.8 us
    pallas_call x1, Pallas kernels, tail(): pl.pallas_call(tail_kernel, out_shape=[jax.ShapeDtypeStruct(share, FLOAT)...  64.6 us
  transfers between devices with their start and end apart: 14, of which 1 were waited for; matrix products, arithmetic and copies ran while one was open for 17% of the time, Pallas kernels for 57%

profile of v3, /device:TPU:0, one launch (start us, length us, event | category | flops | bytes accessed | tf_op | source)
XLA Modules:
  0.0 755.1 jit_solution(10078448319038886298)
XLA Ops:
  11.8 87.8 %head.1 = (bf16[16,72,3456]{2,1,0:T(8,128)(2,1)}, bf16[16,72,1152]{2,1,0:T(8,128)(2,1)}, f32[2,8,3456]{2,1,0:T(8,128)S(1)}, bf16[16,16,72]{2,1,0:T(8,128)(2,1)S(1)}, bf16[1024,1152]{1,0:T(8,128)(2,1)S(1)}) custom-call(bf16[72,1728]{1,0:T(8,128)(2,1)S(1)} %copy-done.3, bf16[72,576]{1,0:T(8,128)(2,1)S(1)} %copy-done.4, bf16[16,16,72]{2,1,0:T(8,128)(2,1)S(1)} %bitcast.109, ...), custom_call_target="tpu_custom_call" | custom-call | bytes 209715200 | tf_op jit(solution)/shard_map/head/pallas_call | solution.py:1361
  100.8 1.1 collective-permute-start.2
  102.9 1.9 dynamic-slice_bitcast_fusion.1
  104.8 2.5 pad_maximum_fusion.refs_0_.refs_1_.refs_2_.refs_4_
  110.2 28.3 %project.1 = (bf16[2048,1152]{1,0:T(8,128)(2,1)}, bf16[2048,1152]{1,0:T(8,128)(2,1)}, bf16[2048,1152]{1,0:T(8,128)(2,1)}, bf16[2048,1152]{1,0:T(8,128)(2,1)}) custom-call(bf16[2048,1152]{1,0:T(8,128)(2,1)} %pad_maximum_fusion.refs_0_.refs_1_.refs_2_.refs_4_, f32[16,1,1152]{2,1,0:T(1,128)} %bitcast.122, f32[16,1,1152]{2,1,0:T(1,128)} %get-tuple-element.177.refs_2_.refs_6_, ...), custom_call_target="tpu_custom_call" | custom-call | flops 16307453952 | bytes 31716864 | tf_op jit(solution)/shard_map/project/pallas_call | solution.py:670
  139.8 1.8 dynamic-slice_bitcast_fusion
  147.3 64.5 %attend.1 = (bf16[2048,1152]{1,0:T(8,128)(2,1)}, f32[16,1,2048]{2,1,0:T(1,128)}) custom-call(s32[16]{0:T(128)} %pad_add_fusion.info, bf16[2048,1152]{1,0:T(8,128)(2,1)} %get-tuple-element.83.q_ref, bf16[2048,1152]{1,0:T(8,128)(2,1)} %get-tuple-element.84.k_ref, bf16[2048,1152]{1,0:T(8,128)(2,1)} %get-tuple-element.85.v_ref), custom_call_target="tpu_custom_call" | custom-call | flops 70000001024 | bytes 31457280 | tf_op jit(solution)/shard_map/attend/pallas_call | solution.py:610
  212.5 15.2 %mix.1 = (f32[2048,1152]{1,0:T(8,128)}, bf16[2048,1152]{1,0:T(8,128)(2,1)}) custom-call(bf16[2048,1152]{1,0:T(8,128)(2,1)} %get-tuple-element.86.refs_0_.refs_1_, bf16[2048,1152]{1,0:T(8,128)(2,1)} %pad_maximum_fusion.refs_0_.refs_1_.refs_2_.refs_4_, f32[16,1,1152]{2,1,0:T(1,128)} %get-tuple-element.175.refs_2_.refs_5_, ...), custom_call_target="tpu_custom_call" | custom-call | flops 5435817984 | bytes 26472960 | tf_op jit(solution)/shard_map/mix/pallas_call | solution.py:670
  228.3 8.6 %join.1 = (bf16[2048,1152]{1,0:T(8,128)(2,1)}, bf16[2048,1152]{1,0:T(8,128)(2,1)}) custom-call(s32[1]{0:T(128)} %bitcast.refs_0_.strip, bf16[2,1024,1152]{2,1,0:T(8,128)(2,1)} %bitcast.114, bf16[1024,1152]{1,0:T(8,128)(2,1)} %collective-permute-done.1.refs_2_, f32[16,1,1152]{2,1,0:T(1,128)} %get-tuple-element.174.refs_3_.refs_6_), custom_call_target="tpu_custom_call" | custom-call | bytes 16588800 | tf_op jit(solution)/shard_map/join/pallas_call | solution.py:670
  236.9 42.9 %up.1 = (bf16[2048,4608]{1,0:T(8,128)(2,1)}, bf16[2048,4608]{1,0:T(8,128)(2,1)}) custom-call(bf16[2048,1152]{1,0:T(8,128)(2,1)} %get-tuple-element.88.refs_0_, bf16[2,1152,2304]{2,1,0:T(8,128)(2,1)} %bitcast.124, f32[1,4608]{1,0:T(1,128)} %maximum_convert_fusion.refs_2_), custom_call_target="tpu_custom_call" | custom-call | flops 21743271936 | bytes 53102592 | tf_op jit(solution)/shard_map/up/pallas_call | solution.py:670
  279.8 30.9 %convolution_convert_fusion.1 = bf16[4608,1152]{1,0:T(8,128)(2,1)} fusion(bf16[2048,4608]{1,0:T(8,128)(2,1)} %get-tuple-element.90.refs_1_, bf16[2048,1152]{1,0:T(8,128)(2,1)} %get-tuple-element.96.refs_0_), kind=kOutput, calls=%fused_computation.1 | convolution fusion | flops 21748580352 | bytes 34209792 | tf_op jit(solution)/shard_map/dot_general | solution.py:25
  312.1 36.5 %down_grad.1 = (bf16[2048,4608]{1,0:T(8,128)(2,1)}, f32[8,1,1152]{2,1,0:T(1,128)}, f32[8,1,4608]{2,1,0:T(1,128)}) custom-call(bf16[2048,1152]{1,0:T(8,128)(2,1)} %get-tuple-element.96.refs_0_, bf16[2048,4608]{1,0:T(8,128)(2,1)} %get-tuple-element.97.refs_1_, bf16[4608,1152]{1,0:T(8,128)(2,1)} %all-gather.5.cloned.1.call-done.refs_7_.refs_2_), custom_call_target="tpu_custom_call" | custom-call | flops 21743271936 | bytes 53268480 | tf_op jit(solution)/shard_map/down_grad/pallas_call | solution.py:670
  348.5 28.8 %convolution_convert_fusion = bf16[1152,4608]{1,0:T(8,128)(2,1)} fusion(bf16[2048,1152]{1,0:T(8,128)(2,1)} %get-tuple-element.88.refs_0_, bf16[2048,4608]{1,0:T(8,128)(2,1)} %get-tuple-element.101.refs_0_), kind=kOutput, calls=%fused_computation | convolution fusion | flops 21748580352 | bytes 34209792 | tf_op jit(solution)/shard_map/dot_general | solution.py:25
  377.3 34.5 %finish.1 = (f32[2,1024,1152]{2,1,0:T(8,128)}, bf16[1024,1152]{1,0:T(8,128)(2,1)}, f32[16,1,1152]{2,1,0:T(1,128)}) custom-call(s32[1]{0:T(128)} %bitcast.refs_0_.strip, bf16[2048,4608]{1,0:T(8,128)(2,1)} %get-tuple-element.90.refs_1_, bf16[2048,1152]{1,0:T(8,128)(2,1)} %pad_maximum_fusion.refs_0_.refs_1_.refs_2_.refs_4_, ...), custom_call_target="tpu_custom_call" | custom-call | flops 21743271936 | bytes 60387840 | tf_op jit(solution)/shard_map/finish/pallas_call | solution.py:670
  411.9 61.0 %mix_grad.1 = (f32[2048,1152]{1,0:T(8,128)}, bf16[2048,1152]{1,0:T(8,128)(2,1)}, bf16[2048,1152]{1,0:T(8,128)(2,1)}, f32[16,1,2048]{2,1,0:T(1,128)}, f32[16,1,11...) custom-call(bf16[2048,4608]{1,0:T(8,128)(2,1)} %get-tuple-element.101.refs_0_, ...), custom_call_target="tpu_custom_call" | custom-call | flops 27179089920 | bytes 75186176 | tf_op jit(solution)/shard_map/mix_grad/pallas_call | solution.py:670
  472.9 1.7 collective-permute-start.3
  474.6 1.5 reduce_sum.80
  477.5 11.6 %convolution_convert_fusion.3 = bf16[1152,1152]{1,0:T(8,128)(2,1)} fusion(bf16[2048,1152]{1,0:T(8,128)(2,1)} %get-tuple-element.86.refs_0_.refs_1_, bf16[2048,1152]{1,0:T(8,128)(2,1)} %get-tuple-element.103), kind=kOutput, calls=%fused_computation.8 | convolution fusion | flops 5437145088 | bytes 12091392 | tf_op jit(solution)/shard_map/dot_general | solution.py:25
  489.1 99.6 %attend_backward.1 = (bf16[2048,1152]{1,0:T(8,128)(2,1)}, bf16[2048,1152]{1,0:T(8,128)(2,1)}, bf16[2048,1152]{1,0:T(8,128)(2,1)}) custom-call(s32[16]{0:T(128)} %pad_add_fusion.info, bf16[2048,1152]{1,0:T(8,128)(2,1)} %get-tuple-element.83.q_ref, bf16[2048,1152]{1,0:T(8,128)(2,1)} %get-tuple-element.84.k_ref, bf16[2048,1152]{1,0:T(8,128)(2,1)} %get-tuple-element.85.v_ref, ...), custom_call_target="tpu_custom_call" | custom-call | flops 140000002048 | bytes 31457280 | tf_op jit(solution)/shard_map/attend_backward/pallas_call | solution.py:610
  588.8 32.7 %project_grad.1 = (f32[2,1024,1152]{2,1,0:T(8,128)}, bf16[1024,1152]{1,0:T(8,128)(2,1)}, f32[16,1,1152]{2,1,0:T(1,128)}, f32[16,1,1152]{2,1,0:T(1,128)}, f32[16,1,1152]{2,1,0:T(1,128)}, /*index=5*/f32[16,1,1152]{2,1,0:T(1,128)}) custom-call(s32[1]{0:T(128)} %bitcast.refs_0_.strip, bf16[2048,1152]{1,0:T(8,128)(2,1)} %get-tuple-element.112.refs_1_, ...), custom_call_target="tpu_custom_call" | custom-call | flops 16307453952 | bytes 48439296 | tf_op jit(solution)/shard_map/project_grad/pallas_call | solution.py:670
  624.8 1.9 collective-permute-start.7
  626.7 4.5 fill.2
  631.5 25.0 %convolution_convert_fusion.2 = bf16[1152,3456]{1,0:T(8,128)(2,1)} fusion(bf16[2048,1152]{1,0:T(8,128)(2,1)} %get-tuple-element.117, bf16[2048,1152]{1,0:T(8,128)(2,1)} %get-tuple-element.114.refs_3_, bf16[2048,1152]{1,0:T(8,128)(2,1)} %get-tuple-element.113.refs_2_, bf16[2048,1152]{1,0:T(8,128)(2,1)} %get-tuple-element.112.refs_1_), kind=kOutput, calls=%fused_computation.2 | convolution fusion | flops 16353902592 | bytes 26836992 | tf_op jit(solution)/shard_map/dot_general | solution.py:25
  657.9 1.9 convert_add_fusion.1
  659.8 64.6 %tail.1 = (f32[72,1728]{1,0:T(8,128)S(1)}, bf16[16,16,3456]{2,1,0:T(8,128)(2,1)S(1)}, f32[72,128]{1,0:T(8,128)S(1)}, bf16[1024,1152]{1,0:T(8,128)(2,1)S(1)}) custom-call(bf16[16,72,3456]{2,1,0:T(8,128)(2,1)} %bitcast.117, f32[2,8,3456]{2,1,0:T(8,128)S(1)} %convolution_bitcast_fusion.1.half_ref, f32[72,128]{1,0:T(8,128)S(1)} %bitcast.110, ...), custom_call_target="tpu_custom_call" | custom-call | bytes 209715200 | tf_op jit(solution)/shard_map/tail/pallas_call | solution.py:1546
  724.4 1.4 copy-done
  725.8 1.3 fusion.5
  728.0 4.1 all-to-all-start
  732.1 1.4 convolution_bitcast_fusion
  733.6 1.8 collective-permute-start.5
  735.4 4.4 fill.3
  742.5 4.1 collective-permute-done.4
  (162 shorter events, 30.7 us)
Async XLA Ops:
  7.2 92.5 %copy-start.24 = (bf16[576]{0:T(1024)(128)(2,1)S(1)}, bf16[576]{0:T(1024)(128)(2,1)}, u32[]{:S(2)}) copy-start(bf16[576]{0:T(1024)(128)(2,1)} %param.29) | copy-start | bytes 3460
  7.2 92.5 %copy-start.25 = (bf16[576]{0:T(1024)(128)(2,1)S(1)}, bf16[576]{0:T(1024)(128)(2,1)}, u32[]{:S(2)}) copy-start(bf16[576]{0:T(1024)(128)(2,1)} %param.25) | copy-start | bytes 3460
  7.2 92.5 %copy-start.26 = (bf16[576]{0:T(1024)(128)(2,1)S(1)}, bf16[576]{0:T(1024)(128)(2,1)}, u32[]{:S(2)}) copy-start(bf16[576]{0:T(1024)(128)(2,1)} %param.26) | copy-start | bytes 3460
  7.2 92.5 %copy-start.27 = (bf16[576]{0:T(1024)(128)(2,1)S(1)}, bf16[576]{0:T(1024)(128)(2,1)}, u32[]{:S(2)}) copy-start(bf16[576]{0:T(1024)(128)(2,1)} %param.27) | copy-start | bytes 3460
  7.2 92.5 %copy-start.23 = (bf16[2304]{0:T(1024)(128)(2,1)S(1)}, bf16[2304]{0:T(1024)(128)(2,1)}, u32[]{:S(2)}) copy-start(bf16[2304]{0:T(1024)(128)(2,1)} %param.28) | copy-start | bytes 13828
  7.2 94.7 %copy-start.30 = (s32[1,2,8]{2,1,0:T(2,128)S(1)}, s32[1,2,8]{2,1,0:T(2,128)}, u32[]{:S(2)}) copy-start(s32[1,2,8]{2,1,0:T(2,128)} %param.18) | copy-start | bytes 196
  7.2 229.6 %all-gather.3.cloned.1.call-start = ((), (), s32[]{:S(2)}) async-start(), calls=%async_computation.4 | async-start | bytes 10948608 | tf_op jit(solution)/shard_map/all_gather | solution.py:1646
  11.8 89.0 %copy-start.8 = (bf16[288,576]{1,0:T(8,128)(2,1)S(1)}, bf16[288,576]{1,0:T(8,128)(2,1)}, u32[]{:S(2)}) copy-start(bf16[288,576]{1,0:T(8,128)(2,1)} %param.23) | copy-start | bytes 995332
  99.6 212.4 %all-gather.5.cloned.1.call-start = ((), (), s32[]{:S(2)}) async-start(), calls=%async_computation.5 | async-start | bytes 11280384 | tf_op jit(solution)/shard_map/all_gather | solution.py:1683
  99.8 9.0 %collective-permute-start = (bf16[4608]{0:T(1024)(128)(2,1)S(1)}, bf16[4608]{0:T(1024)(128)(2,1)S(1)}, u32[]{:S(2)}, u32[]{:S(2)}) collective-permute-start(bf16[4608]{0:T(1024)(128)(2,1)S(1)} %concatenate.78), channel_id=1, source_target_pairs={{0,1},{1,0},{2,3},{3,2},{4,5},{5,4},{6,7},{7,6},{8,9},{9,8},{10,11... | collective-permute-start | bytes 27656 | tf_op jit(solution)/shard_map/ppermute | solution.py:1581
  100.8 37.7 %collective-permute-start.2 = (bf16[288,576]{1,0:T(8,128)(2,1)S(1)}, bf16[288,576]{1,0:T(8,128)(2,1)S(1)}, u32[]{:S(2)}, u32[]{:S(2)}) collective-permute-start(bf16[288,576]{1,0:T(8,128)(2,1)S(1)} %copy-done.8), channel_id=1, source_target_pairs={{0,1},{1,0},{2,3},{3,2},{4,5},{5,4},{6,7},{7,6},{8,9},{9,8},{10,11... | collective-permute-start | bytes 995336 | tf_op jit(solution)/shard_map/ppermute | solution.py:1581
  139.6 349.5 %reduce-scatter.6.cloned.1.call-start = ((), (), s32[]{:S(2)}) async-start(), calls=%async_computation.6 | async-start | bytes 11280384 | tf_op jit(solution)/shard_map/reduce_scatter | solution.py:1694
  141.7 86.6 %collective-permute-start.1 = (bf16[1024,1152]{1,0:T(8,128)(2,1)S(1)}, bf16[1024,1152]{1,0:T(8,128)(2,1)}, u32[]{:S(2)}, u32[]{:S(2)}) collective-permute-start(bf16[1024,1152]{1,0:T(8,128)(2,1)S(1)} %dynamic-slice_bitcast_fusion), channel_id=1, source_target_pairs={{0,1},{1,0},{2,3},{3,2},{4,5},{5,4},{6,7},{7,6},{8,9},{9,8},{10,11... | collective-permute-start | bytes 7077896 | tf_op jit(solution)/shard_map/ppermute | solution.py:1581
  310.7 278.0 %reduce-scatter.8.cloned.1.call-start = ((), (), s32[]{:S(2)}) async-start(), calls=%async_computation.7 | async-start | bytes 11280384 | tf_op jit(solution)/shard_map/reduce_scatter | solution.py:1699
  411.8 64.3 %copy-start.20 = (f32[8,1,1152]{2,1,0:T(1,128)S(1)}, f32[8,1,1152]{2,1,0:T(1,128)}, u32[]{:S(2)}) copy-start(f32[8,1,1152]{2,1,0:T(1,128)} %get-tuple-element.129) | copy-start | bytes 110596
  411.8 65.0 %copy-start.10 = (f32[8,1,4608]{2,1,0:T(1,128)S(1)}, f32[8,1,4608]{2,1,0:T(1,128)}, u32[]{:S(2)}) copy-start(f32[8,1,4608]{2,1,0:T(1,128)} %get-tuple-element.130) | copy-start | bytes 442372
  411.9 248.0 %reduce-scatter.10.cloned.1.call-start = ((), (), s32[]{:S(2)}) async-start(), calls=%async_computation.8 | async-start | bytes 2820096
  472.9 115.8 %collective-permute-start.3 = (bf16[1024,1152]{1,0:T(8,128)(2,1)}, bf16[1024,1152]{1,0:T(8,128)(2,1)}, u32[]{:S(2)}, u32[]{:S(2)}) collective-permute-start(bf16[1024,1152]{1,0:T(8,128)(2,1)} %get-tuple-element.110), channel_id=1, source_target_pairs={{0,1},{1,0},{2,3},{3,2},{4,5},{5,4},{6,7},{7,6},{8,9},{9,8},{10,11... | collective-permute-start | bytes 7077896 | tf_op jit(solution)/shard_map/ppermute | solution.py:1581
  588.8 35.5 %copy-start.7 = (bf16[72,4608]{1,0:T(8,128)(2,1)S(1)}, bf16[72,4608]{1,0:T(8,128)(2,1)}, u32[]{:S(2)}) copy-start(bf16[72,4608]{1,0:T(8,128)(2,1)} %reduce-scatter.8.cloned.1.call-done) | copy-start | bytes 1990660
  588.8 35.8 %copy-start.6 = (bf16[288,1152]{1,0:T(8,128)(2,1)S(1)}, bf16[288,1152]{1,0:T(8,128)(2,1)}, u32[]{:S(2)}) copy-start(bf16[288,1152]{1,0:T(8,128)(2,1)} %reduce-scatter.6.cloned.1.call-done) | copy-start | bytes 1990660
  624.3 33.6 %collective-permute-start.6 = (bf16[72,2304]{1,0:T(8,128)(2,1)S(1)}, bf16[72,2304]{1,0:T(8,128)(2,1)}, u32[]{:S(2)}, u32[]{:S(2)}) collective-permute-start(bf16[72,2304]{1,0:T(8,128)(2,1)S(1)} %constant_dynamic-slice_fusion.1), channel_id=1, source_target_pairs={{0,1},{1,0},{2,3},{3,2},{4,5},{5,4},{6,7},{7,6},{8,9},{9,8},{10,11... | collective-permute-start | bytes 995336 | tf_op jit(solution)/shard_map/ppermute | solution.py:1581
  624.8 32.1 %collective-permute-start.7 = (bf16[288,576]{1,0:T(8,128)(2,1)S(1)}, bf16[288,576]{1,0:T(8,128)(2,1)S(1)}, u32[]{:S(2)}, u32[]{:S(2)}) collective-permute-start(bf16[288,576]{1,0:T(8,128)(2,1)S(1)} %constant_dynamic-slice_fusion), channel_id=1, source_target_pairs={{0,1},{1,0},{2,3},{3,2},{4,5},{5,4},{6,7},{7,6},{8,9},{9,8},{10,11... | collective-permute-start | bytes 995336 | tf_op jit(solution)/shard_map/ppermute | solution.py:1581
  626.7 4.7 copy-start.22
  626.7 4.7 copy-start.13
  631.5 25.0 %copy-start.19 = (f32[16,8,1]{0,1,2:T(8,128)S(1)}, f32[16,8,1]{0,1,2:T(8,128)}, u32[]{:S(2)}) copy-start(f32[16,8,1]{0,1,2:T(8,128)} %copy-done.18) | copy-start | bytes 1540
  631.5 25.4 %copy-start.12 = (f32[4608]{0:T(1024)S(1)}, f32[4608]{0:T(1024)}, u32[]{:S(2)}) copy-start(f32[4608]{0:T(1024)} %reduce_sum.82) | copy-start | bytes 55300
  659.8 66.0 %copy-start.2 = (bf16[72,3456]{1,0:T(8,128)(2,1)S(1)}, bf16[72,3456]{1,0:T(8,128)(2,1)}, u32[]{:S(2)}) copy-start(bf16[72,3456]{1,0:T(8,128)(2,1)} %adaptive_ref.1) | copy-start | bytes 1492996
  725.8 7.7 %copy-start.9 = (bf16[72,1152]{1,0:T(8,128)(2,1)S(1)}, bf16[72,1152]{1,0:T(8,128)(2,1)}, u32[]{:S(2)}) copy-start(bf16[72,1152]{1,0:T(8,128)(2,1)} %reduce-scatter.10.cloned.1.call-done) | copy-start | bytes 497668
  728.0 13.1 %all-to-all-start = ((f32[16,16,72]{2,1,0:T(8,128)}), f32[16,16,72]{2,1,0:T(8,128)S(1)}, u32[]{:S(2)}, u32[]{:S(2)}) async-start(f32[16,16,72]{2,1,0:T(8,128)} %fusion.5), calls=%async_computation.2 | async-start | bytes 262144 | tf_op jit(solution)/shard_map/all_to_all | solution.py:1766
  733.6 8.2 %collective-permute-start.5 = (bf16[72,576]{1,0:T(8,128)(2,1)S(1)}, bf16[72,576]{1,0:T(8,128)(2,1)S(1)}, u32[]{:S(2)}, u32[]{:S(2)}) collective-permute-start(bf16[72,576]{1,0:T(8,128)(2,1)S(1)} %constant_dynamic-slice_fusion.2), channel_id=1, source_target_pairs={{0,1},{1,0},{2,3},{3,2},{4,5},{5,4},{6,7},{7,6},{8,9},{9,8},{10,11... | collective-permute-start | bytes 248840 | tf_op jit(solution)/shard_map/ppermute | solution.py:1581
  735.4 11.5 %copy-start.11 = (bf16[1,2,8,1152]{3,2,1,0:T(8,128)(2,1)S(1)}, bf16[1,2,8,1152]{3,2,1,0:T(8,128)(2,1)}, u32[]{:S(2)}) copy-start(bf16[1,2,8,1152]{3,2,1,0:T(8,128)(2,1)} %param.17) | copy-start | bytes 110596
  741.1 5.6 collective-permute-start.4
  (13 other events, 34.0 us)
Sparse Core Ops, SparseCore 0:
  99.8 104.0 all-gather.2
  206.7 86.8 all-gather.4
  310.8 118.0 reduce-scatter.5
  432.8 120.0 reduce-scatter.7
  588.9 60.9 reduce-scatter.9
